TPU v7x, 256 devices: a whole 4x4x8 slice. The times are simulated.
256 devices in a mesh: dom: 32 (over x_lo, z, core), ka: 8 (over y, x_hi).
Axes of the slice: x: 4 (x_hi: 2, x_lo: 2; x = x_hi * 2 + x_lo), y: 4, z: 8, core: 2. Of those that a mesh axis runs over, the one named last changes fastest.
Arguments:
- grad_out: bfloat16 [64, 196608], P(None, 'dom'), may hold values from -6 to 6
- frac_pos: float32 [3, 196608], P(None, 'dom'), may hold values from 0 to 1, as said below
- k_index: int32 [3, 4096], P(None, 'ka'), may hold values from -10 to 10
- ewald_filter: float32 [64, 4096], P(None, 'ka'), may hold values from 2.1143198e-05 to 0.00021143198
- struct_fac: float32 [2, 64, 4096], P(None, None, 'ka'), may hold values from -1792 to 1792
- out_weight: bfloat16 [64, 64], replicated, may hold values from -0.75 to 0.75
- pair_mix: bfloat16 [64, 64], replicated, may hold values from -0.75 to 0.75
- pair_weight: float32 [48, 196608], P(None, 'dom'), may hold values from -4 to 4
- nbr_index: int32 [48, 196608], P(None, 'dom'), may hold values from 0 to 7679, as said below
- nbr_count: int32 [196608], P('dom'), may hold values from 12 to 48, as said below
- halo_send: int32 [2, 24576], P(None, 'dom'), may hold values from 0 to 6143, as said below
Outputs:
- d_feat: bfloat16 [64, 196608], P(None, ('dom', 'ka'))
- d_filter: float32 [64, 4096], P(None, 'ka')
Inputs may be any that keep to these rules, and one draw needn't show every extreme that they name: `frac_pos`: atoms of a later domain have a larger first coordinate; all coordinates lie in the unit box. The first nbr_count[a] slots of an atom are live. `nbr_index`: a value v below 6144 names the atom at position v of the same domain; 6144 + j names ghost j from the previous domain on the cycle, 6912 + j ghost j from the next domain. `halo_send`: for each domain, 768 positions of its atoms: row 0 those sent to the next domain, row 1 those sent to the previous one.
All inputs are finite; a program needn't handle non-finite values.
Results may differ from a plain program's by a relative error of at most 0.0059.
Values may be sent and summed in bfloat16 or wider, within the bound.
No kernel may reach another device: no remote copies, remote signals or barrier semaphores. Data moves between devices by JAX's collectives and lax.ppermute only.
A program may use at most 128 MiB of HBM per device.

v0:
```python
import math

import jax
import jax.numpy as jnp
from jax import lax
from jax.sharding import PartitionSpec as P

FULL_TURN = 2.0 * math.pi


def shifted(block, axis, distance):
    devices = range(lax.axis_size(axis))
    route = [((i - distance) % len(devices), i) for i in devices]
    return lax.ppermute(block, axis, route)


def phase_pair(frac_block, k_float):
    angles = FULL_TURN * (
        frac_block[0][:, None] * k_float[0][None, :]
        + frac_block[1][:, None] * k_float[1][None, :]
        + frac_block[2][:, None] * k_float[2][None, :]
    )
    return (jnp.cos(angles).astype(jnp.bfloat16), jnp.sin(angles).astype(jnp.bfloat16))


def contract_k(coefficient, table):
    return lax.dot_general(
        coefficient, table, (((1,), (1,)), ((), ())), preferred_element_type=jnp.float32
    )


def local(
    grad_out,
    frac_pos,
    k_index,
    ewald_filter,
    struct_fac,
    out_weight,
    pair_mix,
    pair_weight,
    nbr_index,
    nbr_count,
    halo_send,
):
    channels, local_atoms = grad_out.shape
    own_rows = local_atoms // lax.axis_size("ka")
    own_start = lax.axis_index("ka") * own_rows
    lr_cot = jnp.dot(out_weight, grad_out, preferred_element_type=jnp.float32).astype(jnp.bfloat16)
    sr_cot = jnp.dot(pair_mix, grad_out, preferred_element_type=jnp.float32).astype(jnp.bfloat16)
    send_next = jnp.take(sr_cot, halo_send[0], axis=1)
    send_prev = jnp.take(sr_cot, halo_send[1], axis=1)
    from_left = shifted(send_next, "dom", 1)
    from_right = shifted(send_prev, "dom", -1)
    k_float = k_index.astype(jnp.float32)
    block_size = math.gcd(local_atoms, 512)
    block_count = local_atoms // block_size

    def add_block(step_index, summed):
        first_atom = step_index * block_size
        frac_block = lax.dynamic_slice_in_dim(frac_pos, first_atom, block_size, 1)
        cot_block = lax.dynamic_slice_in_dim(lr_cot, first_atom, block_size, 1)
        cos_table, sin_table = phase_pair(frac_block, k_float)
        new_cos = summed[0] + jnp.dot(cot_block, cos_table, preferred_element_type=jnp.float32)
        new_sin = summed[1] + jnp.dot(cot_block, sin_table, preferred_element_type=jnp.float32)
        return (new_cos, new_sin)

    zero_k = jnp.zeros((channels, k_float.shape[1]), jnp.float32)
    q_cos, q_sin = lax.fori_loop(0, block_count, add_block, (zero_k, zero_k))
    q_cos, q_sin = lax.psum((q_cos, q_sin), "dom")
    atom_total = local_atoms * lax.axis_size("dom")
    d_filter = (struct_fac[0] * q_cos + struct_fac[1] * q_sin) / atom_total
    p_cos = (ewald_filter * q_cos).astype(jnp.bfloat16)
    p_sin = (ewald_filter * q_sin).astype(jnp.bfloat16)

    def long_block(step_index, summed):
        first_atom = step_index * block_size
        frac_block = lax.dynamic_slice_in_dim(frac_pos, first_atom, block_size, 1)
        cos_table, sin_table = phase_pair(frac_block, k_float)
        block_part = contract_k(p_cos, cos_table) + contract_k(p_sin, sin_table)
        return lax.dynamic_update_slice_in_dim(summed, block_part, first_atom, 1)

    long_all = lax.fori_loop(
        0, block_count, long_block, jnp.zeros((channels, local_atoms), jnp.float32)
    )
    long_own = lax.psum_scatter(long_all, "ka", scatter_dimension=1, tiled=True)
    extended = jnp.concatenate([sr_cot, from_left, from_right], axis=1)
    own_index = lax.dynamic_slice_in_dim(nbr_index, own_start, own_rows, 1)
    own_weight = lax.dynamic_slice_in_dim(pair_weight, own_start, own_rows, 1)
    own_count = lax.dynamic_slice_in_dim(nbr_count, own_start, own_rows, 0)
    slot_ids = lax.broadcasted_iota(jnp.int32, own_index.shape, 0)
    masked = jnp.where(slot_ids < own_count[None, :], own_weight, jnp.zeros_like(own_weight))
    picked = jnp.take(extended, own_index.reshape(-1), axis=1).reshape(
        channels, own_index.shape[0], own_rows
    )
    short_own = jnp.sum(picked.astype(jnp.float32) * masked[None, :, :], axis=1)
    own_grad = lax.dynamic_slice_in_dim(grad_out, own_start, own_rows, 1).astype(jnp.float32)
    d_feat = (own_grad + long_own + short_own).astype(jnp.bfloat16)
    return (d_feat, d_filter)


def solution(mesh):
    return jax.shard_map(
        local,
        mesh=mesh,
        in_specs=(
            P(None, "dom"),
            P(None, "dom"),
            P(None, "ka"),
            P(None, "ka"),
            P(None, None, "ka"),
            P(),
            P(),
            P(None, "dom"),
            P(None, "dom"),
            P("dom"),
            P(None, "dom"),
        ),
        out_specs=(P(None, ("dom", "ka")), P(None, "ka")),
        check_vma=False,
    )
```

profile of v0, /device:TPU:1, one launch (start us, length us, event | category | flops | bytes accessed | tf_op | source)
XLA Modules:
  0.0 640.1 jit_solution(783853013526556622)
XLA Ops:
  8.6 1.1 convolution_convert_fusion
  10.6 1.9 gather_fusion.1
  13.3 3.1 collective-permute-start
  16.4 1.9 gather_fusion.2
  18.8 1.1 convolution_convert_fusion.1
  19.9 106.0 %while.30 = (s32[]{:T(128)}, f32[64,512]{1,0:T(8,128)S(1)}, f32[64,512]{1,0:T(8,128)S(1)}, bf16[64,6144]{1,0:T(8,128)(2,1)S(1)}, f32[3,6144]{1,0:T(4,128)}, /*in...) while((s32[]{:T(128)}, f32[64,512]{1,0:T(8,128)S(1)}, ...), condition=%wide.region_1.2_spmd.clone, body=%wide.region_0.1_spmd.clone.sunk | while | flops 70909960 | bytes 704730 | solution.py:68
  20.8 4.0 convolution_add_fusion.6
  24.8 3.9 convolution_add_fusion.5
  29.6 4.0 convolution_add_fusion.6
  33.6 3.9 convolution_add_fusion.5
  38.5 4.0 convolution_add_fusion.6
  42.4 3.9 convolution_add_fusion.5
  47.3 4.0 convolution_add_fusion.6
  51.3 3.9 convolution_add_fusion.5
  56.1 4.0 convolution_add_fusion.6
  60.1 3.9 convolution_add_fusion.5
  64.9 4.0 convolution_add_fusion.6
  68.9 3.9 convolution_add_fusion.5
  73.8 4.0 convolution_add_fusion.6
  77.7 3.9 convolution_add_fusion.5
  82.6 4.0 convolution_add_fusion.6
  86.6 3.9 convolution_add_fusion.5
  91.4 4.0 convolution_add_fusion.6
  95.4 3.9 convolution_add_fusion.5
  100.3 4.0 convolution_add_fusion.6
  104.2 3.9 convolution_add_fusion.5
  109.1 4.0 convolution_add_fusion.6
  113.1 3.9 convolution_add_fusion.5
  117.9 4.0 convolution_add_fusion.6
  121.9 3.9 convolution_add_fusion.5
  128.8 1.6 dynamic-slice_select_fusion
  130.4 220.4 %all-reduce.3.cloned.1.call-done = (f32[64,512]{1,0:T(8,128)}, f32[64,512]{1,0:T(8,128)}) async-done(((f32[64,512]{1,0:T(8,128)}, f32[64,512]{1,0:T(8,128)}), (f32[64,512]{1,0:T(8,128)}, f32[64,512]{1,0:T(8,128)})) %all-reduce.3.cloned.1.call-update) | async-done | bytes 262160 | tf_op jit(solution)/shard_map/psum | solution.py:69
  350.8 1.7 fusion.33
  352.6 115.4 %while.29 = (s32[]{:T(128)}, f32[64,6144]{1,0:T(8,128)S(1)}, f32[3,6144]{1,0:T(4,128)}, f32[3,512]{1,0:T(4,128)S(1)}, bf16[64,512]{1,0:T(8,128)(2,1)}, /*index=5...) while((s32[]{:T(128)}, f32[64,6144]{1,0:T(8,128)S(1)}, ...), condition=%wide.region_5.6_spmd, body=%wide.region_4.5_spmd.sunk | while | flops 70811656 | bytes 835815 | solution.py:82
  353.5 4.7 fusion.50
  358.3 3.9 fusion.51
  363.2 4.7 fusion.50
  367.9 3.9 fusion.51
  372.8 4.7 fusion.50
  377.5 3.9 fusion.51
  382.4 4.7 fusion.50
  387.1 3.9 fusion.51
  392.0 4.7 fusion.50
  396.7 3.9 fusion.51
  401.6 4.7 fusion.50
  406.4 3.9 fusion.51
  411.2 4.7 fusion.50
  416.0 3.9 fusion.51
  420.9 4.7 fusion.50
  425.6 3.9 fusion.51
  430.5 4.7 fusion.50
  435.2 3.9 fusion.51
  440.1 4.7 fusion.50
  444.8 3.9 fusion.51
  449.7 4.7 fusion.50
  454.4 3.9 fusion.51
  459.3 4.7 fusion.50
  464.1 3.9 fusion.51
  468.0 2.3 copy.19
  471.8 1.6 compare_and_fusion
  473.4 1.9 pad_maximum_fusion
  475.3 2.0 copy.24
  477.4 140.2 %gather_fusion = bf16[36864,64]{1,0:T(8,128)(2,1)} fusion(bf16[64,7680]{0,1:T(8,128)(2,1)S(1)} %copy.24, s32[36864]{0:T(1024)} %broadcast_clamp_fusion), kind=kCustom, calls=%fused_computation.2 | custom fusion | bytes 9584640 | tf_op jit(solution)/shard_map/jit(_take)/gather | solution.py:92
  617.6 13.8 %multiply_reduce_fusion = f32[64,768]{0,1:T(8,128)S(1)} fusion(f32[48,768]{1,0:T(8,128)S(1)} %copy-done.2, bf16[64,48,768]{0,2,1:T(8,128)(2,1)} %bitcast.75, pred[48,768]{1,0:T(8,128)(4,1)S(1)} %copy-done.4), kind=kLoop, calls=%fused_computation.46 | loop fusion | flops 9388032 | bytes 5099520 | tf_op jit(solution)/shard_map/reduce_sum | solution.py:95
  (99 shorter events, 31.6 us)
Async XLA Ops:
  7.2 1.4 copy-start
  7.2 343.6 %all-reduce.3.cloned.1.call-start = ((), (), s32[]{:S(2)}) async-start(), calls=%async_computation.2 | async-start | bytes 524288 | tf_op jit(solution)/shard_map/psum | solution.py:69
  10.5 8.2 %copy-start.9 = (s32[3,512]{1,0:T(4,128)S(1)}, s32[3,512]{1,0:T(4,128)}, u32[]{:S(2)}) copy-start(s32[3,512]{1,0:T(4,128)} %param.19) | copy-start | bytes 18436
  13.3 460.1 %collective-permute-start = (bf16[64,768]{1,0:T(8,128)(2,1)S(1)}, bf16[64,768]{1,0:T(8,128)(2,1)}, u32[]{:S(2)}, u32[]{:S(2)}) collective-permute-start(bf16[64,768]{1,0:T(8,128)(2,1)S(1)} %select_bitcast_fusion.1), channel_id=1, source_target_pairs={{248,0},{0,8},{8,16},{16,24},{24,32},{32,40},{40,48},{48,56},{56,6... | collective-permute-start | bytes 294920 | tf_op jit(solution)/shard_map/ppermute | solution.py:14
  18.5 454.9 %collective-permute-start.1 = (bf16[64,768]{1,0:T(8,128)(2,1)S(1)}, bf16[64,768]{1,0:T(8,128)(2,1)}, u32[]{:S(2)}, u32[]{:S(2)}) collective-permute-start(bf16[64,768]{1,0:T(8,128)(2,1)S(1)} %select_bitcast_fusion), channel_id=1, source_target_pairs={{8,0},{16,8},{24,16},{32,24},{40,32},{48,40},{56,48},{64,56},{72,6... | collective-permute-start | bytes 294920 | tf_op jit(solution)/shard_map/ppermute | solution.py:14
  19.9 330.9 %copy-start.3 = (f32[2,64,512]{2,1,0:T(8,128)S(1)}, f32[2,64,512]{2,1,0:T(8,128)}, u32[]{:S(2)}) copy-start(f32[2,64,512]{2,1,0:T(8,128)} %param.21) | copy-start | bytes 786436
  19.9 330.9 %copy-start.5 = (f32[64,512]{1,0:T(8,128)S(1)}, f32[64,512]{1,0:T(8,128)}, u32[]{:S(2)}) copy-start(f32[64,512]{1,0:T(8,128)} %param.20) | copy-start | bytes 393220
  125.8 0.7 copy-start.6
  125.9 0.7 copy-start.7
  126.6 504.9 %reduce-scatter.2.cloned.1.call-start = ((), (), s32[]{:S(2)}) async-start(), calls=%async_computation.1 | async-start | bytes 3538944 | tf_op jit(solution)/shard_map/reduce_scatter | solution.py:85
  352.6 5.6 copy-start.8
  362.2 5.6 copy-start.8
  371.9 5.6 copy-start.8
  381.5 5.6 copy-start.8
  391.1 5.6 copy-start.8
  400.7 5.6 copy-start.8
  410.3 5.6 copy-start.8
  419.9 5.6 copy-start.8
  429.6 5.6 copy-start.8
  439.2 5.6 copy-start.8
  448.8 5.6 copy-start.8
  458.4 5.6 copy-start.8
  477.4 140.2 %copy-start.2 = (f32[48,768]{1,0:T(8,128)S(1)}, f32[48,768]{1,0:T(8,128)}, u32[]{:S(2)}) copy-start(f32[48,768]{1,0:T(8,128)} %dynamic-slice_select_fusion) | copy-start | bytes 442372
  477.4 140.2 %copy-start.4 = (pred[48,768]{1,0:T(8,128)(4,1)S(1)}, pred[48,768]{1,0:T(8,128)(4,1)}, u32[]{:S(2)}) copy-start(pred[48,768]{1,0:T(8,128)(4,1)} %compare_and_fusion) | copy-start | bytes 110596
  617.6 13.9 %copy-start.1 = (bf16[64,768]{0,1:T(8,128)(2,1)S(1)}, bf16[64,768]{0,1:T(8,128)(2,1)}, u32[]{:S(2)}) copy-start(bf16[64,768]{0,1:T(8,128)(2,1)} %copy.26) | copy-start | bytes 294916
Sparse Core Ops, SparseCore 0:
  126.7 224.0 all-reduce.2
  470.4 81.4 reduce-scatter.1
where the time goes:
time: 645 us; the launch traced here: 640 us
  waiting for transfers between devices  220 us (34%)
  matrix products  201 us (31%)
  local copies, waits for them, and re-layouts  176 us (27%)
  other arithmetic  23.8 us (4%)
  between operations  14.3 us (2%)
    psum x1, waiting for transfers between devices, local(): q_cos, q_sin = lax.psum((q_cos, q_sin), 'dom')  220 us
    gather x1, local copies, waits for them, and re-layouts, local(): jnp.take(extended, own_index.reshape(-1), axis=1)  140 us
    dot_general x24, matrix products, contract_k(): lax.dot_general(coefficient, table, (((1,), (1,)), ((), ())), preferred_e...  104 us
    dot_general x12, matrix products, add_block(): jnp.dot(cot_block, sin_table, preferred_element_type=jnp.float32)  47.5 us
    dot_general x12, matrix products, add_block(): jnp.dot(cot_block, cos_table, preferred_element_type=jnp.float32)  47.2 us
    slice x24, local copies, waits for them, and re-layouts, phase_pair(): frac_block[0][:, None] * k_float[0][None, :]  21.5 us
    reduce_sum x1, other arithmetic, local(): short_own = jnp.sum(picked.astype(jnp.float32) * masked[None, :, :], axis=1)  13.8 us
  transfers between devices with their start and end apart: 4, of which 1 were waited for; matrix products, arithmetic and copies ran while one was open for 61% of the time, Pallas kernels for 0%

commit v1 on v0

v1 whole, which is shorter than its diff:
```python
import functools
import math

import jax
import jax.numpy as jnp
import numpy as np
from jax import lax
from jax.experimental import pallas as pl
from jax.experimental.pallas import tpu as pltpu
from jax.sharding import PartitionSpec as P

BF16 = jnp.bfloat16
F32 = jnp.float32
LANES = 128


def even_fit(function, terms):
    u = np.cos(np.pi * (np.arange(200) + 0.5) / 200) * 0.125 + 0.125
    fitted = np.polynomial.chebyshev.Chebyshev.fit(u, function(np.sqrt(u)), terms - 1, domain=[0, 0.25])
    return [float(c) for c in fitted.convert(kind=np.polynomial.Polynomial).coef]


SIN_HALF = even_fit(lambda r: math.sqrt(2) * np.sin(np.pi * r) / r, 4)
COS_HALF = even_fit(lambda r: math.sqrt(2) * np.cos(np.pi * r), 4)


def swapped(block, axis, bit):
    return lax.ppermute(block, axis, [(i, i ^ bit) for i in range(lax.axis_size(axis))])


def shifted(block, axis, distance):
    devices = range(lax.axis_size(axis))
    route = [((i - distance) % len(devices), i) for i in devices]
    return lax.ppermute(block, axis, route)


def front_kernel(rows, mix_ref, grad_ref, frac_ref, k_ref, q_ref, table_ref, pieces_ref, turns_ref):
    @pl.when(pl.program_id(0) == 0)
    def _():
        q_ref[...] = jnp.zeros_like(q_ref)
        pieces_ref[...] = jnp.zeros_like(pieces_ref)

    frac = frac_ref[...]
    high = frac.astype(BF16).astype(F32)
    rest = frac - high
    middle = rest.astype(BF16).astype(F32)
    pieces_ref[0:3, :] = high
    pieces_ref[3:6, :] = middle
    pieces_ref[6:9, :] = rest - middle
    turns_ref[...] = jnp.dot(k_ref[...], pieces_ref[...].astype(BF16), preferred_element_type=F32)
    cot = jnp.dot(mix_ref[...], grad_ref[...], preferred_element_type=F32).astype(BF16)
    k_count = k_ref.shape[0]

    def fill(i, carry):
        first = pl.multiple_of(i * rows, rows)
        turns = turns_ref[pl.ds(first, rows), :]
        r = turns - jnp.round(turns)
        u = r * r
        s = r * (SIN_HALF[0] + u * (SIN_HALF[1] + u * (SIN_HALF[2] + u * SIN_HALF[3])))
        c = COS_HALF[0] + u * (COS_HALF[1] + u * (COS_HALF[2] + u * COS_HALF[3]))
        table_ref[pl.ds(first, rows), :] = (1.0 - s * s).astype(BF16)
        table_ref[pl.ds(first + k_count, rows), :] = (s * c).astype(BF16)
        return carry

    lax.fori_loop(0, k_count // rows, fill, 0, unroll=2)
    q_ref[...] += lax.dot_general(
        cot, table_ref[...], (((1,), (1,)), ((), ())), preferred_element_type=F32
    )


def front(mix, grad, frac, k_triple, rows=16, block=1024):
    channels, atoms = grad.shape
    k_count = k_triple.shape[0]
    return pl.pallas_call(
        functools.partial(front_kernel, rows),
        grid=(atoms // block,),
        in_specs=[
            pl.BlockSpec((channels, channels), lambda i: (0, 0)),
            pl.BlockSpec((channels, block), lambda i: (0, i)),
            pl.BlockSpec((3, block), lambda i: (0, i)),
            pl.BlockSpec((k_count, 16), lambda i: (0, 0)),
        ],
        out_specs=[
            pl.BlockSpec((channels, 2 * k_count), lambda i: (0, 0)),
            pl.BlockSpec((2 * k_count, block), lambda i: (0, i)),
        ],
        out_shape=[
            jax.ShapeDtypeStruct((channels, 2 * k_count), F32),
            jax.ShapeDtypeStruct((2 * k_count, atoms), BF16),
        ],
        scratch_shapes=[pltpu.VMEM((16, block), F32), pltpu.VMEM((k_count, block), F32)],
        compiler_params=pltpu.CompilerParams(vmem_limit_bytes=24 << 20),
        cost_estimate=pl.CostEstimate(flops=20_000_000_000, bytes_accessed=14_000_000, transcendentals=0),
        name="structure_sums",
    )(mix, grad, frac, k_triple)


def long_kernel(p_ref, table_ref, out_ref):
    out_ref[0] = jnp.dot(p_ref[...], table_ref[...], preferred_element_type=F32).astype(BF16)


def long_parts(p, table, parts):
    channels, depth = p.shape
    atoms = table.shape[1]
    own = atoms // parts
    return pl.pallas_call(
        long_kernel,
        grid=(parts,),
        in_specs=[
            pl.BlockSpec((channels, depth), lambda i: (0, 0)),
            pl.BlockSpec((depth, own), lambda i: (0, i)),
        ],
        out_specs=pl.BlockSpec((1, channels, own), lambda i: (i, 0, 0)),
        out_shape=jax.ShapeDtypeStruct((parts, channels, own), BF16),
        compiler_params=pltpu.CompilerParams(vmem_limit_bytes=24 << 20),
        cost_estimate=pl.CostEstimate(flops=800_000_000, bytes_accessed=14_000_000, transcendentals=0),
        name="long_parts",
    )(p, table)


def short_kernel(atoms, slots, index_ref, weight_ref, rows_ref, out_ref):
    sublane = lax.broadcasted_iota(jnp.int32, (8, LANES), 0)

    def group(g, carry):
        first = pl.multiple_of(g * 8, 8)
        weights = weight_ref[pl.ds(first, 8), :]
        total = jnp.zeros((8, LANES), F32)
        for s in range(slots):
            picked = jnp.broadcast_to(rows_ref[index_ref[s * atoms + first]], (8, LANES))
            for a in range(1, 8):
                row = jnp.broadcast_to(rows_ref[index_ref[s * atoms + first + a]], (8, LANES))
                picked = jnp.where(sublane == a, row, picked)
            total = total + picked * weights[:, s : s + 1]
        out_ref[pl.ds(first, 8), :] = total
        return carry

    lax.fori_loop(0, atoms // 8, group, 0)


def short_sums(index, weight, rows):
    slots, atoms = index.shape
    return pl.pallas_call(
        functools.partial(short_kernel, atoms, slots),
        in_specs=[
            pl.BlockSpec(memory_space=pltpu.SMEM),
            pl.BlockSpec(memory_space=pltpu.VMEM),
            pl.BlockSpec(memory_space=pltpu.VMEM),
        ],
        out_specs=pl.BlockSpec(memory_space=pltpu.VMEM),
        out_shape=jax.ShapeDtypeStruct((atoms, LANES), F32),
        compiler_params=pltpu.CompilerParams(vmem_limit_bytes=24 << 20),
        cost_estimate=pl.CostEstimate(
            flops=100_000 * slots * atoms, bytes_accessed=4_000_000, transcendentals=0
        ),
        name="short_sums",
    )(index.reshape(-1), weight.T, rows)


def local(
    grad_out,
    frac_pos,
    k_index,
    ewald_filter,
    struct_fac,
    out_weight,
    pair_mix,
    pair_weight,
    nbr_index,
    nbr_count,
    halo_send,
):
    channels, local_atoms = grad_out.shape
    ka_size, dom_size = lax.axis_size("ka"), lax.axis_size("dom")
    own_rows = local_atoms // ka_size
    own_start = lax.axis_index("ka") * own_rows
    k_count = k_index.shape[1]

    mix_wide = jnp.zeros((LANES, channels), BF16).at[:channels].set(pair_mix)
    sr_rows = lax.dot_general(
        grad_out, mix_wide, (((0,), (1,)), ((), ())), preferred_element_type=F32
    ).astype(BF16)
    sr_cot = jnp.dot(pair_mix, grad_out, preferred_element_type=F32).astype(BF16)
    from_left = shifted(jnp.take(sr_cot, halo_send[0], axis=1), "dom", 1)
    from_right = shifted(jnp.take(sr_cot, halo_send[1], axis=1), "dom", -1)
    ghosts = jnp.concatenate([from_left, from_right], axis=1).T
    ghosts = jnp.pad(ghosts, ((0, 0), (0, LANES - channels)))
    extended = jnp.concatenate([sr_rows.astype(F32), ghosts.astype(F32)], axis=0)[:, None, :]

    own_index = lax.dynamic_slice_in_dim(nbr_index, own_start, own_rows, 1)
    own_weight = lax.dynamic_slice_in_dim(pair_weight, own_start, own_rows, 1)
    own_count = lax.dynamic_slice_in_dim(nbr_count, own_start, own_rows, 0)
    slot_ids = lax.broadcasted_iota(jnp.int32, own_index.shape, 0)
    masked = jnp.where(slot_ids < own_count[None, :], own_weight, jnp.zeros_like(own_weight))
    piece_atoms = 128
    short = []

    def beside(value, bit):
        at = len(short) * piece_atoms
        index = own_index[:, at : at + piece_atoms]
        value, index = lax.optimization_barrier((value, index))
        received = swapped(value, "dom", bit)
        piece = short_sums(index, masked[:, at : at + piece_atoms], extended)
        received, piece = lax.optimization_barrier((received, piece))
        short.append(piece)
        return received.astype(F32)

    k_rows = k_index.astype(BF16).T
    k_triple = jnp.concatenate([k_rows, k_rows, k_rows, jnp.zeros((k_count, 7), BF16)], axis=1)
    q, table = front(out_weight, grad_out, frac_pos, k_triple)

    half = channels // 2
    core = lax.axis_index("dom") % 2
    mine = lax.dynamic_slice_in_dim(q, core * half, half, 0)
    other = lax.dynamic_slice_in_dim(q, (1 - core) * half, half, 0)
    total = mine + beside(other.astype(BF16), 1)
    bit = 2
    while bit < dom_size:
        rounded = total.astype(BF16)
        total = rounded.astype(F32) + beside(rounded, bit)
        bit *= 2
    partner = beside(total, 1)
    q = jnp.where(
        core == 0,
        jnp.concatenate([total, partner], axis=0),
        jnp.concatenate([partner, total], axis=0),
    )
    q_cos, q_sin = q[:, :k_count], q[:, k_count:]
    atom_total = local_atoms * dom_size
    d_filter = (struct_fac[0] * q_cos + struct_fac[1] * q_sin) / atom_total
    p = jnp.concatenate([ewald_filter * q_cos, ewald_filter * q_sin], axis=1).astype(BF16)

    parts = lax.all_to_all(long_parts(p, table, ka_size), "ka", 0, 0, tiled=True)
    long_own = jnp.sum(parts.astype(F32), axis=0)
    short_own = jnp.concatenate(short, axis=0)[:, :channels].T
    own_grad = lax.dynamic_slice_in_dim(grad_out, own_start, own_rows, 1).astype(F32)
    d_feat = (own_grad + long_own + short_own).astype(BF16)
    return (d_feat, d_filter)


def solution(mesh):
    return jax.shard_map(
        local,
        mesh=mesh,
        in_specs=(
            P(None, "dom"),
            P(None, "dom"),
            P(None, "ka"),
            P(None, "ka"),
            P(None, None, "ka"),
            P(),
            P(),
            P(None, "dom"),
            P(None, "dom"),
            P("dom"),
            P(None, "dom"),
        ),
        out_specs=(P(None, ("dom", "ka")), P(None, "ka")),
        check_vma=False,
    )
```

time: 645 us -> 132 us (0.20)
  waiting for transfers between devices: 220 us -> 14 us
  matrix products: 201 us -> 3.42 us
  local copies, waits for them, and re-layouts: 176 us -> 23.9 us
  Pallas kernels: 0 us -> 58.7 us
  starting transfers between devices: 3.68 us -> 23.3 us
  other arithmetic: 23.8 us -> 6.93 us
  between operations: 14.3 us -> 1.09 us
    psum x1 -> x0, waiting for transfers between devices: 220 us -> none  [local(): q_cos, q_sin = lax.psum((q_cos, q_sin), 'dom')]
    dot_general x50 -> x2, matrix products: 201 us -> 3.42 us  [the longest x1 1.92 us: local(): lax.dot_general(grad_out, mix_wide, (((0,), (1,)), ((), ())), preferred_e...]
    gather x5 -> x2, local copies, waits for them, and re-layouts: 144 us -> 6.48 us  [the longest x1 3.28 us: local(): from_right = shifted(jnp.take(sr_cot, halo_send[1], axis=1), 'dom', -1)]
    pallas_call x0 -> x8, Pallas kernels: none -> 58.7 us  [the longest x6 35.9 us: short_sums(): pl.pallas_call(functools.partial(short_kernel, atoms, slots), in_specs=[p...]
    slice x25 -> x2, local copies, waits for them, and re-layouts: 22.3 us -> 1.66 us  [the longest x1 0.84 us: beside(): index = own_index[:, at:at + piece_atoms]]
    all_to_all x0 -> x1, waiting for transfers between devices: none -> 14 us  [local(): lax.all_to_all(long_parts(p, table, ka_size), 'ka', 0, 0, tiled=True)]
    reduce_sum x1, other arithmetic: 13.8 us -> 0.1 us  [local(): long_own = jnp.sum(parts.astype(F32), axis=0)]
    ppermute x0 -> x6, starting transfers between devices: none -> 13.6 us  [swapped(): lax.ppermute(block, axis, [(i, i ^ bit) for i in range(lax.axis_size(axis...]
  transfers between devices with their start and end apart: 4 -> 9, of which waited for: 1 -> 1; matrix products, arithmetic and copies ran while one was open for 61% -> 9% of each run, Pallas kernels for 0% -> 41%
where the time goes in v1:
time: 132 us; the launch traced here: 131 us
  Pallas kernels  58.7 us (44%)
  local copies, waits for them, and re-layouts  23.9 us (18%)
  starting transfers between devices  23.3 us (18%)
  waiting for transfers between devices  14 us (11%)
  other arithmetic  6.93 us (5%)
  matrix products  3.42 us (3%)
    pallas_call x6, Pallas kernels, short_sums(): pl.pallas_call(functools.partial(short_kernel, atoms, slots), in_specs=[p...  35.9 us
    pallas_call x1, Pallas kernels, front(): pl.pallas_call(functools.partial(front_kernel, rows), grid=(atoms // bloc...  17.7 us
    all_to_all x1, waiting for transfers between devices, local(): lax.all_to_all(long_parts(p, table, ka_size), 'ka', 0, 0, tiled=True)  14 us
    ppermute x6, starting transfers between devices, swapped(): lax.ppermute(block, axis, [(i, i ^ bit) for i in range(lax.axis_size(axis...  13.6 us
    unnamed x34, local copies, waits for them, and re-layouts  12.4 us
    all_to_all x1, starting transfers between devices, local(): lax.all_to_all(long_parts(p, table, ka_size), 'ka', 0, 0, tiled=True)  6.35 us
    pallas_call x1, Pallas kernels, long_parts(): pl.pallas_call(long_kernel, grid=(parts,), in_specs=[pl.BlockSpec((channe...  5.03 us
    ppermute x2, starting transfers between devices, shifted(): return lax.ppermute(block, axis, route)  3.33 us
  transfers between devices with their start and end apart: 9, of which 1 were waited for; matrix products, arithmetic and copies ran while one was open for 9% of the time, Pallas kernels for 41%

profile of v1, /device:TPU:1, one launch (start us, length us, event | category | flops | bytes accessed | tf_op | source)
XLA Modules:
  0.0 131.3 jit_solution(5981420962715677157)
XLA Ops:
  0.6 0.0 copy-start
  0.6 0.8 slice_reduce_fusion.1
  1.5 1.5 %convolution_convert_fusion.1 = bf16[64,6144]{1,0:T(8,128)(2,1)S(1)} fusion(bf16[64,64]{1,0:T(8,128)(2,1)} %param.21, bf16[64,6144]{1,0:T(8,128)(2,1)} %grad_ref.1), kind=kOutput, calls=%fused_computation.4 | convolution fusion | flops 50724864 | bytes 1581056 | tf_op jit(solution)/shard_map/dot_general | solution.py:182
  3.0 0.0 copy-start.12
  3.0 1.6 %copy.24 = bf16[64,6144]{0,1:T(8,128)(2,1)} copy(bf16[64,6144]{1,0:T(8,128)(2,1)S(1)} %convolution_convert_fusion.1) | data formatting | bytes 1572864 | tf_op jit(solution)/shard_map/convert_element_type | solution.py:182
  4.6 3.3 %gather_fusion.1 = bf16[768,64]{1,0:T(8,128)(2,1)S(1)} fusion(bf16[64,6144]{0,1:T(8,128)(2,1)} %copy.24, s32[1024]{0:T(1024)S(1)} %pad_clamp_fusion), kind=kCustom, calls=%fused_computation.1.clone | custom fusion | bytes 199680 | tf_op jit(solution)/shard_map/jit(_take)/gather | solution.py:184
  7.9 0.2 select_bitcast_fusion
  8.1 3.3 %collective-permute-start.2 = (bf16[64,768]{0,1:T(8,128)(2,1)S(1)}, bf16[64,768]{0,1:T(8,128)(2,1)}, u32[]{:S(2)}, u32[]{:S(2)}) collective-permute-start(bf16[64,768]{0,1:T(8,128)(2,1)S(1)} %select_bitcast_fusion), channel_id=1, source_target_pairs={{8,0},{16,8},{24,16},{32,24},{40,32},{48,40},{56,48},{64,56},{72,6... | collective-permute-start | bytes 294920 | tf_op jit(solution)/shard_map/ppermute | solution.py:34
  11.4 3.2 %gather_fusion = bf16[768,64]{1,0:T(8,128)(2,1)S(1)} fusion(bf16[64,6144]{0,1:T(8,128)(2,1)} %copy.24, s32[1024]{0:T(1024)S(1)} %pad_clamp_fusion.1), kind=kCustom, calls=%fused_computation.clone | custom fusion | bytes 199680 | tf_op jit(solution)/shard_map/jit(_take)/gather | solution.py:183
  14.6 0.9 select_bitcast_fusion.1
  15.5 0.0 collective-permute-start.1
  15.5 0.0 copy-done.12
  15.5 0.1 pad.21.clone
  15.6 0.1 maximum_maximum_fusion
  15.7 0.1 copy.21.k_ref
  15.8 0.0 copy-done.5
  15.8 0.0 copy-done.6
  15.8 0.0 copy-start.11
  15.8 17.7 %structure_sums.1 = (f32[64,1024]{1,0:T(8,128)S(1)}, bf16[1024,6144]{1,0:T(8,128)(2,1)S(1)}) custom-call(bf16[64,64]{1,0:T(8,128)(2,1)S(1)} %copy-done.7, bf16[64,6144]{1,0:T(8,128)(2,1)S(1)} %copy-done.5, f32[3,6144]{1,0:T(4,128)S(1)} %copy-done.6, bf16[512,16]{1,0:T(8,128)(2,1)S(1)} %copy.21.k_ref), custom_call_target="tpu_custom_call" | custom-call | flops 20000000000 | bytes 14000000 | tf_op jit(solution)/shard_map/structure_sums/pallas_call | solution.py:74
  33.5 4.5 %copy-done.3 = bf16[1024,6144]{1,0:T(8,128)(2,1)} copy-done((bf16[1024,6144]{1,0:T(8,128)(2,1)}, bf16[1024,6144]{1,0:T(8,128)(2,1)S(1)}, u32[]{:S(2)}) %copy-start.3) | copy-done | bytes 12582936
  38.1 0.6 dynamic-slice_convert_fusion
  38.7 0.8 constant_dynamic-slice_fusion.6
  39.5 4.6 %collective-permute-start = (bf16[32,1024]{1,0:T(8,128)(2,1)}, bf16[32,1024]{1,0:T(8,128)(2,1)}, u32[]{:S(2)}, u32[]{:S(2)}) collective-permute-start(bf16[32,1024]{1,0:T(8,128)(2,1)} %dynamic-slice_convert_fusion), channel_id=1, source_target_pairs={{0,8},{8,0},{16,24},{24,16},{32,40},{40,32},{48,56},{56,48},{64,72... | collective-permute-start | bytes 196616 | tf_op jit(solution)/shard_map/ppermute | solution.py:28
  44.1 1.9 %fusion = bf16[6144,128]{1,0:T(8,128)(2,1)} fusion(bf16[64,6144]{1,0:T(8,128)(2,1)S(1)} %copy-done.5, bf16[64,64]{1,0:T(8,128)(2,1)S(1)} %copy-done.11), kind=kOutput, calls=%fused_computation.3 | convolution fusion | flops 101449728 | bytes 2367488 | tf_op jit(solution)/shard_map/dot_general | solution.py:179
  46.0 0.8 dynamic_slice.22
  46.8 0.2 copy.30
  47.0 0.2 fusion.6
  47.2 0.0 collective-permute-done.2
  47.2 0.0 collective-permute-done.1
  47.2 1.1 maximum_bitcast_fusion
  48.3 1.7 %fusion.3 = f32[7680,128]{1,0:T(8,128)S(1)} fusion(bf16[1536,64]{1,0:T(8,128)(2,1)S(1)} %maximum_bitcast_fusion, bf16[6144,128]{1,0:T(8,128)(2,1)} %fusion), kind=kLoop, calls=%fused_computation.8 | loop fusion | flops 5898240 | bytes 5701632 | tf_op jit(solution)/shard_map/broadcast_in_dim | solution.py:187
  50.0 0.0 copy-start.1
  50.0 6.0 %short_sums.6 = f32[128,128]{1,0:T(8,128)S(1)} custom-call(s32[6144]{0:T(1024)S(1)} %bitcast.59, f32[128,48]{1,0:T(8,128)S(1)} %get-tuple-element.86.weight_ref, f32[7680,1,128]{2,1,0:T(1,128)S(1)} %bitcast.48), custom_call_target="tpu_custom_call" | custom-call | flops 614400000 | bytes 4000000 | tf_op jit(solution)/shard_map/short_sums/pallas_call | solution.py:142
  56.0 0.0 collective-permute-done
  56.0 0.9 add_convert_fusion.3
  56.9 0.1 collective-permute-start.3
  57.0 6.0 %short_sums.7 = f32[128,128]{1,0:T(8,128)S(1)} custom-call(s32[6144]{0:T(1024)S(1)} %bitcast.58, f32[128,48]{1,0:T(8,128)S(1)} %get-tuple-element.85.weight_ref, f32[7680,1,128]{2,1,0:T(1,128)S(1)} %bitcast.49), custom_call_target="tpu_custom_call" | custom-call | flops 614400000 | bytes 4000000 | tf_op jit(solution)/shard_map/short_sums/pallas_call | solution.py:142
  63.0 0.0 collective-permute-done.3
  63.0 1.2 collective-permute-start.4
  64.3 6.0 %short_sums.8 = f32[128,128]{1,0:T(8,128)S(1)} custom-call(s32[6144]{0:T(1024)S(1)} %bitcast.57, f32[128,48]{1,0:T(8,128)S(1)} %get-tuple-element.84.weight_ref, f32[7680,1,128]{2,1,0:T(1,128)S(1)} %bitcast.50), custom_call_target="tpu_custom_call" | custom-call | flops 614400000 | bytes 4000000 | tf_op jit(solution)/shard_map/short_sums/pallas_call | solution.py:142
  70.3 0.0 collective-permute-done.4
  70.3 4.7 %collective-permute-start.5 = (bf16[32,1024]{1,0:T(8,128)(2,1)S(1)}, bf16[32,1024]{1,0:T(8,128)(2,1)S(1)}, u32[]{:S(2)}, u32[]{:S(2)}) collective-permute-start(bf16[32,1024]{1,0:T(8,128)(2,1)S(1)} %add_convert_fusion.1), channel_id=1, source_target_pairs={{0,64},{8,72},{16,80},{24,88},{32,96},{40,104},{48,112},{56,120},{... | collective-permute-start | bytes 196616 | tf_op jit(solution)/shard_map/ppermute | solution.py:28
  75.0 6.0 %short_sums.9 = f32[128,128]{1,0:T(8,128)S(1)} custom-call(s32[6144]{0:T(1024)S(1)} %bitcast.56, f32[128,48]{1,0:T(8,128)S(1)} %get-tuple-element.83.weight_ref, f32[7680,1,128]{2,1,0:T(1,128)S(1)} %bitcast.51), custom_call_target="tpu_custom_call" | custom-call | flops 614400000 | bytes 4000000 | tf_op jit(solution)/shard_map/short_sums/pallas_call | solution.py:142
  81.0 0.0 collective-permute-done.5
  81.1 1.3 collective-permute-start.6
  82.4 6.0 %short_sums.10 = f32[128,128]{1,0:T(8,128)S(1)} custom-call(s32[6144]{0:T(1024)S(1)} %bitcast.55, f32[128,48]{1,0:T(8,128)S(1)} %get-tuple-element.82.weight_ref, f32[7680,1,128]{2,1,0:T(1,128)S(1)} %bitcast.52), custom_call_target="tpu_custom_call" | custom-call | flops 614400000 | bytes 4000000 | tf_op jit(solution)/shard_map/short_sums/pallas_call | solution.py:142
  88.4 0.0 collective-permute-done.6
  88.4 1.7 %collective-permute-start.7 = (f32[32,1024]{1,0:T(8,128)S(1)}, f32[32,1024]{1,0:T(8,128)S(1)}, u32[]{:S(2)}, u32[]{:S(2)}) collective-permute-start(f32[32,1024]{1,0:T(8,128)S(1)} %convert_add_fusion), channel_id=1, source_target_pairs={{0,8},{8,0},{16,24},{24,16},{32,40},{40,32},{48,56},{56,48},{64,72... | collective-permute-start | bytes 393224 | tf_op jit(solution)/shard_map/ppermute | solution.py:28
  90.1 2.1 %copy-done.2 = f32[7680,128]{1,0:T(8,128)S(1)} copy-done((f32[7680,128]{1,0:T(8,128)S(1)}, f32[7680,128]{1,0:T(8,128)}, u32[]{:S(2)}) %copy-start.2) | copy-done | bytes 3932184
  92.2 6.0 %short_sums.11 = f32[128,128]{1,0:T(8,128)S(1)} custom-call(s32[6144]{0:T(1024)S(1)} %bitcast.54, f32[128,48]{1,0:T(8,128)S(1)} %get-tuple-element.81.weight_ref, f32[7680,1,128]{2,1,0:T(1,128)S(1)} %bitcast.53), custom_call_target="tpu_custom_call" | custom-call | flops 614400000 | bytes 4000000 | tf_op jit(solution)/shard_map/short_sums/pallas_call | solution.py:142
  98.2 0.0 collective-permute-done.7
  98.2 0.0 copy-done.9
  98.3 0.0 copy-done.10
  98.3 0.7 multiply_convert_fusion.1
  99.0 0.0 copy-start.4
  99.0 4.6 %copy-done.4 = bf16[1024,6144]{1,0:T(8,128)(2,1)S(1)} copy-done((bf16[1024,6144]{1,0:T(8,128)(2,1)S(1)}, bf16[1024,6144]{1,0:T(8,128)(2,1)}, u32[]{:S(2)}) %copy-start.4) | copy-done | bytes 12582936
  103.6 5.0 %long_parts.1 = bf16[8,64,768]{2,1,0:T(8,128)(2,1)} custom-call(bf16[64,1024]{1,0:T(8,128)(2,1)S(1)} %pad_maximum_fusion.p_ref, bf16[1024,6144]{1,0:T(8,128)(2,1)S(1)} %copy-done.4), custom_call_target="tpu_custom_call" | custom-call | flops 800000000 | bytes 14000000 | tf_op jit(solution)/shard_map/long_parts/pallas_call | solution.py:106
  108.6 6.4 %all-to-all-start = ((bf16[8,64,768]{2,1,0:T(8,128)(2,1)}), bf16[8,64,768]{2,1,0:T(8,128)(2,1)S(1)}, u32[]{:S(2)}, u32[]{:S(2)}) async-start(bf16[8,64,768]{2,1,0:T(8,128)(2,1)} %long_parts.1), calls=%async_computation | async-start | bytes 1572864 | tf_op jit(solution)/shard_map/all_to_all | solution.py:232
  115.0 0.2 copy.29
  115.2 14.0 %all-to-all-done = bf16[8,64,768]{2,1,0:T(8,128)(2,1)S(1)} async-done(((bf16[8,64,768]{2,1,0:T(8,128)(2,1)}), bf16[8,64,768]{2,1,0:T(8,128)(2,1)S(1)}, u32[]{:S(2)}, u32[]{:S(2)}) %all-to-all-start) | async-done | bytes 786464 | tf_op jit(solution)/shard_map/all_to_all | solution.py:232
  129.2 0.1 convert_reduce_fusion
  129.3 0.2 copy.26
  129.5 1.1 fusion.5
  130.5 0.8 copy.27
  (36 shorter events, 0.3 us)
Async XLA Ops:
  0.6 46.2 %copy-start = (f32[48,6144]{1,0:T(8,128)S(1)}, f32[48,6144]{1,0:T(8,128)}, u32[]{:S(2)}) copy-start(f32[48,6144]{1,0:T(8,128)} %param.22) | copy-start | bytes 3538948
  3.0 12.5 %copy-start.12 = (s32[3,512]{1,0:T(4,128)S(1)}, s32[3,512]{1,0:T(4,128)}, u32[]{:S(2)}) copy-start(s32[3,512]{1,0:T(4,128)} %param.17) | copy-start | bytes 18436
  4.6 11.2 %copy-start.5 = (bf16[64,6144]{1,0:T(8,128)(2,1)S(1)}, bf16[64,6144]{1,0:T(8,128)(2,1)}, u32[]{:S(2)}) copy-start(bf16[64,6144]{1,0:T(8,128)(2,1)} %grad_ref.1) | copy-start | bytes 2359300
  4.6 11.2 %copy-start.6 = (f32[3,6144]{1,0:T(4,128)S(1)}, f32[3,6144]{1,0:T(4,128)}, u32[]{:S(2)}) copy-start(f32[3,6144]{1,0:T(4,128)} %frac_ref.1) | copy-start | bytes 221188
  4.6 11.2 %copy-start.7 = (bf16[64,64]{1,0:T(8,128)(2,1)S(1)}, bf16[64,64]{1,0:T(8,128)(2,1)}, u32[]{:S(2)}) copy-start(bf16[64,64]{1,0:T(8,128)(2,1)} %mix_ref.1) | copy-start | bytes 24580
  8.1 39.2 %collective-permute-start.2 = (bf16[64,768]{0,1:T(8,128)(2,1)S(1)}, bf16[64,768]{0,1:T(8,128)(2,1)}, u32[]{:S(2)}, u32[]{:S(2)}) collective-permute-start(bf16[64,768]{0,1:T(8,128)(2,1)S(1)} %select_bitcast_fusion), channel_id=1, source_target_pairs={{8,0},{16,8},{24,16},{32,24},{40,32},{48,40},{56,48},{64,56},{72,6... | collective-permute-start | bytes 294920 | tf_op jit(solution)/shard_map/ppermute | solution.py:34
  15.5 31.7 %collective-permute-start.1 = (bf16[64,768]{0,1:T(8,128)(2,1)}, bf16[64,768]{0,1:T(8,128)(2,1)}, u32[]{:S(2)}, u32[]{:S(2)}) collective-permute-start(bf16[64,768]{0,1:T(8,128)(2,1)} %select_bitcast_fusion.1), channel_id=1, source_target_pairs={{248,0},{0,8},{8,16},{16,24},{24,32},{32,40},{40,48},{48,56},{56,6... | collective-permute-start | bytes 294920 | tf_op jit(solution)/shard_map/ppermute | solution.py:34
  15.8 28.3 %copy-start.11 = (bf16[64,64]{1,0:T(8,128)(2,1)S(1)}, bf16[64,64]{1,0:T(8,128)(2,1)}, u32[]{:S(2)}) copy-start(bf16[64,64]{1,0:T(8,128)(2,1)} %param.21) | copy-start | bytes 24580
  33.5 4.5 %copy-start.3 = (bf16[1024,6144]{1,0:T(8,128)(2,1)}, bf16[1024,6144]{1,0:T(8,128)(2,1)S(1)}, u32[]{:S(2)}) copy-start(bf16[1024,6144]{1,0:T(8,128)(2,1)S(1)} %get-tuple-element.60.table_ref) | copy-start | bytes 37748740
  39.5 16.5 %collective-permute-start = (bf16[32,1024]{1,0:T(8,128)(2,1)}, bf16[32,1024]{1,0:T(8,128)(2,1)}, u32[]{:S(2)}, u32[]{:S(2)}) collective-permute-start(bf16[32,1024]{1,0:T(8,128)(2,1)} %dynamic-slice_convert_fusion), channel_id=1, source_target_pairs={{0,8},{8,0},{16,24},{24,16},{32,40},{40,32},{48,56},{56,48},{64,72... | collective-permute-start | bytes 196616 | tf_op jit(solution)/shard_map/ppermute | solution.py:28
  50.0 32.4 %copy-start.1 = (f32[7680,128]{1,0:T(8,128)}, f32[7680,128]{1,0:T(8,128)S(1)}, u32[]{:S(2)}) copy-start(f32[7680,128]{1,0:T(8,128)S(1)} %fusion.3) | copy-start | bytes 11796484
  56.9 6.1 %collective-permute-start.3 = (bf16[32,1024]{1,0:T(8,128)(2,1)S(1)}, bf16[32,1024]{1,0:T(8,128)(2,1)S(1)}, u32[]{:S(2)}, u32[]{:S(2)}) collective-permute-start(bf16[32,1024]{1,0:T(8,128)(2,1)S(1)} %add_convert_fusion.3), channel_id=1, source_target_pairs={{0,16},{8,24},{16,0},{24,8},{32,48},{40,56},{48,32},{56,40},{64,80... | collective-permute-start | bytes 196616 | tf_op jit(solution)/shard_map/ppermute | solution.py:28
  63.0 7.2 %collective-permute-start.4 = (bf16[32,1024]{1,0:T(8,128)(2,1)S(1)}, bf16[32,1024]{1,0:T(8,128)(2,1)S(1)}, u32[]{:S(2)}, u32[]{:S(2)}) collective-permute-start(bf16[32,1024]{1,0:T(8,128)(2,1)S(1)} %add_convert_fusion.2), channel_id=1, source_target_pairs={{0,32},{8,40},{16,48},{24,56},{32,0},{40,8},{48,16},{56,24},{64,96... | collective-permute-start | bytes 196616 | tf_op jit(solution)/shard_map/ppermute | solution.py:28
  70.3 10.7 %collective-permute-start.5 = (bf16[32,1024]{1,0:T(8,128)(2,1)S(1)}, bf16[32,1024]{1,0:T(8,128)(2,1)S(1)}, u32[]{:S(2)}, u32[]{:S(2)}) collective-permute-start(bf16[32,1024]{1,0:T(8,128)(2,1)S(1)} %add_convert_fusion.1), channel_id=1, source_target_pairs={{0,64},{8,72},{16,80},{24,88},{32,96},{40,104},{48,112},{56,120},{... | collective-permute-start | bytes 196616 | tf_op jit(solution)/shard_map/ppermute | solution.py:28
  81.1 7.3 %collective-permute-start.6 = (bf16[32,1024]{1,0:T(8,128)(2,1)S(1)}, bf16[32,1024]{1,0:T(8,128)(2,1)S(1)}, u32[]{:S(2)}, u32[]{:S(2)}) collective-permute-start(bf16[32,1024]{1,0:T(8,128)(2,1)S(1)} %add_convert_fusion), channel_id=1, source_target_pairs={{0,128},{8,136},{16,144},{24,152},{32,160},{40,168},{48,176},{56,1... | collective-permute-start | bytes 196616 | tf_op jit(solution)/shard_map/ppermute | solution.py:28
  88.4 9.8 %collective-permute-start.7 = (f32[32,1024]{1,0:T(8,128)S(1)}, f32[32,1024]{1,0:T(8,128)S(1)}, u32[]{:S(2)}, u32[]{:S(2)}) collective-permute-start(f32[32,1024]{1,0:T(8,128)S(1)} %convert_add_fusion), channel_id=1, source_target_pairs={{0,8},{8,0},{16,24},{24,16},{32,40},{40,32},{48,56},{56,48},{64,72... | collective-permute-start | bytes 393224 | tf_op jit(solution)/shard_map/ppermute | solution.py:28
  90.1 2.1 %copy-start.2 = (f32[7680,128]{1,0:T(8,128)S(1)}, f32[7680,128]{1,0:T(8,128)}, u32[]{:S(2)}) copy-start(f32[7680,128]{1,0:T(8,128)} %copy-done.1) | copy-start | bytes 11796484
  92.2 6.0 %copy-start.9 = (f32[2,64,512]{2,1,0:T(8,128)S(1)}, f32[2,64,512]{2,1,0:T(8,128)}, u32[]{:S(2)}) copy-start(f32[2,64,512]{2,1,0:T(8,128)} %param.19) | copy-start | bytes 786436
  92.2 6.1 %copy-start.10 = (f32[64,512]{1,0:T(8,128)S(1)}, f32[64,512]{1,0:T(8,128)}, u32[]{:S(2)}) copy-start(f32[64,512]{1,0:T(8,128)} %param.18) | copy-start | bytes 393220
  99.0 4.6 %copy-start.4 = (bf16[1024,6144]{1,0:T(8,128)(2,1)S(1)}, bf16[1024,6144]{1,0:T(8,128)(2,1)}, u32[]{:S(2)}) copy-start(bf16[1024,6144]{1,0:T(8,128)(2,1)} %copy-done.3) | copy-start | bytes 37748740
  108.6 20.6 %all-to-all-start = ((bf16[8,64,768]{2,1,0:T(8,128)(2,1)}), bf16[8,64,768]{2,1,0:T(8,128)(2,1)S(1)}, u32[]{:S(2)}, u32[]{:S(2)}) async-start(bf16[8,64,768]{2,1,0:T(8,128)(2,1)} %long_parts.1), calls=%async_computation | async-start | bytes 1572864 | tf_op jit(solution)/shard_map/all_to_all | solution.py:232
  115.2 14.0 %copy-start.8 = (f32[768,128]{1,0:T(8,128)}, f32[768,128]{1,0:T(8,128)S(1)}, u32[]{:S(2)}) copy-start(f32[768,128]{1,0:T(8,128)S(1)} %constant_dynamic-update-slice_fusion) | copy-start | bytes 1179652

commit v2 on v1

v2 whole, which is shorter than its diff:
```python
import functools
import math

import jax
import jax.numpy as jnp
import numpy as np
from jax import lax
from jax.experimental import pallas as pl
from jax.experimental.pallas import tpu as pltpu
from jax.sharding import PartitionSpec as P

BF16 = jnp.bfloat16
F32 = jnp.float32
LANES = 128


def even_fit(function, terms):
    u = np.cos(np.pi * (np.arange(200) + 0.5) / 200) * 0.125 + 0.125
    fitted = np.polynomial.chebyshev.Chebyshev.fit(u, function(np.sqrt(u)), terms - 1, domain=[0, 0.25])
    return [float(c) for c in fitted.convert(kind=np.polynomial.Polynomial).coef]


SIN_HALF = even_fit(lambda r: math.sqrt(2) * np.sin(np.pi * r) / r, 4)
COS_HALF = even_fit(lambda r: math.sqrt(2) * np.cos(np.pi * r), 4)


def swapped(block, axis, bit):
    return lax.ppermute(block, axis, [(i, i ^ bit) for i in range(lax.axis_size(axis))])


def shifted(block, axis, distance):
    devices = range(lax.axis_size(axis))
    route = [((i - distance) % len(devices), i) for i in devices]
    return lax.ppermute(block, axis, route)


def front_kernel(
    rows, mix_ref, grad_ref, frac_ref, k_ref, q_ref, whole_ref, pieces_ref, turns_ref, held_ref, sems
):
    step, last = pl.program_id(0), pl.num_programs(0) - 1
    slot = lax.rem(step, 2)
    table_ref = held_ref.at[slot]
    block = grad_ref.shape[1]

    def keep(at, slot):
        columns = pl.ds(pl.multiple_of(at * block, block), block)
        return pltpu.make_async_copy(held_ref.at[slot], whole_ref.at[:, columns], sems.at[slot])

    @pl.when(step == 0)
    def _():
        q_ref[...] = jnp.zeros_like(q_ref)
        pieces_ref[...] = jnp.zeros_like(pieces_ref)

    @pl.when(step >= 2)
    def _():
        keep(step - 2, slot).wait()

    frac = frac_ref[...]
    high = frac.astype(BF16).astype(F32)
    rest = frac - high
    middle = rest.astype(BF16).astype(F32)
    pieces_ref[0:3, :] = high
    pieces_ref[3:6, :] = middle
    pieces_ref[6:9, :] = rest - middle
    turns_ref[...] = jnp.dot(k_ref[...], pieces_ref[...].astype(BF16), preferred_element_type=F32)
    cot = jnp.dot(mix_ref[...], grad_ref[...], preferred_element_type=F32).astype(BF16)
    k_count = k_ref.shape[0]

    def fill(i, carry):
        first = pl.multiple_of(i * rows, rows)
        turns = turns_ref[pl.ds(first, rows), :]
        r = turns - jnp.round(turns)
        u = r * r
        s = r * (SIN_HALF[0] + u * (SIN_HALF[1] + u * (SIN_HALF[2] + u * SIN_HALF[3])))
        c = COS_HALF[0] + u * (COS_HALF[1] + u * (COS_HALF[2] + u * COS_HALF[3]))
        table_ref[pl.ds(first, rows), :] = (1.0 - s * s).astype(BF16)
        table_ref[pl.ds(first + k_count, rows), :] = (s * c).astype(BF16)
        return carry

    lax.fori_loop(0, k_count // rows, fill, 0, unroll=2)
    q_ref[...] += lax.dot_general(
        cot, table_ref[...], (((1,), (1,)), ((), ())), preferred_element_type=F32
    )
    keep(step, slot).start()

    @pl.when(step == last)
    def _():
        keep(step - 1, 1 - slot).wait()
        keep(step, slot).wait()


def front(mix, grad, frac, k_triple, rows=16, block=1024):
    channels, atoms = grad.shape
    k_count = k_triple.shape[0]
    return pl.pallas_call(
        functools.partial(front_kernel, rows),
        grid=(atoms // block,),
        in_specs=[
            pl.BlockSpec((channels, channels), lambda i: (0, 0)),
            pl.BlockSpec((channels, block), lambda i: (0, i)),
            pl.BlockSpec((3, block), lambda i: (0, i)),
            pl.BlockSpec((k_count, 16), lambda i: (0, 0)),
        ],
        out_specs=[
            pl.BlockSpec((channels, 2 * k_count), lambda i: (0, 0)),
            pl.BlockSpec(memory_space=pltpu.HBM),
        ],
        out_shape=[
            jax.ShapeDtypeStruct((channels, 2 * k_count), F32),
            pltpu.HBM((2 * k_count, atoms), BF16),
        ],
        scratch_shapes=[
            pltpu.VMEM((16, block), F32),
            pltpu.VMEM((k_count, block), F32),
            pltpu.VMEM((2, 2 * k_count, block), BF16),
            pltpu.SemaphoreType.DMA((2,)),
        ],
        compiler_params=pltpu.CompilerParams(vmem_limit_bytes=12 << 20),
        cost_estimate=pl.CostEstimate(flops=20_000_000_000, bytes_accessed=14_000_000, transcendentals=0),
        name="structure_sums",
    )(mix, grad, frac, k_triple)


def long_kernel(p_ref, table_ref, out_ref, held_ref, sems):
    parts, _, own = out_ref.shape
    depth = held_ref.shape[0]

    def fetch(at):
        columns = slice(at * own, (at + 1) * own)
        return pltpu.make_async_copy(
            table_ref.at[:, columns], held_ref.at[at % depth], sems.at[at % depth]
        )

    for at in range(depth - 1):
        fetch(at).start()
    for at in range(parts):
        if at + depth - 1 < parts:
            fetch(at + depth - 1).start()
        fetch(at).wait()
        out_ref[at] = jnp.dot(
            p_ref[...], held_ref[at % depth], preferred_element_type=F32
        ).astype(BF16)


def long_parts(p, table, parts):
    channels, depth = p.shape
    own = table.shape[1] // parts
    return pl.pallas_call(
        long_kernel,
        in_specs=[pl.BlockSpec(memory_space=pltpu.VMEM), pl.BlockSpec(memory_space=pltpu.HBM)],
        out_specs=pl.BlockSpec(memory_space=pltpu.VMEM),
        out_shape=jax.ShapeDtypeStruct((parts, channels, own), BF16),
        scratch_shapes=[pltpu.VMEM((4, depth, own), BF16), pltpu.SemaphoreType.DMA((4,))],
        compiler_params=pltpu.CompilerParams(vmem_limit_bytes=12 << 20),
        cost_estimate=pl.CostEstimate(flops=800_000_000, bytes_accessed=14_000_000, transcendentals=0),
        name="long_parts",
    )(p, table)


def prepare_kernel(
    ka_ref, halo_ref, mix_ref, grad_ref, index_ref, weight_ref, count_ref,
    rows_ref, send_ref, slots_ref, masked_ref, picked_ref,
):
    atoms = grad_ref.shape[1]
    block = math.gcd(atoms, 512)
    sends, per_side = send_ref.shape[0], halo_ref.shape[1]

    def mix(i, carry):
        first = pl.multiple_of(i * block, block)
        mixed = lax.dot_general(
            grad_ref[:, pl.ds(first, block)], mix_ref[...], (((0,), (1,)), ((), ())),
            preferred_element_type=F32,
        )
        rows_ref[pl.ds(first, block), :] = mixed.astype(BF16).astype(F32)
        return carry

    lax.fori_loop(0, atoms // block, mix, 0)

    for side in range(2):
        def pick(i, carry, side=side):
            first = pl.multiple_of(i * 32, 32)
            for j in range(32):
                picked_ref[pl.ds(side * per_side + first + j, 1), :] = rows_ref[
                    pl.ds(halo_ref[side, first + j], 1), :
                ]
            return carry

        lax.fori_loop(0, per_side // 32, pick, 0)
    send_ref[...] = picked_ref[...].astype(BF16)

    slot = lax.broadcasted_iota(jnp.int32, weight_ref.shape, 0)
    masked = jnp.where(slot < count_ref[...], weight_ref[...], 0.0)
    for piece in range(slots_ref.shape[0]):
        cut = slice(piece * LANES, (piece + 1) * LANES)
        slots_ref[piece] = index_ref[:, cut]
        masked_ref[cut, :] = masked[:, cut].T


def prepare(ka, mix_wide, grad, index, weight, count, halo):
    channels, atoms = grad.shape
    slots = index.shape[0]
    per_side = halo.shape[1]
    own = atoms // lax.axis_size("ka")
    whole = pl.BlockSpec(memory_space=pltpu.VMEM)
    return pl.pallas_call(
        prepare_kernel,
        grid_spec=pltpu.PrefetchScalarGridSpec(
            num_scalar_prefetch=1,
            grid=(1,),
            in_specs=[
                pl.BlockSpec(memory_space=pltpu.SMEM),
                whole,
                whole,
                pl.BlockSpec((slots, own), lambda i, ka: (0, ka[0])),
                pl.BlockSpec((slots, own), lambda i, ka: (0, ka[0])),
                pl.BlockSpec((1, own), lambda i, ka: (0, ka[0])),
            ],
            out_specs=[whole, whole, whole, whole],
            scratch_shapes=[pltpu.VMEM((2 * per_side, LANES), F32)],
        ),
        out_shape=[
            jax.ShapeDtypeStruct((atoms + 2 * per_side, LANES), F32),
            jax.ShapeDtypeStruct((2 * per_side, LANES), BF16),
            jax.ShapeDtypeStruct((own // LANES, slots, LANES), jnp.int32),
            jax.ShapeDtypeStruct((own, slots), F32),
        ],
        compiler_params=pltpu.CompilerParams(vmem_limit_bytes=12 << 20),
        cost_estimate=pl.CostEstimate(flops=1_000_000_000, bytes_accessed=8_000_000, transcendentals=0),
        name="prepare",
    )(ka, halo, mix_wide, grad, index, weight, count)


def short_kernel(index_ref, weight_ref, rows_ref, out_ref, sums_ref):
    sublane = lax.broadcasted_iota(jnp.int32, (8, LANES), 0)

    def group(g, carry):
        first = pl.multiple_of(g * 8, 8)
        weights = weight_ref[pl.ds(first, 8), :]
        total = jnp.zeros((8, LANES), F32)
        for s in range(index_ref.shape[1]):
            picked = jnp.broadcast_to(rows_ref[index_ref[0, s, first]], (8, LANES))
            for a in range(1, 8):
                row = jnp.broadcast_to(rows_ref[index_ref[0, s, first + a]], (8, LANES))
                picked = jnp.where(sublane == a, row, picked)
            total = total + picked * weights[:, s : s + 1]
        sums_ref[pl.ds(first, 8), :] = total
        return carry

    lax.fori_loop(0, LANES // 8, group, 0)
    out_ref[...] = sums_ref[...].T[: out_ref.shape[0], :]


def short_sums(piece, channels, index, weight, rows):
    slots = index.shape[1]
    return pl.pallas_call(
        short_kernel,
        grid=(1,),
        in_specs=[
            pl.BlockSpec((1, slots, LANES), lambda i: (piece, 0, 0), memory_space=pltpu.SMEM),
            pl.BlockSpec((LANES, slots), lambda i: (piece, 0)),
            pl.BlockSpec(memory_space=pltpu.VMEM),
        ],
        out_specs=pl.BlockSpec(memory_space=pltpu.VMEM),
        out_shape=jax.ShapeDtypeStruct((channels, LANES), F32),
        scratch_shapes=[pltpu.VMEM((LANES, LANES), F32)],
        compiler_params=pltpu.CompilerParams(vmem_limit_bytes=6 << 20),
        cost_estimate=pl.CostEstimate(flops=4_000_000_000, bytes_accessed=4_000_000, transcendentals=0),
        name="short_sums",
    )(index, weight, rows)


def local(
    grad_out,
    frac_pos,
    k_index,
    ewald_filter,
    struct_fac,
    out_weight,
    pair_mix,
    pair_weight,
    nbr_index,
    nbr_count,
    halo_send,
):
    channels, local_atoms = grad_out.shape
    ka_size, dom_size = lax.axis_size("ka"), lax.axis_size("dom")
    own_rows = local_atoms // ka_size
    k_count = k_index.shape[1]

    ka = lax.axis_index("ka").astype(jnp.int32)
    mix_wide = jnp.pad(pair_mix, ((0, LANES - channels), (0, 0)))
    rows, send, slots, masked = prepare(
        ka[None], mix_wide, grad_out, nbr_index, pair_weight, nbr_count[None, :], halo_send
    )
    per_side = halo_send.shape[1]
    from_left = shifted(send[:per_side], "dom", 1)
    from_right = shifted(send[per_side:], "dom", -1)
    short = []

    def short_piece():
        short.append(short_sums(len(short), channels, slots, masked, extended))

    def beside(value, bit, pieces):
        nonlocal slots
        value, slots = lax.optimization_barrier((value, slots))
        received = swapped(value, "dom", bit)
        start = len(short)
        for _ in range(pieces):
            short_piece()
        received, short[start:] = lax.optimization_barrier((received, short[start:]))
        return received.astype(F32)

    k_rows = k_index.astype(BF16).T
    k_triple = jnp.concatenate([k_rows, k_rows, k_rows, jnp.zeros((k_count, 7), BF16)], axis=1)
    frac_late, send_late = lax.optimization_barrier((frac_pos, send))
    q, table = front(out_weight, grad_out, frac_late, k_triple)
    q, from_left, from_right = lax.optimization_barrier((q, from_left, from_right))
    extended = jnp.concatenate(
        [rows[:local_atoms], from_left.astype(F32), from_right.astype(F32)], axis=0
    )[:, None, :]

    half = channels // 2
    core = lax.axis_index("dom") % 2
    mine = lax.dynamic_slice_in_dim(q, core * half, half, 0)
    other = lax.dynamic_slice_in_dim(q, (1 - core) * half, half, 0)
    total = mine + beside(other.astype(BF16), 1, 0)
    bit = 2
    while bit < dom_size:
        rounded = total.astype(BF16)
        total = rounded.astype(F32) + beside(rounded, bit, 1)
        bit *= 2
    partner = beside(total, 1, 0)
    q = jnp.where(
        core == 0,
        jnp.concatenate([total, partner], axis=0),
        jnp.concatenate([partner, total], axis=0),
    )
    q_cos, q_sin = q[:, :k_count], q[:, k_count:]
    atom_total = local_atoms * dom_size
    d_filter = (struct_fac[0] * q_cos + struct_fac[1] * q_sin) / atom_total
    p = jnp.concatenate([ewald_filter * q_cos, ewald_filter * q_sin], axis=1).astype(BF16)

    parts = long_parts(p, table, ka_size)
    parts, slots = lax.optimization_barrier((parts, slots))
    parts = lax.all_to_all(parts, "ka", 0, 0, tiled=True)
    while len(short) < own_rows // LANES:
        short_piece()
    long_own = jnp.sum(parts.astype(F32), axis=0)
    own_grad = lax.dynamic_slice_in_dim(grad_out, ka * own_rows, own_rows, 1).astype(F32)
    d_feat = (own_grad + long_own + jnp.concatenate(short, axis=1)).astype(BF16)
    return (d_feat, d_filter)


def solution(mesh):
    return jax.shard_map(
        local,
        mesh=mesh,
        in_specs=(
            P(None, "dom"),
            P(None, "dom"),
            P(None, "ka"),
            P(None, "ka"),
            P(None, None, "ka"),
            P(),
            P(),
            P(None, "dom"),
            P(None, "dom"),
            P("dom"),
            P(None, "dom"),
        ),
        out_specs=(P(None, ("dom", "ka")), P(None, "ka")),
        check_vma=False,
    )
```

time: 132 us -> 135 us (1.023)
  Pallas kernels: 58.7 us -> 83.9 us
  local copies, waits for them, and re-layouts: 23.9 us -> 13.9 us
  waiting for transfers between devices: 14 us -> 8.01 us
  matrix products: 3.42 us -> 0 us
  other arithmetic: 6.93 us -> 3.89 us
    pallas_call x7 -> x8, Pallas kernels: 41 us -> 66.4 us  [the longest x6 53.4 us: short_sums(): pl.pallas_call(short_kernel, grid=(1,), in_specs=[pl.BlockSpec((1, slots,...]
    all_to_all x1, waiting for transfers between devices: 14 us -> 0.01 us  [local(): parts = lax.all_to_all(parts, 'ka', 0, 0, tiled=True)]
    ppermute x6, waiting for transfers between devices: 0.02 us -> 8 us  [swapped(): lax.ppermute(block, axis, [(i, i ^ bit) for i in range(lax.axis_size(axis...]
    gather x2 -> x0, local copies, waits for them, and re-layouts: 6.48 us -> none  [the longest x1 3.28 us: local(): from_right = shifted(jnp.take(sr_cot, halo_send[1], axis=1), 'dom', -1)]
    dot_general x2 -> x0, matrix products: 3.42 us -> none  [the longest x1 1.92 us: local(): lax.dot_general(grad_out, mix_wide, (((0,), (1,)), ((), ())), preferred_e...]
    unnamed x34 -> x41, local copies, waits for them, and re-layouts: 12.4 us -> 9.14 us
    convert_element_type x2 -> x1, local copies, waits for them, and re-layouts: 2.19 us -> 0.01 us  [local(): total = mine + beside(other.astype(BF16), 1, 0)]
    concatenate x0 -> x1, other arithmetic: none -> 2.14 us  [local(): jnp.concatenate([rows[:local_atoms], from_left.astype(F32), from_right.as...]
  transfers between devices with their start and end apart: 9 -> 9, of which waited for: 1 -> 3; matrix products, arithmetic and copies ran while one was open for 9% -> 5% of each run, Pallas kernels for 41% -> 39%
where the time goes in v2:
time: 135 us; the launch traced here: 134 us
  Pallas kernels  83.9 us (62%)
  starting transfers between devices  23.7 us (18%)
  local copies, waits for them, and re-layouts  13.9 us (10%)
  waiting for transfers between devices  8.01 us (6%)
  other arithmetic  3.89 us (3%)
    pallas_call x6, Pallas kernels, short_sums(): pl.pallas_call(short_kernel, grid=(1,), in_specs=[pl.BlockSpec((1, slots,...  53.4 us
    pallas_call x1, Pallas kernels, front(): pl.pallas_call(functools.partial(front_kernel, rows), grid=(atoms // bloc...  17.5 us
    ppermute x6, starting transfers between devices, swapped(): lax.ppermute(block, axis, [(i, i ^ bit) for i in range(lax.axis_size(axis...  13.9 us
    unnamed x41, local copies, waits for them, and re-layouts  9.14 us
    ppermute x6, waiting for transfers between devices, swapped(): lax.ppermute(block, axis, [(i, i ^ bit) for i in range(lax.axis_size(axis...  8 us
    pallas_call x1, Pallas kernels, prepare(): pl.pallas_call(prepare_kernel, grid_spec=pltpu.PrefetchScalarGridSpec(num...  6.68 us
    pallas_call x1, Pallas kernels, long_parts(): pl.pallas_call(long_kernel, in_specs=[pl.BlockSpec(memory_space=pltpu.VME...  6.39 us
    all_to_all x1, starting transfers between devices, local(): parts = lax.all_to_all(parts, 'ka', 0, 0, tiled=True)  6.37 us
  transfers between devices with their start and end apart: 9, of which 3 were waited for; matrix products, arithmetic and copies ran while one was open for 5% of the time, Pallas kernels for 39%

profile of v2, /device:TPU:1, one launch (start us, length us, event | category | flops | bytes accessed | tf_op | source)
XLA Modules:
  0.0 134.3 jit_solution(12367009379587209474)
XLA Ops:
  0.6 0.0 copy-start.14
  0.6 0.0 copy-start.10
  0.7 0.7 pad.4.mix_ref
  1.4 0.0 copy-start.4
  1.4 1.1 copy-done.4
  2.5 1.3 copy-done.6
  3.8 0.0 copy-start.7
  3.8 1.3 copy-done.7
  5.1 0.7 copy-done.9
  5.8 0.7 copy-done.11
  6.5 6.7 %prepare.1 = (f32[7680,128]{1,0:T(8,128)S(1)}, bf16[1536,128]{1,0:T(8,128)(2,1)S(1)}, s32[6,48,128]{2,1,0:T(8,128)S(1)}, f32[768,48]{1,0:T(8,128)S(1)}) custom-call(s32[1]{0:T(128)} %bitcast.ka_ref, s32[2,768]{1,0:T(2,128)S(1)} %copy-done.11, bf16[128,64]{1,0:T(8,128)(2,1)S(1)} %pad.4.mix_ref, bf16[64,6144]{1,0:T(8,128)(2,1)S(1)} %copy-done.4, ...), custom_call_target="tpu_custom_call" | custom-call | flops 1000000000 | bytes 8000000 | tf_op jit(solution)/shard_map/prepare/pallas_call | solution.py:205
  13.2 1.8 %copy-done.3 = f32[7680,128]{1,0:T(8,128)} copy-done((f32[7680,128]{1,0:T(8,128)}, f32[7680,128]{1,0:T(8,128)S(1)}, u32[]{:S(2)}) %copy-start.3) | copy-done | bytes 3932184
  15.1 3.1 %collective-permute-start = (bf16[768,128]{1,0:T(8,128)(2,1)S(1)}, bf16[768,128]{1,0:T(8,128)(2,1)S(1)}, u32[]{:S(2)}, u32[]{:S(2)}) collective-permute-start(bf16[768,128]{1,0:T(8,128)(2,1)S(1)} %get-tuple-element.69), channel_id=1, source_target_pairs={{248,0},{0,8},{8,16},{16,24},{24,32},{32,40},{40,48},{48,56},{56,6... | collective-permute-start | bytes 589832 | tf_op jit(solution)/shard_map/ppermute | solution.py:34
  18.2 0.3 collective-permute-start.1
  18.5 0.0 copy-done.14
  18.5 0.1 pad.17.clone
  18.6 0.1 maximum_maximum_fusion
  18.6 0.1 copy.14.k_ref
  18.8 0.0 copy-done.10
  18.8 0.0 copy-done.5
  18.8 0.0 copy-done.8
  18.8 17.5 %structure_sums.1 = (f32[64,1024]{1,0:T(8,128)S(1)}, bf16[1024,6144]{1,0:T(8,128)(2,1)}) custom-call(bf16[64,64]{1,0:T(8,128)(2,1)S(1)} %copy-done.10, bf16[64,6144]{1,0:T(8,128)(2,1)S(1)} %copy-done.5, f32[3,6144]{1,0:T(4,128)S(1)} %copy-done.8, bf16[512,16]{1,0:T(8,128)(2,1)S(1)} %copy.14.k_ref), custom_call_target="tpu_custom_call" | custom-call | flops 20000000000 | bytes 14000000 | tf_op jit(solution)/shard_map/structure_sums/pallas_call | solution.py:95
  36.3 3.7 %slice.23 = f32[6144,128]{1,0:T(8,128)} slice(f32[7680,128]{1,0:T(8,128)} %copy-done.3), slice={[0:6144], [0:128]} | slice | bytes 6291456 | tf_op jit(solution)/shard_map/slice | solution.py:319
  40.0 0.0 collective-permute-done
  40.1 0.0 collective-permute-done.1
  40.1 4.6 %collective-permute-start.2 = (bf16[32,1024]{1,0:T(8,128)(2,1)S(1)}, bf16[32,1024]{1,0:T(8,128)(2,1)S(1)}, u32[]{:S(2)}, u32[]{:S(2)}) collective-permute-start(bf16[32,1024]{1,0:T(8,128)(2,1)S(1)} %dynamic-slice_convert_fusion), channel_id=1, source_target_pairs={{0,8},{8,0},{16,24},{24,16},{32,40},{40,32},{48,56},{56,48},{64,72... | collective-permute-start | bytes 196616 | tf_op jit(solution)/shard_map/ppermute | solution.py:28
  44.7 2.1 %pad_maximum_fusion = f32[7680,128]{1,0:T(8,128)S(1)} fusion(f32[768,128]{1,0:T(8,128)S(1)} %convert_element_type.70, f32[768,128]{1,0:T(8,128)S(1)} %convert_element_type.69, f32[6144,128]{1,0:T(8,128)} %slice.23), kind=kLoop, calls=%fused_computation | loop fusion | flops 1966080 | bytes 7864320 | tf_op jit(solution)/shard_map/concatenate | solution.py:318
  46.8 0.0 copy-start
  46.9 0.0 collective-permute-done.2
  46.9 0.1 collective-permute-start.3
  47.0 8.9 %short_sums.6 = f32[64,128]{1,0:T(8,128)S(1)} custom-call(s32[6,48,128]{2,1,0:T(8,128)S(1)} %get-tuple-element.65.index_ref, f32[768,48]{1,0:T(8,128)S(1)} %get-tuple-element.43.weight_ref, f32[7680,1,128]{2,1,0:T(1,128)S(1)} %bitcast.17), custom_call_target="tpu_custom_call" | custom-call | flops 4000000000 | bytes 4000000 | tf_op jit(solution)/shard_map/short_sums/pallas_call | solution.py:255
  55.9 0.0 collective-permute-done.3
  55.9 8.9 %short_sums.7 = f32[64,128]{1,0:T(8,128)S(1)} custom-call(s32[6,48,128]{2,1,0:T(8,128)S(1)} %get-tuple-element.65.index_ref, f32[768,48]{1,0:T(8,128)S(1)} %get-tuple-element.43.weight_ref, f32[7680,1,128]{2,1,0:T(1,128)S(1)} %bitcast.18), custom_call_target="tpu_custom_call" | custom-call | flops 4000000000 | bytes 4000000 | tf_op jit(solution)/shard_map/short_sums/pallas_call | solution.py:255
  64.8 1.2 collective-permute-start.4
  66.0 3.5 %collective-permute-done.4 = bf16[32,1024]{1,0:T(8,128)(2,1)S(1)} collective-permute-done((bf16[32,1024]{1,0:T(8,128)(2,1)S(1)}, bf16[32,1024]{1,0:T(8,128)(2,1)S(1)}, u32[]{:S(2)}, u32[]{:S(2)}) %collective-permute-start.4) | collective-permute-done | bytes 65568 | tf_op jit(solution)/shard_map/ppermute | solution.py:28
  69.5 0.0 slice-start
  69.6 0.0 slice-start.1
  69.6 8.9 %short_sums.8 = f32[64,128]{1,0:T(8,128)S(1)} custom-call(s32[6,48,128]{2,1,0:T(8,128)S(1)} %get-tuple-element.65.index_ref, f32[768,48]{1,0:T(8,128)S(1)} %get-tuple-element.43.weight_ref, f32[7680,1,128]{2,1,0:T(1,128)S(1)} %bitcast.19), custom_call_target="tpu_custom_call" | custom-call | flops 4000000000 | bytes 4000000 | tf_op jit(solution)/shard_map/short_sums/pallas_call | solution.py:255
  78.5 3.6 %collective-permute-start.5 = (bf16[32,1024]{1,0:T(8,128)(2,1)S(1)}, bf16[32,1024]{1,0:T(8,128)(2,1)S(1)}, u32[]{:S(2)}, u32[]{:S(2)}) collective-permute-start(bf16[32,1024]{1,0:T(8,128)(2,1)S(1)} %add_convert_fusion.2), channel_id=1, source_target_pairs={{0,64},{8,72},{16,80},{24,88},{32,96},{40,104},{48,112},{56,120},{... | collective-permute-start | bytes 196616 | tf_op jit(solution)/shard_map/ppermute | solution.py:28
  82.1 3.5 %collective-permute-done.5 = bf16[32,1024]{1,0:T(8,128)(2,1)S(1)} collective-permute-done((bf16[32,1024]{1,0:T(8,128)(2,1)S(1)}, bf16[32,1024]{1,0:T(8,128)(2,1)S(1)}, u32[]{:S(2)}, u32[]{:S(2)}) %collective-permute-start.5) | collective-permute-done | bytes 65568 | tf_op jit(solution)/shard_map/ppermute | solution.py:28
  85.6 0.0 copy-start.12
  85.6 0.0 copy-start.13
  85.6 0.0 slice-start.2
  85.6 0.3 collective-permute-start.6
  85.9 0.0 copy-done
  85.9 8.9 %short_sums.9 = f32[64,128]{1,0:T(8,128)S(1)} custom-call(s32[6,48,128]{2,1,0:T(8,128)S(1)} %get-tuple-element.65.index_ref, f32[768,48]{1,0:T(8,128)S(1)} %get-tuple-element.43.weight_ref, f32[7680,1,128]{2,1,0:T(1,128)S(1)} %bitcast.20), custom_call_target="tpu_custom_call" | custom-call | flops 4000000000 | bytes 4000000 | tf_op jit(solution)/shard_map/short_sums/pallas_call | solution.py:255
  94.8 0.0 collective-permute-done.6
  94.9 4.1 %collective-permute-start.7 = (f32[32,1024]{1,0:T(8,128)S(1)}, f32[32,1024]{1,0:T(8,128)S(1)}, u32[]{:S(2)}, u32[]{:S(2)}) collective-permute-start(f32[32,1024]{1,0:T(8,128)S(1)} %convert_add_fusion), channel_id=1, source_target_pairs={{0,8},{8,0},{16,24},{24,16},{32,40},{40,32},{48,56},{56,48},{64,72... | collective-permute-start | bytes 393224 | tf_op jit(solution)/shard_map/ppermute | solution.py:28
  99.0 1.0 collective-permute-done.7
  100.0 0.0 copy-done.12
  100.1 0.0 copy-done.13
  100.1 0.7 multiply_convert_fusion.1
  100.8 0.0 slice-done
  100.8 0.0 slice-done.1
  100.8 0.0 slice-done.2
  100.8 6.4 %long_parts.1 = bf16[8,64,768]{2,1,0:T(8,128)(2,1)} custom-call(bf16[64,1024]{1,0:T(8,128)(2,1)S(1)} %pad_maximum_fusion.1.p_ref, bf16[1024,6144]{1,0:T(8,128)(2,1)S(1)} %bitcast.16), custom_call_target="tpu_custom_call" | custom-call | flops 800000000 | bytes 14000000 | tf_op jit(solution)/shard_map/long_parts/pallas_call | solution.py:148
  107.2 6.4 %all-to-all-start = ((bf16[8,64,768]{2,1,0:T(8,128)(2,1)}), bf16[8,64,768]{2,1,0:T(8,128)(2,1)S(1)}, u32[]{:S(2)}, u32[]{:S(2)}) async-start(bf16[8,64,768]{2,1,0:T(8,128)(2,1)} %long_parts.1), calls=%async_computation | async-start | bytes 1572864 | tf_op jit(solution)/shard_map/all_to_all | solution.py:345
  113.6 2.1 %copy-done.1 = f32[7680,128]{1,0:T(8,128)S(1)} copy-done((f32[7680,128]{1,0:T(8,128)S(1)}, f32[7680,128]{1,0:T(8,128)}, u32[]{:S(2)}) %copy-start.1) | copy-done | bytes 3932184
  115.7 8.9 %short_sums.10 = f32[64,128]{1,0:T(8,128)S(1)} custom-call(s32[6,48,128]{2,1,0:T(8,128)S(1)} %get-tuple-element.65.index_ref, f32[768,48]{1,0:T(8,128)S(1)} %get-tuple-element.43.weight_ref, f32[7680,1,128]{2,1,0:T(1,128)S(1)} %bitcast.21), custom_call_target="tpu_custom_call" | custom-call | flops 4000000000 | bytes 4000000 | tf_op jit(solution)/shard_map/short_sums/pallas_call | solution.py:255
  124.6 0.0 copy-done.2
  124.6 8.9 %short_sums.11 = f32[64,128]{1,0:T(8,128)S(1)} custom-call(s32[6,48,128]{2,1,0:T(8,128)S(1)} %get-tuple-element.65.index_ref, f32[768,48]{1,0:T(8,128)S(1)} %get-tuple-element.43.weight_ref, f32[7680,1,128]{2,1,0:T(1,128)S(1)} %bitcast.22), custom_call_target="tpu_custom_call" | custom-call | flops 4000000000 | bytes 4000000 | tf_op jit(solution)/shard_map/short_sums/pallas_call | solution.py:255
  133.5 0.0 all-to-all-done
  133.6 0.1 convert_reduce_fusion
  133.7 0.7 add_convert_fusion
  (28 shorter events, 0.3 us)
Async XLA Ops:
  0.6 17.9 %copy-start.14 = (s32[3,512]{1,0:T(4,128)S(1)}, s32[3,512]{1,0:T(4,128)}, u32[]{:S(2)}) copy-start(s32[3,512]{1,0:T(4,128)} %param.13) | copy-start | bytes 18436
  0.6 18.1 %copy-start.10 = (bf16[64,64]{1,0:T(8,128)(2,1)S(1)}, bf16[64,64]{1,0:T(8,128)(2,1)}, u32[]{:S(2)}) copy-start(bf16[64,64]{1,0:T(8,128)(2,1)} %mix_ref.1) | copy-start | bytes 24580
  1.4 1.1 copy-start.4
  2.5 1.3 copy-start.6
  3.8 1.3 copy-start.7
  5.1 0.7 copy-start.9
  5.8 0.7 copy-start.11
  6.5 12.3 %copy-start.5 = (bf16[64,6144]{1,0:T(8,128)(2,1)S(1)}, bf16[64,6144]{1,0:T(8,128)(2,1)}, u32[]{:S(2)}) copy-start(bf16[64,6144]{1,0:T(8,128)(2,1)} %grad_ref.3) | copy-start | bytes 2359300
  6.5 12.3 %copy-start.8 = (f32[3,6144]{1,0:T(4,128)S(1)}, f32[3,6144]{1,0:T(4,128)}, u32[]{:S(2)}) copy-start(f32[3,6144]{1,0:T(4,128)} %frac_ref) | copy-start | bytes 221188
  13.2 1.9 %copy-start.3 = (f32[7680,128]{1,0:T(8,128)}, f32[7680,128]{1,0:T(8,128)S(1)}, u32[]{:S(2)}) copy-start(f32[7680,128]{1,0:T(8,128)S(1)} %get-tuple-element.44) | copy-start | bytes 11796484
  15.1 25.0 %collective-permute-start = (bf16[768,128]{1,0:T(8,128)(2,1)S(1)}, bf16[768,128]{1,0:T(8,128)(2,1)S(1)}, u32[]{:S(2)}, u32[]{:S(2)}) collective-permute-start(bf16[768,128]{1,0:T(8,128)(2,1)S(1)} %get-tuple-element.69), channel_id=1, source_target_pairs={{248,0},{0,8},{8,16},{16,24},{24,32},{32,40},{40,48},{48,56},{56,6... | collective-permute-start | bytes 589832 | tf_op jit(solution)/shard_map/ppermute | solution.py:34
  18.2 21.9 %collective-permute-start.1 = (bf16[768,128]{1,0:T(8,128)(2,1)S(1)}, bf16[768,128]{1,0:T(8,128)(2,1)S(1)}, u32[]{:S(2)}, u32[]{:S(2)}) collective-permute-start(bf16[768,128]{1,0:T(8,128)(2,1)S(1)} %get-tuple-element.68), channel_id=1, source_target_pairs={{8,0},{16,8},{24,16},{32,24},{40,32},{48,40},{56,48},{64,56},{72,6... | collective-permute-start | bytes 589832 | tf_op jit(solution)/shard_map/ppermute | solution.py:34
  40.1 6.8 %collective-permute-start.2 = (bf16[32,1024]{1,0:T(8,128)(2,1)S(1)}, bf16[32,1024]{1,0:T(8,128)(2,1)S(1)}, u32[]{:S(2)}, u32[]{:S(2)}) collective-permute-start(bf16[32,1024]{1,0:T(8,128)(2,1)S(1)} %dynamic-slice_convert_fusion), channel_id=1, source_target_pairs={{0,8},{8,0},{16,24},{24,16},{32,40},{40,32},{48,56},{56,48},{64,72... | collective-permute-start | bytes 196616 | tf_op jit(solution)/shard_map/ppermute | solution.py:28
  46.8 39.1 %copy-start = (f32[7680,128]{1,0:T(8,128)}, f32[7680,128]{1,0:T(8,128)S(1)}, u32[]{:S(2)}) copy-start(f32[7680,128]{1,0:T(8,128)S(1)} %pad_maximum_fusion) | copy-start | bytes 11796484
  46.9 9.0 %collective-permute-start.3 = (bf16[32,1024]{1,0:T(8,128)(2,1)S(1)}, bf16[32,1024]{1,0:T(8,128)(2,1)S(1)}, u32[]{:S(2)}, u32[]{:S(2)}) collective-permute-start(bf16[32,1024]{1,0:T(8,128)(2,1)S(1)} %add_convert_fusion.4), channel_id=1, source_target_pairs={{0,16},{8,24},{16,0},{24,8},{32,48},{40,56},{48,32},{56,40},{64,80... | collective-permute-start | bytes 196616 | tf_op jit(solution)/shard_map/ppermute | solution.py:28
  64.8 4.7 %collective-permute-start.4 = (bf16[32,1024]{1,0:T(8,128)(2,1)S(1)}, bf16[32,1024]{1,0:T(8,128)(2,1)S(1)}, u32[]{:S(2)}, u32[]{:S(2)}) collective-permute-start(bf16[32,1024]{1,0:T(8,128)(2,1)S(1)} %add_convert_fusion.3), channel_id=1, source_target_pairs={{0,32},{8,40},{16,48},{24,56},{32,0},{40,8},{48,16},{56,24},{64,96... | collective-permute-start | bytes 196616 | tf_op jit(solution)/shard_map/ppermute | solution.py:28
  69.5 31.2 %slice-start = ((s8[12582912]{0:T(1024)(128)(4,1)}), s8[4194304]{0:T(1024)(128)(4,1)S(1)}, s32[]{:S(2)}) async-start(s8[12582912]{0:T(1024)(128)(4,1)} %bitcast.15), calls=%async_computation.1 | async-start | bytes 8388608
  69.6 31.2 %slice-start.1 = ((s8[12582912]{0:T(1024)(128)(4,1)}), s8[4194304]{0:T(1024)(128)(4,1)S(1)}, s32[]{:S(2)}) async-start(s8[12582912]{0:T(1024)(128)(4,1)} %bitcast.15), calls=%async_computation.2 | async-start | bytes 8388608
  78.5 7.1 %collective-permute-start.5 = (bf16[32,1024]{1,0:T(8,128)(2,1)S(1)}, bf16[32,1024]{1,0:T(8,128)(2,1)S(1)}, u32[]{:S(2)}, u32[]{:S(2)}) collective-permute-start(bf16[32,1024]{1,0:T(8,128)(2,1)S(1)} %add_convert_fusion.2), channel_id=1, source_target_pairs={{0,64},{8,72},{16,80},{24,88},{32,96},{40,104},{48,112},{56,120},{... | collective-permute-start | bytes 196616 | tf_op jit(solution)/shard_map/ppermute | solution.py:28
  85.6 14.4 %copy-start.12 = (f32[2,64,512]{2,1,0:T(8,128)S(1)}, f32[2,64,512]{2,1,0:T(8,128)}, u32[]{:S(2)}) copy-start(f32[2,64,512]{2,1,0:T(8,128)} %param.15) | copy-start | bytes 786436
  85.6 14.4 %copy-start.13 = (f32[64,512]{1,0:T(8,128)S(1)}, f32[64,512]{1,0:T(8,128)}, u32[]{:S(2)}) copy-start(f32[64,512]{1,0:T(8,128)} %param.14) | copy-start | bytes 393220
  85.6 15.2 %slice-start.2 = ((s8[12582912]{0:T(1024)(128)(4,1)}), s8[4194304]{0:T(1024)(128)(4,1)S(1)}, s32[]{:S(2)}) async-start(s8[12582912]{0:T(1024)(128)(4,1)} %bitcast.15), calls=%async_computation.3 | async-start | bytes 8388608
  85.6 9.2 %collective-permute-start.6 = (bf16[32,1024]{1,0:T(8,128)(2,1)S(1)}, bf16[32,1024]{1,0:T(8,128)(2,1)S(1)}, u32[]{:S(2)}, u32[]{:S(2)}) collective-permute-start(bf16[32,1024]{1,0:T(8,128)(2,1)S(1)} %add_convert_fusion.1), channel_id=1, source_target_pairs={{0,128},{8,136},{16,144},{24,152},{32,160},{40,168},{48,176},{56,1... | collective-permute-start | bytes 196616 | tf_op jit(solution)/shard_map/ppermute | solution.py:28
  94.9 5.1 %collective-permute-start.7 = (f32[32,1024]{1,0:T(8,128)S(1)}, f32[32,1024]{1,0:T(8,128)S(1)}, u32[]{:S(2)}, u32[]{:S(2)}) collective-permute-start(f32[32,1024]{1,0:T(8,128)S(1)} %convert_add_fusion), channel_id=1, source_target_pairs={{0,8},{8,0},{16,24},{24,16},{32,40},{40,32},{48,56},{56,48},{64,72... | collective-permute-start | bytes 393224 | tf_op jit(solution)/shard_map/ppermute | solution.py:28
  107.2 26.3 %all-to-all-start = ((bf16[8,64,768]{2,1,0:T(8,128)(2,1)}), bf16[8,64,768]{2,1,0:T(8,128)(2,1)S(1)}, u32[]{:S(2)}, u32[]{:S(2)}) async-start(bf16[8,64,768]{2,1,0:T(8,128)(2,1)} %long_parts.1), calls=%async_computation | async-start | bytes 1572864 | tf_op jit(solution)/shard_map/all_to_all | solution.py:345
  113.6 2.1 %copy-start.1 = (f32[7680,128]{1,0:T(8,128)S(1)}, f32[7680,128]{1,0:T(8,128)}, u32[]{:S(2)}) copy-start(f32[7680,128]{1,0:T(8,128)} %copy-done) | copy-start | bytes 11796484
  115.7 8.9 %copy-start.2 = (f32[7680,128]{1,0:T(8,128)S(1)}, f32[7680,128]{1,0:T(8,128)}, u32[]{:S(2)}) copy-start(f32[7680,128]{1,0:T(8,128)} %copy-done) | copy-start | bytes 11796484

commit v3 on v2

--- a/solution.py
+++ b/solution.py
@@ -159,8 +159,9 @@
 
 def prepare_kernel(
     ka_ref, halo_ref, mix_ref, grad_ref, index_ref, weight_ref, count_ref,
-    rows_ref, send_ref, slots_ref, masked_ref, picked_ref,
+    rows_ref, send_ref, masked_ref, *refs,
 ):
+    *slots_refs, picked_ref = refs
     atoms = grad_ref.shape[1]
     block = math.gcd(atoms, 512)
     sends, per_side = send_ref.shape[0], halo_ref.shape[1]
@@ -190,9 +191,9 @@
 
     slot = lax.broadcasted_iota(jnp.int32, weight_ref.shape, 0)
     masked = jnp.where(slot < count_ref[...], weight_ref[...], 0.0)
-    for piece in range(slots_ref.shape[0]):
+    for piece, slots_ref in enumerate(slots_refs):
         cut = slice(piece * LANES, (piece + 1) * LANES)
-        slots_ref[piece] = index_ref[:, cut]
+        slots_ref[...] = index_ref[:, cut]
         masked_ref[cut, :] = masked[:, cut].T
 
 
@@ -215,15 +216,15 @@
                 pl.BlockSpec((slots, own), lambda i, ka: (0, ka[0])),
                 pl.BlockSpec((1, own), lambda i, ka: (0, ka[0])),
             ],
-            out_specs=[whole, whole, whole, whole],
+            out_specs=[whole] * (3 + own // LANES),
             scratch_shapes=[pltpu.VMEM((2 * per_side, LANES), F32)],
         ),
         out_shape=[
             jax.ShapeDtypeStruct((atoms + 2 * per_side, LANES), F32),
             jax.ShapeDtypeStruct((2 * per_side, LANES), BF16),
-            jax.ShapeDtypeStruct((own // LANES, slots, LANES), jnp.int32),
             jax.ShapeDtypeStruct((own, slots), F32),
-        ],
+        ]
+        + [jax.ShapeDtypeStruct((slots, LANES), jnp.int32)] * (own // LANES),
         compiler_params=pltpu.CompilerParams(vmem_limit_bytes=12 << 20),
         cost_estimate=pl.CostEstimate(flops=1_000_000_000, bytes_accessed=8_000_000, transcendentals=0),
         name="prepare",
@@ -237,10 +238,10 @@
         first = pl.multiple_of(g * 8, 8)
         weights = weight_ref[pl.ds(first, 8), :]
         total = jnp.zeros((8, LANES), F32)
-        for s in range(index_ref.shape[1]):
-            picked = jnp.broadcast_to(rows_ref[index_ref[0, s, first]], (8, LANES))
+        for s in range(weight_ref.shape[1]):
+            picked = jnp.broadcast_to(rows_ref[index_ref[s * LANES + first]], (8, LANES))
             for a in range(1, 8):
-                row = jnp.broadcast_to(rows_ref[index_ref[0, s, first + a]], (8, LANES))
+                row = jnp.broadcast_to(rows_ref[index_ref[s * LANES + first + a]], (8, LANES))
                 picked = jnp.where(sublane == a, row, picked)
             total = total + picked * weights[:, s : s + 1]
         sums_ref[pl.ds(first, 8), :] = total
@@ -251,12 +252,12 @@
 
 
 def short_sums(piece, channels, index, weight, rows):
-    slots = index.shape[1]
+    slots = weight.shape[1]
     return pl.pallas_call(
         short_kernel,
         grid=(1,),
         in_specs=[
-            pl.BlockSpec((1, slots, LANES), lambda i: (piece, 0, 0), memory_space=pltpu.SMEM),
+            pl.BlockSpec(memory_space=pltpu.SMEM),
             pl.BlockSpec((LANES, slots), lambda i: (piece, 0)),
             pl.BlockSpec(memory_space=pltpu.VMEM),
         ],
@@ -289,8 +290,14 @@
 
     ka = lax.axis_index("ka").astype(jnp.int32)
     mix_wide = jnp.pad(pair_mix, ((0, LANES - channels), (0, 0)))
-    rows, send, slots, masked = prepare(
-        ka[None], mix_wide, grad_out, nbr_index, pair_weight, nbr_count[None, :], halo_send
+    rows, send, masked, *slots = prepare(
+        ka[None],
+        mix_wide,
+        grad_out,
+        pltpu.with_memory_space_constraint(nbr_index, pltpu.HBM),
+        pltpu.with_memory_space_constraint(pair_weight, pltpu.HBM),
+        nbr_count[None, :],
+        halo_send,
     )
     per_side = halo_send.shape[1]
     from_left = shifted(send[:per_side], "dom", 1)
@@ -298,7 +305,8 @@
     short = []
 
     def short_piece():
-        short.append(short_sums(len(short), channels, slots, masked, extended))
+        piece = len(short)
+        short.append(short_sums(piece, channels, slots[piece].reshape(-1), masked, extended))
 
     def beside(value, bit, pieces):
         nonlocal slots
@@ -315,9 +323,9 @@
     frac_late, send_late = lax.optimization_barrier((frac_pos, send))
     q, table = front(out_weight, grad_out, frac_late, k_triple)
     q, from_left, from_right = lax.optimization_barrier((q, from_left, from_right))
-    extended = jnp.concatenate(
-        [rows[:local_atoms], from_left.astype(F32), from_right.astype(F32)], axis=0
-    )[:, None, :]
+    ghosts = jnp.concatenate([from_left, from_right], axis=0).astype(F32)
+    extended = lax.dynamic_update_slice_in_dim(rows, ghosts, local_atoms, 0)
+    extended = lax.optimization_barrier(extended)[:, None, :]
 
     half = channels // 2
     core = lax.axis_index("dom") % 2
@@ -327,7 +335,7 @@
     bit = 2
     while bit < dom_size:
         rounded = total.astype(BF16)
-        total = rounded.astype(F32) + beside(rounded, bit, 1)
+        total = rounded.astype(F32) + beside(rounded, bit, 0 if bit == 8 else 1)
         bit *= 2
     partner = beside(total, 1, 0)
     q = jnp.where(
@@ -340,6 +348,7 @@
     d_filter = (struct_fac[0] * q_cos + struct_fac[1] * q_sin) / atom_total
     p = jnp.concatenate([ewald_filter * q_cos, ewald_filter * q_sin], axis=1).astype(BF16)
 
+    table = pltpu.with_memory_space_constraint(table, pltpu.HBM)
     parts = long_parts(p, table, ka_size)
     parts, slots = lax.optimization_barrier((parts, slots))
     parts = lax.all_to_all(parts, "ka", 0, 0, tiled=True)

time: 135 us -> 114 us (0.84)
  Pallas kernels: 83.9 us -> 67.4 us
  local copies, waits for them, and re-layouts: 13.9 us -> 9.66 us
  waiting for transfers between devices: 8.01 us -> 10.6 us
  starting transfers between devices: 23.7 us -> 22.3 us
    pallas_call x6, Pallas kernels: 53.4 us -> 36.4 us  [short_sums(): pl.pallas_call(short_kernel, grid=(1,), in_specs=[pl.BlockSpec(memory_spa...]
    all_to_all x1, waiting for transfers between devices: 0.01 us -> 5.32 us  [local(): parts = lax.all_to_all(parts, 'ka', 0, 0, tiled=True)]
    slice x1 -> x0, local copies, waits for them, and re-layouts: 3.75 us -> none  [local(): rows[:local_atoms]]
    ppermute x6, waiting for transfers between devices: 8 us -> 5.26 us  [swapped(): lax.ppermute(block, axis, [(i, i ^ bit) for i in range(lax.axis_size(axis...]
    concatenate x1 -> x0, other arithmetic: 2.14 us -> none  [local(): jnp.concatenate([rows[:local_atoms], from_left.astype(F32), from_right.as...]
    ppermute x6, starting transfers between devices: 13.9 us -> 12.5 us  [swapped(): lax.ppermute(block, axis, [(i, i ^ bit) for i in range(lax.axis_size(axis...]
    unnamed x41 -> x31, local copies, waits for them, and re-layouts: 9.14 us -> 8.67 us
  transfers between devices with their start and end apart: 9 -> 9, of which waited for: 3 -> 3; matrix products, arithmetic and copies ran while one was open for 5% -> 1% of each run, Pallas kernels for 39% -> 37%
where the time goes in v3:
time: 114 us; the launch traced here: 113 us
  Pallas kernels  67.4 us (59%)
  starting transfers between devices  22.3 us (20%)
  waiting for transfers between devices  10.6 us (9%)
  local copies, waits for them, and re-layouts  9.66 us (8%)
  other arithmetic  2.64 us (2%)
    pallas_call x6, Pallas kernels, short_sums(): pl.pallas_call(short_kernel, grid=(1,), in_specs=[pl.BlockSpec(memory_spa...  36.4 us
    pallas_call x1, Pallas kernels, front(): pl.pallas_call(functools.partial(front_kernel, rows), grid=(atoms // bloc...  17.5 us
    ppermute x6, starting transfers between devices, swapped(): lax.ppermute(block, axis, [(i, i ^ bit) for i in range(lax.axis_size(axis...  12.5 us
    unnamed x31, local copies, waits for them, and re-layouts  8.67 us
    pallas_call x1, Pallas kernels, prepare(): pl.pallas_call(prepare_kernel, grid_spec=pltpu.PrefetchScalarGridSpec(num...  7.12 us
    all_to_all x1, starting transfers between devices, local(): parts = lax.all_to_all(parts, 'ka', 0, 0, tiled=True)  6.37 us
    pallas_call x1, Pallas kernels, long_parts(): pl.pallas_call(long_kernel, in_specs=[pl.BlockSpec(memory_space=pltpu.VME...  6.31 us
    all_to_all x1, waiting for transfers between devices, local(): parts = lax.all_to_all(parts, 'ka', 0, 0, tiled=True)  5.32 us
  transfers between devices with their start and end apart: 9, of which 3 were waited for; matrix products, arithmetic and copies ran while one was open for 1% of the time, Pallas kernels for 37%

profile of v3, /device:TPU:1, one launch (start us, length us, event | category | flops | bytes accessed | tf_op | source)
XLA Modules:
  0.0 113.5 jit_solution(12053855955290006784)
XLA Ops:
  0.6 0.0 copy-start.12
  0.6 0.0 copy-start.8
  0.7 0.7 pad.4.mix_ref
  1.4 0.0 copy-start
  1.4 1.1 copy-done
  2.5 0.0 copy-start.7
  2.5 0.7 copy-done.7
  3.3 0.0 copy-start.9
  3.3 0.7 copy-done.9
  4.0 0.0 copy-start.1
  4.0 0.0 copy-start.6
  4.0 7.1 %prepare.1 = (f32[7680,128]{1,0:T(8,128)S(1)}, bf16[1536,128]{1,0:T(8,128)(2,1)S(1)}, f32[768,48]{1,0:T(8,128)S(1)}, s32[48,128]{1,0:T(8,128)S(1)}, s32[48,128]{...) custom-call(s32[1]{0:T(128)} %bitcast.ka_ref, ...), custom_call_target="tpu_custom_call" | custom-call | flops 1000000000 | bytes 8000000 | tf_op jit(solution)/shard_map/prepare/pallas_call | solution.py:206
  11.1 0.0 copy-start.2
  11.1 1.8 %copy-done.2 = f32[7680,128]{1,0:T(8,128)} copy-done((f32[7680,128]{1,0:T(8,128)}, f32[7680,128]{1,0:T(8,128)S(1)}, u32[]{:S(2)}) %copy-start.2) | copy-done | bytes 3932184
  13.0 3.1 %collective-permute-start = (bf16[768,128]{1,0:T(8,128)(2,1)S(1)}, bf16[768,128]{1,0:T(8,128)(2,1)S(1)}, u32[]{:S(2)}, u32[]{:S(2)}) collective-permute-start(bf16[768,128]{1,0:T(8,128)(2,1)S(1)} %get-tuple-element.123), channel_id=1, source_target_pairs={{248,0},{0,8},{8,16},{16,24},{24,32},{32,40},{40,48},{48,56},{56,6... | collective-permute-start | bytes 589832 | tf_op jit(solution)/shard_map/ppermute | solution.py:34
  16.1 0.3 collective-permute-start.1
  16.4 0.0 copy-done.12
  16.4 0.1 pad.16.clone
  16.5 0.1 maximum_maximum_fusion
  16.5 0.1 copy.14.k_ref
  16.7 0.0 copy-done.8
  16.7 0.0 copy-done.1
  16.7 0.0 copy-done.6
  16.7 17.5 %structure_sums.1 = (f32[64,1024]{1,0:T(8,128)S(1)}, bf16[1024,6144]{1,0:T(8,128)(2,1)}) custom-call(bf16[64,64]{1,0:T(8,128)(2,1)S(1)} %copy-done.8, bf16[64,6144]{1,0:T(8,128)(2,1)S(1)} %copy-done.1, f32[3,6144]{1,0:T(4,128)S(1)} %copy-done.6, bf16[512,16]{1,0:T(8,128)(2,1)S(1)} %copy.14.k_ref), custom_call_target="tpu_custom_call" | custom-call | flops 20000000000 | bytes 14000000 | tf_op jit(solution)/shard_map/structure_sums/pallas_call | solution.py:95
  34.2 0.0 collective-permute-done
  34.2 0.0 collective-permute-done.1
  34.3 4.6 %collective-permute-start.2 = (bf16[32,1024]{1,0:T(8,128)(2,1)S(1)}, bf16[32,1024]{1,0:T(8,128)(2,1)S(1)}, u32[]{:S(2)}, u32[]{:S(2)}) collective-permute-start(bf16[32,1024]{1,0:T(8,128)(2,1)S(1)} %dynamic-slice_convert_fusion), channel_id=1, source_target_pairs={{0,8},{8,0},{16,24},{24,16},{32,40},{40,32},{48,56},{56,48},{64,72... | collective-permute-start | bytes 196616 | tf_op jit(solution)/shard_map/ppermute | solution.py:28
  38.8 0.9 convert_dynamic-update-slice_fusion
  39.8 0.0 collective-permute-done.2
  39.8 0.1 collective-permute-start.3
  39.9 0.0 copy-start.3
  39.9 2.1 %copy-done.3 = f32[7680,128]{1,0:T(8,128)S(1)} copy-done((f32[7680,128]{1,0:T(8,128)S(1)}, f32[7680,128]{1,0:T(8,128)}, u32[]{:S(2)}) %copy-start.3) | copy-done | bytes 3932184
  42.0 0.0 copy-start.4
  42.0 6.1 %short_sums.6 = f32[64,128]{1,0:T(8,128)S(1)} custom-call(s32[6144]{0:T(1024)S(1)} %bitcast.33, f32[768,48]{1,0:T(8,128)S(1)} %get-tuple-element.80.weight_ref, f32[7680,1,128]{2,1,0:T(1,128)S(1)} %bitcast.21), custom_call_target="tpu_custom_call" | custom-call | flops 4000000000 | bytes 4000000 | tf_op jit(solution)/shard_map/short_sums/pallas_call | solution.py:256
  48.1 0.0 collective-permute-done.3
  48.1 1.5 %collective-permute-start.4 = (bf16[32,1024]{1,0:T(8,128)(2,1)S(1)}, bf16[32,1024]{1,0:T(8,128)(2,1)S(1)}, u32[]{:S(2)}, u32[]{:S(2)}) collective-permute-start(bf16[32,1024]{1,0:T(8,128)(2,1)S(1)} %add_convert_fusion.3), channel_id=1, source_target_pairs={{0,32},{8,40},{16,48},{24,56},{32,0},{40,8},{48,16},{56,24},{64,96... | collective-permute-start | bytes 196616 | tf_op jit(solution)/shard_map/ppermute | solution.py:28
  49.6 0.0 copy-done.4
  49.6 6.1 %short_sums.7 = f32[64,128]{1,0:T(8,128)S(1)} custom-call(s32[6144]{0:T(1024)S(1)} %bitcast.32, f32[768,48]{1,0:T(8,128)S(1)} %get-tuple-element.80.weight_ref, f32[7680,1,128]{2,1,0:T(1,128)S(1)} %bitcast.22), custom_call_target="tpu_custom_call" | custom-call | flops 4000000000 | bytes 4000000 | tf_op jit(solution)/shard_map/short_sums/pallas_call | solution.py:256
  55.7 0.0 collective-permute-done.4
  55.7 3.0 %collective-permute-start.5 = (bf16[32,1024]{1,0:T(8,128)(2,1)S(1)}, bf16[32,1024]{1,0:T(8,128)(2,1)S(1)}, u32[]{:S(2)}, u32[]{:S(2)}) collective-permute-start(bf16[32,1024]{1,0:T(8,128)(2,1)S(1)} %add_convert_fusion.2), channel_id=1, source_target_pairs={{0,64},{8,72},{16,80},{24,88},{32,96},{40,104},{48,112},{56,120},{... | collective-permute-start | bytes 196616 | tf_op jit(solution)/shard_map/ppermute | solution.py:28
  58.7 4.2 %collective-permute-done.5 = bf16[32,1024]{1,0:T(8,128)(2,1)S(1)} collective-permute-done((bf16[32,1024]{1,0:T(8,128)(2,1)S(1)}, bf16[32,1024]{1,0:T(8,128)(2,1)S(1)}, u32[]{:S(2)}, u32[]{:S(2)}) %collective-permute-start.5) | collective-permute-done | bytes 65568 | tf_op jit(solution)/shard_map/ppermute | solution.py:28
  63.0 1.2 %collective-permute-start.6 = (bf16[32,1024]{1,0:T(8,128)(2,1)S(1)}, bf16[32,1024]{1,0:T(8,128)(2,1)S(1)}, u32[]{:S(2)}, u32[]{:S(2)}) collective-permute-start(bf16[32,1024]{1,0:T(8,128)(2,1)S(1)} %add_convert_fusion.1), channel_id=1, source_target_pairs={{0,128},{8,136},{16,144},{24,152},{32,160},{40,168},{48,176},{56,1... | collective-permute-start | bytes 196616 | tf_op jit(solution)/shard_map/ppermute | solution.py:28
  64.1 0.0 copy-start.10
  64.1 0.0 copy-start.11
  64.1 6.1 %short_sums.8 = f32[64,128]{1,0:T(8,128)S(1)} custom-call(s32[6144]{0:T(1024)S(1)} %bitcast.31, f32[768,48]{1,0:T(8,128)S(1)} %get-tuple-element.80.weight_ref, f32[7680,1,128]{2,1,0:T(1,128)S(1)} %bitcast.23), custom_call_target="tpu_custom_call" | custom-call | flops 4000000000 | bytes 4000000 | tf_op jit(solution)/shard_map/short_sums/pallas_call | solution.py:256
  70.2 0.0 collective-permute-done.6
  70.3 2.3 %collective-permute-start.7 = (f32[32,1024]{1,0:T(8,128)S(1)}, f32[32,1024]{1,0:T(8,128)S(1)}, u32[]{:S(2)}, u32[]{:S(2)}) collective-permute-start(f32[32,1024]{1,0:T(8,128)S(1)} %convert_add_fusion), channel_id=1, source_target_pairs={{0,8},{8,0},{16,24},{24,16},{32,40},{40,32},{48,56},{56,48},{64,72... | collective-permute-start | bytes 393224 | tf_op jit(solution)/shard_map/ppermute | solution.py:28
  72.5 1.0 collective-permute-done.7
  73.5 0.0 copy-done.10
  73.6 0.0 copy-done.11
  73.6 0.7 multiply_convert_fusion.1
  74.3 6.3 %long_parts.1 = bf16[8,64,768]{2,1,0:T(8,128)(2,1)} custom-call(bf16[64,1024]{1,0:T(8,128)(2,1)S(1)} %pad_maximum_fusion.p_ref, bf16[1024,6144]{1,0:T(8,128)(2,1)} %get-tuple-element.109.table_ref), custom_call_target="tpu_custom_call" | custom-call | flops 800000000 | bytes 14000000 | tf_op jit(solution)/shard_map/long_parts/pallas_call | solution.py:148
  80.6 6.1 %short_sums.10 = f32[64,128]{1,0:T(8,128)S(1)} custom-call(s32[6144]{0:T(1024)S(1)} %bitcast.30, f32[768,48]{1,0:T(8,128)S(1)} %get-tuple-element.80.weight_ref, f32[7680,1,128]{2,1,0:T(1,128)S(1)} %bitcast.24), custom_call_target="tpu_custom_call" | custom-call | flops 4000000000 | bytes 4000000 | tf_op jit(solution)/shard_map/short_sums/pallas_call | solution.py:256
  86.7 6.1 %short_sums.9 = f32[64,128]{1,0:T(8,128)S(1)} custom-call(s32[6144]{0:T(1024)S(1)} %bitcast.29, f32[768,48]{1,0:T(8,128)S(1)} %get-tuple-element.80.weight_ref, f32[7680,1,128]{2,1,0:T(1,128)S(1)} %bitcast.25), custom_call_target="tpu_custom_call" | custom-call | flops 4000000000 | bytes 4000000 | tf_op jit(solution)/shard_map/short_sums/pallas_call | solution.py:256
  92.8 6.4 %all-to-all-start = ((bf16[8,64,768]{2,1,0:T(8,128)(2,1)}), bf16[8,64,768]{2,1,0:T(8,128)(2,1)S(1)}, u32[]{:S(2)}, u32[]{:S(2)}) async-start(bf16[8,64,768]{2,1,0:T(8,128)(2,1)} %long_parts.1), calls=%async_computation | async-start | bytes 1572864 | tf_op jit(solution)/shard_map/all_to_all | solution.py:354
  99.2 0.0 copy-start.5
  99.2 2.1 %copy-done.5 = f32[7680,128]{1,0:T(8,128)S(1)} copy-done((f32[7680,128]{1,0:T(8,128)S(1)}, f32[7680,128]{1,0:T(8,128)}, u32[]{:S(2)}) %copy-start.5) | copy-done | bytes 3932184
  101.3 6.1 %short_sums.11 = f32[64,128]{1,0:T(8,128)S(1)} custom-call(s32[6144]{0:T(1024)S(1)} %bitcast.28, f32[768,48]{1,0:T(8,128)S(1)} %get-tuple-element.80.weight_ref, f32[7680,1,128]{2,1,0:T(1,128)S(1)} %bitcast.26), custom_call_target="tpu_custom_call" | custom-call | flops 4000000000 | bytes 4000000 | tf_op jit(solution)/shard_map/short_sums/pallas_call | solution.py:256
  107.4 5.3 %all-to-all-done = bf16[8,64,768]{2,1,0:T(8,128)(2,1)S(1)} async-done(((bf16[8,64,768]{2,1,0:T(8,128)(2,1)}), bf16[8,64,768]{2,1,0:T(8,128)(2,1)S(1)}, u32[]{:S(2)}, u32[]{:S(2)}) %all-to-all-start) | async-done | bytes 786464 | tf_op jit(solution)/shard_map/all_to_all | solution.py:354
  112.7 0.1 convert_reduce_fusion
  112.8 0.7 add_convert_fusion
  (17 shorter events, 0.2 us)
Async XLA Ops:
  0.6 15.7 %copy-start.12 = (s32[3,512]{1,0:T(4,128)S(1)}, s32[3,512]{1,0:T(4,128)}, u32[]{:S(2)}) copy-start(s32[3,512]{1,0:T(4,128)} %param.13) | copy-start | bytes 18436
  0.6 16.0 %copy-start.8 = (bf16[64,64]{1,0:T(8,128)(2,1)S(1)}, bf16[64,64]{1,0:T(8,128)(2,1)}, u32[]{:S(2)}) copy-start(bf16[64,64]{1,0:T(8,128)(2,1)} %mix_ref.1) | copy-start | bytes 24580
  1.4 1.1 copy-start
  2.5 0.7 copy-start.7
  3.3 0.7 copy-start.9
  4.0 12.7 %copy-start.1 = (bf16[64,6144]{1,0:T(8,128)(2,1)S(1)}, bf16[64,6144]{1,0:T(8,128)(2,1)}, u32[]{:S(2)}) copy-start(bf16[64,6144]{1,0:T(8,128)(2,1)} %grad_ref.3) | copy-start | bytes 2359300
  4.0 12.7 %copy-start.6 = (f32[3,6144]{1,0:T(4,128)S(1)}, f32[3,6144]{1,0:T(4,128)}, u32[]{:S(2)}) copy-start(f32[3,6144]{1,0:T(4,128)} %frac_ref) | copy-start | bytes 221188
  11.1 1.9 %copy-start.2 = (f32[7680,128]{1,0:T(8,128)}, f32[7680,128]{1,0:T(8,128)S(1)}, u32[]{:S(2)}) copy-start(f32[7680,128]{1,0:T(8,128)S(1)} %get-tuple-element.81) | copy-start | bytes 11796484
  13.0 21.3 %collective-permute-start = (bf16[768,128]{1,0:T(8,128)(2,1)S(1)}, bf16[768,128]{1,0:T(8,128)(2,1)S(1)}, u32[]{:S(2)}, u32[]{:S(2)}) collective-permute-start(bf16[768,128]{1,0:T(8,128)(2,1)S(1)} %get-tuple-element.123), channel_id=1, source_target_pairs={{248,0},{0,8},{8,16},{16,24},{24,32},{32,40},{40,48},{48,56},{56,6... | collective-permute-start | bytes 589832 | tf_op jit(solution)/shard_map/ppermute | solution.py:34
  16.1 18.2 %collective-permute-start.1 = (bf16[768,128]{1,0:T(8,128)(2,1)S(1)}, bf16[768,128]{1,0:T(8,128)(2,1)S(1)}, u32[]{:S(2)}, u32[]{:S(2)}) collective-permute-start(bf16[768,128]{1,0:T(8,128)(2,1)S(1)} %get-tuple-element.122), channel_id=1, source_target_pairs={{8,0},{16,8},{24,16},{32,24},{40,32},{48,40},{56,48},{64,56},{72,6... | collective-permute-start | bytes 589832 | tf_op jit(solution)/shard_map/ppermute | solution.py:34
  34.3 5.5 %collective-permute-start.2 = (bf16[32,1024]{1,0:T(8,128)(2,1)S(1)}, bf16[32,1024]{1,0:T(8,128)(2,1)S(1)}, u32[]{:S(2)}, u32[]{:S(2)}) collective-permute-start(bf16[32,1024]{1,0:T(8,128)(2,1)S(1)} %dynamic-slice_convert_fusion), channel_id=1, source_target_pairs={{0,8},{8,0},{16,24},{24,16},{32,40},{40,32},{48,56},{56,48},{64,72... | collective-permute-start | bytes 196616 | tf_op jit(solution)/shard_map/ppermute | solution.py:28
  39.8 8.3 %collective-permute-start.3 = (bf16[32,1024]{1,0:T(8,128)(2,1)S(1)}, bf16[32,1024]{1,0:T(8,128)(2,1)S(1)}, u32[]{:S(2)}, u32[]{:S(2)}) collective-permute-start(bf16[32,1024]{1,0:T(8,128)(2,1)S(1)} %add_convert_fusion.4), channel_id=1, source_target_pairs={{0,16},{8,24},{16,0},{24,8},{32,48},{40,56},{48,32},{56,40},{64,80... | collective-permute-start | bytes 196616 | tf_op jit(solution)/shard_map/ppermute | solution.py:28
  39.9 2.1 %copy-start.3 = (f32[7680,128]{1,0:T(8,128)S(1)}, f32[7680,128]{1,0:T(8,128)}, u32[]{:S(2)}) copy-start(f32[7680,128]{1,0:T(8,128)} %convert_dynamic-update-slice_fusion) | copy-start | bytes 11796484
  42.0 7.6 %copy-start.4 = (f32[7680,128]{1,0:T(8,128)S(1)}, f32[7680,128]{1,0:T(8,128)}, u32[]{:S(2)}) copy-start(f32[7680,128]{1,0:T(8,128)} %convert_dynamic-update-slice_fusion) | copy-start | bytes 11796484
  48.1 7.5 %collective-permute-start.4 = (bf16[32,1024]{1,0:T(8,128)(2,1)S(1)}, bf16[32,1024]{1,0:T(8,128)(2,1)S(1)}, u32[]{:S(2)}, u32[]{:S(2)}) collective-permute-start(bf16[32,1024]{1,0:T(8,128)(2,1)S(1)} %add_convert_fusion.3), channel_id=1, source_target_pairs={{0,32},{8,40},{16,48},{24,56},{32,0},{40,8},{48,16},{56,24},{64,96... | collective-permute-start | bytes 196616 | tf_op jit(solution)/shard_map/ppermute | solution.py:28
  55.7 7.2 %collective-permute-start.5 = (bf16[32,1024]{1,0:T(8,128)(2,1)S(1)}, bf16[32,1024]{1,0:T(8,128)(2,1)S(1)}, u32[]{:S(2)}, u32[]{:S(2)}) collective-permute-start(bf16[32,1024]{1,0:T(8,128)(2,1)S(1)} %add_convert_fusion.2), channel_id=1, source_target_pairs={{0,64},{8,72},{16,80},{24,88},{32,96},{40,104},{48,112},{56,120},{... | collective-permute-start | bytes 196616 | tf_op jit(solution)/shard_map/ppermute | solution.py:28
  63.0 7.3 %collective-permute-start.6 = (bf16[32,1024]{1,0:T(8,128)(2,1)S(1)}, bf16[32,1024]{1,0:T(8,128)(2,1)S(1)}, u32[]{:S(2)}, u32[]{:S(2)}) collective-permute-start(bf16[32,1024]{1,0:T(8,128)(2,1)S(1)} %add_convert_fusion.1), channel_id=1, source_target_pairs={{0,128},{8,136},{16,144},{24,152},{32,160},{40,168},{48,176},{56,1... | collective-permute-start | bytes 196616 | tf_op jit(solution)/shard_map/ppermute | solution.py:28
  64.1 9.4 %copy-start.10 = (f32[2,64,512]{2,1,0:T(8,128)S(1)}, f32[2,64,512]{2,1,0:T(8,128)}, u32[]{:S(2)}) copy-start(f32[2,64,512]{2,1,0:T(8,128)} %param.15) | copy-start | bytes 786436
  64.1 9.4 %copy-start.11 = (f32[64,512]{1,0:T(8,128)S(1)}, f32[64,512]{1,0:T(8,128)}, u32[]{:S(2)}) copy-start(f32[64,512]{1,0:T(8,128)} %param.14) | copy-start | bytes 393220
  70.3 3.3 %collective-permute-start.7 = (f32[32,1024]{1,0:T(8,128)S(1)}, f32[32,1024]{1,0:T(8,128)S(1)}, u32[]{:S(2)}, u32[]{:S(2)}) collective-permute-start(f32[32,1024]{1,0:T(8,128)S(1)} %convert_add_fusion), channel_id=1, source_target_pairs={{0,8},{8,0},{16,24},{24,16},{32,40},{40,32},{48,56},{56,48},{64,72... | collective-permute-start | bytes 393224 | tf_op jit(solution)/shard_map/ppermute | solution.py:28
  92.8 19.9 %all-to-all-start = ((bf16[8,64,768]{2,1,0:T(8,128)(2,1)}), bf16[8,64,768]{2,1,0:T(8,128)(2,1)S(1)}, u32[]{:S(2)}, u32[]{:S(2)}) async-start(bf16[8,64,768]{2,1,0:T(8,128)(2,1)} %long_parts.1), calls=%async_computation | async-start | bytes 1572864 | tf_op jit(solution)/shard_map/all_to_all | solution.py:354
  99.2 2.1 %copy-start.5 = (f32[7680,128]{1,0:T(8,128)S(1)}, f32[7680,128]{1,0:T(8,128)}, u32[]{:S(2)}) copy-start(f32[7680,128]{1,0:T(8,128)} %convert_dynamic-update-slice_fusion) | copy-start | bytes 11796484

commit v4 on v3

--- a/solution.py
+++ b/solution.py
@@ -161,7 +161,7 @@
     ka_ref, halo_ref, mix_ref, grad_ref, index_ref, weight_ref, count_ref,
     rows_ref, send_ref, masked_ref, *refs,
 ):
-    *slots_refs, picked_ref = refs
+    *slots_refs, picked_ref, held_ref, sem = refs
     atoms = grad_ref.shape[1]
     block = math.gcd(atoms, 512)
     sends, per_side = send_ref.shape[0], halo_ref.shape[1]
@@ -172,16 +172,18 @@
             grad_ref[:, pl.ds(first, block)], mix_ref[...], (((0,), (1,)), ((), ())),
             preferred_element_type=F32,
         )
-        rows_ref[pl.ds(first, block), :] = mixed.astype(BF16).astype(F32)
+        held_ref[pl.ds(first, block), :] = mixed.astype(BF16).astype(F32)
         return carry
 
     lax.fori_loop(0, atoms // block, mix, 0)
+    leave = pltpu.make_async_copy(held_ref, rows_ref.at[pl.ds(0, atoms)], sem)
+    leave.start()
 
     for side in range(2):
         def pick(i, carry, side=side):
             first = pl.multiple_of(i * 32, 32)
             for j in range(32):
-                picked_ref[pl.ds(side * per_side + first + j, 1), :] = rows_ref[
+                picked_ref[pl.ds(side * per_side + first + j, 1), :] = held_ref[
                     pl.ds(halo_ref[side, first + j], 1), :
                 ]
             return carry
@@ -195,6 +197,7 @@
         cut = slice(piece * LANES, (piece + 1) * LANES)
         slots_ref[...] = index_ref[:, cut]
         masked_ref[cut, :] = masked[:, cut].T
+    leave.wait()
 
 
 def prepare(ka, mix_wide, grad, index, weight, count, halo):
@@ -216,11 +219,15 @@
                 pl.BlockSpec((slots, own), lambda i, ka: (0, ka[0])),
                 pl.BlockSpec((1, own), lambda i, ka: (0, ka[0])),
             ],
-            out_specs=[whole] * (3 + own // LANES),
-            scratch_shapes=[pltpu.VMEM((2 * per_side, LANES), F32)],
+            out_specs=[pl.BlockSpec(memory_space=pltpu.HBM)] + [whole] * (2 + own // LANES),
+            scratch_shapes=[
+                pltpu.VMEM((2 * per_side, LANES), F32),
+                pltpu.VMEM((atoms, LANES), F32),
+                pltpu.SemaphoreType.DMA(()),
+            ],
         ),
         out_shape=[
-            jax.ShapeDtypeStruct((atoms + 2 * per_side, LANES), F32),
+            pltpu.HBM((atoms + 2 * per_side, LANES), F32),
             jax.ShapeDtypeStruct((2 * per_side, LANES), BF16),
             jax.ShapeDtypeStruct((own, slots), F32),
         ]
@@ -265,7 +272,7 @@
         out_shape=jax.ShapeDtypeStruct((channels, LANES), F32),
         scratch_shapes=[pltpu.VMEM((LANES, LANES), F32)],
         compiler_params=pltpu.CompilerParams(vmem_limit_bytes=6 << 20),
-        cost_estimate=pl.CostEstimate(flops=4_000_000_000, bytes_accessed=4_000_000, transcendentals=0),
+        cost_estimate=pl.CostEstimate(flops=100_000_000, bytes_accessed=400_000, transcendentals=0),
         name="short_sums",
     )(index, weight, rows)
 

time: 114 us -> 108 us (0.947)
  waiting for transfers between devices: 10.6 us -> 6.19 us
  local copies, waits for them, and re-layouts: 9.66 us -> 7.83 us
    all_to_all x1, waiting for transfers between devices: 5.32 us -> 0.01 us  [local(): parts = lax.all_to_all(parts, 'ka', 0, 0, tiled=True)]
    unnamed x31 -> x29, local copies, waits for them, and re-layouts: 8.67 us -> 6.84 us
  transfers between devices with their start and end apart: 9 -> 9, of which waited for: 3 -> 3; matrix products, arithmetic and copies ran while one was open for 1% -> 1% of each run, Pallas kernels for 37% -> 50%
where the time goes in v4:
time: 108 us; the launch traced here: 107 us
  Pallas kernels  67.4 us (62%)
  starting transfers between devices  22.3 us (21%)
  local copies, waits for them, and re-layouts  7.83 us (7%)
  waiting for transfers between devices  6.19 us (6%)
  other arithmetic  2.63 us (2%)
    pallas_call x6, Pallas kernels, short_sums(): pl.pallas_call(short_kernel, grid=(1,), in_specs=[pl.BlockSpec(memory_spa...  36.4 us
    pallas_call x1, Pallas kernels, front(): pl.pallas_call(functools.partial(front_kernel, rows), grid=(atoms // bloc...  17.5 us
    ppermute x6, starting transfers between devices, swapped(): lax.ppermute(block, axis, [(i, i ^ bit) for i in range(lax.axis_size(axis...  12.5 us
    pallas_call x1, Pallas kernels, prepare(): pl.pallas_call(prepare_kernel, grid_spec=pltpu.PrefetchScalarGridSpec(num...  7.14 us
    unnamed x29, local copies, waits for them, and re-layouts  6.84 us
    all_to_all x1, starting transfers between devices, local(): parts = lax.all_to_all(parts, 'ka', 0, 0, tiled=True)  6.38 us
    pallas_call x1, Pallas kernels, long_parts(): pl.pallas_call(long_kernel, in_specs=[pl.BlockSpec(memory_space=pltpu.VME...  6.32 us
    ppermute x6, waiting for transfers between devices, swapped(): lax.ppermute(block, axis, [(i, i ^ bit) for i in range(lax.axis_size(axis...  6.18 us
  transfers between devices with their start and end apart: 9, of which 3 were waited for; matrix products, arithmetic and copies ran while one was open for 1% of the time, Pallas kernels for 50%

profile of v4, /device:TPU:1, one launch (start us, length us, event | category | flops | bytes accessed | tf_op | source)
XLA Modules:
  0.0 107.3 jit_solution(5340401052820386247)
XLA Ops:
  0.6 0.0 copy-start.11
  0.6 0.0 copy-start.7
  0.7 0.7 pad.4.mix_ref
  1.4 0.0 copy-start.3
  1.4 1.1 %copy-done.3 = bf16[64,6144]{1,0:T(8,128)(2,1)S(1)} copy-done((bf16[64,6144]{1,0:T(8,128)(2,1)S(1)}, bf16[64,6144]{1,0:T(8,128)(2,1)}, u32[]{:S(2)}) %copy-start.3) | copy-done | bytes 786456
  2.5 0.0 copy-start.6
  2.5 0.7 copy-done.6
  3.3 0.0 copy-start.8
  3.3 0.7 copy-done.8
  4.0 0.0 copy-start.4
  4.0 0.0 copy-start.5
  4.0 7.1 %prepare.1 = (f32[7680,128]{1,0:T(8,128)}, bf16[1536,128]{1,0:T(8,128)(2,1)S(1)}, f32[768,48]{1,0:T(8,128)S(1)}, s32[48,128]{1,0:T(8,128)S(1)}, s32[48,128]{1,0:...) custom-call(s32[1]{0:T(128)} %bitcast.ka_ref, ...), custom_call_target="tpu_custom_call" | custom-call | flops 1000000000 | bytes 8000000 | tf_op jit(solution)/shard_map/prepare/pallas_call | solution.py:209
  11.1 3.1 %collective-permute-start = (bf16[768,128]{1,0:T(8,128)(2,1)S(1)}, bf16[768,128]{1,0:T(8,128)(2,1)S(1)}, u32[]{:S(2)}, u32[]{:S(2)}) collective-permute-start(bf16[768,128]{1,0:T(8,128)(2,1)S(1)} %get-tuple-element.123), channel_id=1, source_target_pairs={{248,0},{0,8},{8,16},{16,24},{24,32},{32,40},{40,48},{48,56},{56,6... | collective-permute-start | bytes 589832 | tf_op jit(solution)/shard_map/ppermute | solution.py:34
  14.2 0.3 collective-permute-start.1
  14.5 0.0 copy-done.11
  14.6 0.1 pad.16.clone
  14.6 0.1 maximum_maximum_fusion
  14.7 0.1 copy.14.k_ref
  14.8 0.0 copy-done.7
  14.8 0.0 copy-done.4
  14.9 0.0 copy-done.5
  14.9 17.5 %structure_sums.1 = (f32[64,1024]{1,0:T(8,128)S(1)}, bf16[1024,6144]{1,0:T(8,128)(2,1)}) custom-call(bf16[64,64]{1,0:T(8,128)(2,1)S(1)} %copy-done.7, bf16[64,6144]{1,0:T(8,128)(2,1)S(1)} %copy-done.4, f32[3,6144]{1,0:T(4,128)S(1)} %copy-done.5, bf16[512,16]{1,0:T(8,128)(2,1)S(1)} %copy.14.k_ref), custom_call_target="tpu_custom_call" | custom-call | flops 20000000000 | bytes 14000000 | tf_op jit(solution)/shard_map/structure_sums/pallas_call | solution.py:95
  32.4 0.0 collective-permute-done
  32.4 0.0 collective-permute-done.1
  32.4 4.6 %collective-permute-start.2 = (bf16[32,1024]{1,0:T(8,128)(2,1)S(1)}, bf16[32,1024]{1,0:T(8,128)(2,1)S(1)}, u32[]{:S(2)}, u32[]{:S(2)}) collective-permute-start(bf16[32,1024]{1,0:T(8,128)(2,1)S(1)} %dynamic-slice_convert_fusion), channel_id=1, source_target_pairs={{0,8},{8,0},{16,24},{24,16},{32,40},{40,32},{48,56},{56,48},{64,72... | collective-permute-start | bytes 196616 | tf_op jit(solution)/shard_map/ppermute | solution.py:28
  37.0 0.9 collective-permute-done.2
  37.9 0.1 collective-permute-start.3
  38.0 0.9 convert_dynamic-update-slice_fusion
  38.9 0.0 copy-start
  38.9 2.1 %copy-done = f32[7680,128]{1,0:T(8,128)S(1)} copy-done((f32[7680,128]{1,0:T(8,128)S(1)}, f32[7680,128]{1,0:T(8,128)}, u32[]{:S(2)}) %copy-start) | copy-done | bytes 3932184
  41.1 0.0 copy-start.1
  41.1 6.1 %short_sums.6 = f32[64,128]{1,0:T(8,128)S(1)} custom-call(s32[6144]{0:T(1024)S(1)} %bitcast.32, f32[768,48]{1,0:T(8,128)S(1)} %get-tuple-element.80.weight_ref, f32[7680,1,128]{2,1,0:T(1,128)S(1)} %bitcast.21), custom_call_target="tpu_custom_call" | custom-call | flops 100000000 | bytes 400000 | tf_op jit(solution)/shard_map/short_sums/pallas_call | solution.py:263
  47.1 0.0 collective-permute-done.3
  47.2 1.5 %collective-permute-start.4 = (bf16[32,1024]{1,0:T(8,128)(2,1)S(1)}, bf16[32,1024]{1,0:T(8,128)(2,1)S(1)}, u32[]{:S(2)}, u32[]{:S(2)}) collective-permute-start(bf16[32,1024]{1,0:T(8,128)(2,1)S(1)} %add_convert_fusion.3), channel_id=1, source_target_pairs={{0,32},{8,40},{16,48},{24,56},{32,0},{40,8},{48,16},{56,24},{64,96... | collective-permute-start | bytes 196616 | tf_op jit(solution)/shard_map/ppermute | solution.py:28
  48.7 0.0 copy-done.1
  48.7 0.0 copy-start.9
  48.7 0.0 copy-start.10
  48.7 6.1 %short_sums.7 = f32[64,128]{1,0:T(8,128)S(1)} custom-call(s32[6144]{0:T(1024)S(1)} %bitcast.31, f32[768,48]{1,0:T(8,128)S(1)} %get-tuple-element.80.weight_ref, f32[7680,1,128]{2,1,0:T(1,128)S(1)} %bitcast.22), custom_call_target="tpu_custom_call" | custom-call | flops 100000000 | bytes 400000 | tf_op jit(solution)/shard_map/short_sums/pallas_call | solution.py:263
  54.7 0.0 collective-permute-done.4
  54.8 3.0 %collective-permute-start.5 = (bf16[32,1024]{1,0:T(8,128)(2,1)S(1)}, bf16[32,1024]{1,0:T(8,128)(2,1)S(1)}, u32[]{:S(2)}, u32[]{:S(2)}) collective-permute-start(bf16[32,1024]{1,0:T(8,128)(2,1)S(1)} %add_convert_fusion.2), channel_id=1, source_target_pairs={{0,64},{8,72},{16,80},{24,88},{32,96},{40,104},{48,112},{56,120},{... | collective-permute-start | bytes 196616 | tf_op jit(solution)/shard_map/ppermute | solution.py:28
  57.7 4.2 %collective-permute-done.5 = bf16[32,1024]{1,0:T(8,128)(2,1)S(1)} collective-permute-done((bf16[32,1024]{1,0:T(8,128)(2,1)S(1)}, bf16[32,1024]{1,0:T(8,128)(2,1)S(1)}, u32[]{:S(2)}, u32[]{:S(2)}) %collective-permute-start.5) | collective-permute-done | bytes 65568 | tf_op jit(solution)/shard_map/ppermute | solution.py:28
  62.0 1.2 %collective-permute-start.6 = (bf16[32,1024]{1,0:T(8,128)(2,1)S(1)}, bf16[32,1024]{1,0:T(8,128)(2,1)S(1)}, u32[]{:S(2)}, u32[]{:S(2)}) collective-permute-start(bf16[32,1024]{1,0:T(8,128)(2,1)S(1)} %add_convert_fusion.1), channel_id=1, source_target_pairs={{0,128},{8,136},{16,144},{24,152},{32,160},{40,168},{48,176},{56,1... | collective-permute-start | bytes 196616 | tf_op jit(solution)/shard_map/ppermute | solution.py:28
  63.2 6.1 %short_sums.8 = f32[64,128]{1,0:T(8,128)S(1)} custom-call(s32[6144]{0:T(1024)S(1)} %bitcast.30, f32[768,48]{1,0:T(8,128)S(1)} %get-tuple-element.80.weight_ref, f32[7680,1,128]{2,1,0:T(1,128)S(1)} %bitcast.23), custom_call_target="tpu_custom_call" | custom-call | flops 100000000 | bytes 400000 | tf_op jit(solution)/shard_map/short_sums/pallas_call | solution.py:263
  69.3 0.0 collective-permute-done.6
  69.3 2.2 %collective-permute-start.7 = (f32[32,1024]{1,0:T(8,128)S(1)}, f32[32,1024]{1,0:T(8,128)S(1)}, u32[]{:S(2)}, u32[]{:S(2)}) collective-permute-start(f32[32,1024]{1,0:T(8,128)S(1)} %convert_add_fusion), channel_id=1, source_target_pairs={{0,8},{8,0},{16,24},{24,16},{32,40},{40,32},{48,56},{56,48},{64,72... | collective-permute-start | bytes 393224 | tf_op jit(solution)/shard_map/ppermute | solution.py:28
  71.6 1.0 collective-permute-done.7
  72.6 0.0 copy-done.9
  72.6 0.0 copy-done.10
  72.6 0.7 multiply_convert_fusion.1
  73.3 6.3 %long_parts.1 = bf16[8,64,768]{2,1,0:T(8,128)(2,1)} custom-call(bf16[64,1024]{1,0:T(8,128)(2,1)S(1)} %pad_maximum_fusion.p_ref, bf16[1024,6144]{1,0:T(8,128)(2,1)} %get-tuple-element.109.table_ref), custom_call_target="tpu_custom_call" | custom-call | flops 800000000 | bytes 14000000 | tf_op jit(solution)/shard_map/long_parts/pallas_call | solution.py:148
  79.6 6.4 %all-to-all-start = ((bf16[8,64,768]{2,1,0:T(8,128)(2,1)}), bf16[8,64,768]{2,1,0:T(8,128)(2,1)S(1)}, u32[]{:S(2)}, u32[]{:S(2)}) async-start(bf16[8,64,768]{2,1,0:T(8,128)(2,1)} %long_parts.1), calls=%async_computation | async-start | bytes 1572864 | tf_op jit(solution)/shard_map/all_to_all | solution.py:361
  86.1 0.0 copy-start.2
  86.1 2.1 %copy-done.2 = f32[7680,128]{1,0:T(8,128)S(1)} copy-done((f32[7680,128]{1,0:T(8,128)S(1)}, f32[7680,128]{1,0:T(8,128)}, u32[]{:S(2)}) %copy-start.2) | copy-done | bytes 3932184
  88.2 6.1 %short_sums.11 = f32[64,128]{1,0:T(8,128)S(1)} custom-call(s32[6144]{0:T(1024)S(1)} %bitcast.29, f32[768,48]{1,0:T(8,128)S(1)} %get-tuple-element.80.weight_ref, f32[7680,1,128]{2,1,0:T(1,128)S(1)} %bitcast.24), custom_call_target="tpu_custom_call" | custom-call | flops 100000000 | bytes 400000 | tf_op jit(solution)/shard_map/short_sums/pallas_call | solution.py:263
  94.2 6.1 %short_sums.10 = f32[64,128]{1,0:T(8,128)S(1)} custom-call(s32[6144]{0:T(1024)S(1)} %bitcast.28, f32[768,48]{1,0:T(8,128)S(1)} %get-tuple-element.80.weight_ref, f32[7680,1,128]{2,1,0:T(1,128)S(1)} %bitcast.25), custom_call_target="tpu_custom_call" | custom-call | flops 100000000 | bytes 400000 | tf_op jit(solution)/shard_map/short_sums/pallas_call | solution.py:263
  100.3 6.1 %short_sums.9 = f32[64,128]{1,0:T(8,128)S(1)} custom-call(s32[6144]{0:T(1024)S(1)} %bitcast.27, f32[768,48]{1,0:T(8,128)S(1)} %get-tuple-element.80.weight_ref, f32[7680,1,128]{2,1,0:T(1,128)S(1)} %bitcast.26), custom_call_target="tpu_custom_call" | custom-call | flops 100000000 | bytes 400000 | tf_op jit(solution)/shard_map/short_sums/pallas_call | solution.py:263
  106.5 0.0 all-to-all-done
  106.5 0.1 convert_reduce_fusion
  106.6 0.7 add_convert_fusion
  (17 shorter events, 0.2 us)
Async XLA Ops:
  0.6 13.9 %copy-start.11 = (s32[3,512]{1,0:T(4,128)S(1)}, s32[3,512]{1,0:T(4,128)}, u32[]{:S(2)}) copy-start(s32[3,512]{1,0:T(4,128)} %param.13) | copy-start | bytes 18436
  0.6 14.2 %copy-start.7 = (bf16[64,64]{1,0:T(8,128)(2,1)S(1)}, bf16[64,64]{1,0:T(8,128)(2,1)}, u32[]{:S(2)}) copy-start(bf16[64,64]{1,0:T(8,128)(2,1)} %mix_ref.1) | copy-start | bytes 24580
  1.4 1.1 %copy-start.3 = (bf16[64,6144]{1,0:T(8,128)(2,1)S(1)}, bf16[64,6144]{1,0:T(8,128)(2,1)}, u32[]{:S(2)}) copy-start(bf16[64,6144]{1,0:T(8,128)(2,1)} %grad_ref.3) | copy-start | bytes 2359300
  2.5 0.7 copy-start.6
  3.3 0.7 copy-start.8
  4.0 10.9 %copy-start.4 = (bf16[64,6144]{1,0:T(8,128)(2,1)S(1)}, bf16[64,6144]{1,0:T(8,128)(2,1)}, u32[]{:S(2)}) copy-start(bf16[64,6144]{1,0:T(8,128)(2,1)} %grad_ref.3) | copy-start | bytes 2359300
  4.0 10.9 %copy-start.5 = (f32[3,6144]{1,0:T(4,128)S(1)}, f32[3,6144]{1,0:T(4,128)}, u32[]{:S(2)}) copy-start(f32[3,6144]{1,0:T(4,128)} %frac_ref) | copy-start | bytes 221188
  11.1 21.2 %collective-permute-start = (bf16[768,128]{1,0:T(8,128)(2,1)S(1)}, bf16[768,128]{1,0:T(8,128)(2,1)S(1)}, u32[]{:S(2)}, u32[]{:S(2)}) collective-permute-start(bf16[768,128]{1,0:T(8,128)(2,1)S(1)} %get-tuple-element.123), channel_id=1, source_target_pairs={{248,0},{0,8},{8,16},{16,24},{24,32},{32,40},{40,48},{48,56},{56,6... | collective-permute-start | bytes 589832 | tf_op jit(solution)/shard_map/ppermute | solution.py:34
  14.2 18.1 %collective-permute-start.1 = (bf16[768,128]{1,0:T(8,128)(2,1)S(1)}, bf16[768,128]{1,0:T(8,128)(2,1)S(1)}, u32[]{:S(2)}, u32[]{:S(2)}) collective-permute-start(bf16[768,128]{1,0:T(8,128)(2,1)S(1)} %get-tuple-element.122), channel_id=1, source_target_pairs={{8,0},{16,8},{24,16},{32,24},{40,32},{48,40},{56,48},{64,56},{72,6... | collective-permute-start | bytes 589832 | tf_op jit(solution)/shard_map/ppermute | solution.py:34
  32.4 5.5 %collective-permute-start.2 = (bf16[32,1024]{1,0:T(8,128)(2,1)S(1)}, bf16[32,1024]{1,0:T(8,128)(2,1)S(1)}, u32[]{:S(2)}, u32[]{:S(2)}) collective-permute-start(bf16[32,1024]{1,0:T(8,128)(2,1)S(1)} %dynamic-slice_convert_fusion), channel_id=1, source_target_pairs={{0,8},{8,0},{16,24},{24,16},{32,40},{40,32},{48,56},{56,48},{64,72... | collective-permute-start | bytes 196616 | tf_op jit(solution)/shard_map/ppermute | solution.py:28
  37.9 9.2 %collective-permute-start.3 = (bf16[32,1024]{1,0:T(8,128)(2,1)S(1)}, bf16[32,1024]{1,0:T(8,128)(2,1)S(1)}, u32[]{:S(2)}, u32[]{:S(2)}) collective-permute-start(bf16[32,1024]{1,0:T(8,128)(2,1)S(1)} %add_convert_fusion.4), channel_id=1, source_target_pairs={{0,16},{8,24},{16,0},{24,8},{32,48},{40,56},{48,32},{56,40},{64,80... | collective-permute-start | bytes 196616 | tf_op jit(solution)/shard_map/ppermute | solution.py:28
  38.9 2.1 %copy-start = (f32[7680,128]{1,0:T(8,128)S(1)}, f32[7680,128]{1,0:T(8,128)}, u32[]{:S(2)}) copy-start(f32[7680,128]{1,0:T(8,128)} %convert_dynamic-update-slice_fusion) | copy-start | bytes 11796484
  41.1 7.6 %copy-start.1 = (f32[7680,128]{1,0:T(8,128)S(1)}, f32[7680,128]{1,0:T(8,128)}, u32[]{:S(2)}) copy-start(f32[7680,128]{1,0:T(8,128)} %convert_dynamic-update-slice_fusion) | copy-start | bytes 11796484
  47.2 7.6 %collective-permute-start.4 = (bf16[32,1024]{1,0:T(8,128)(2,1)S(1)}, bf16[32,1024]{1,0:T(8,128)(2,1)S(1)}, u32[]{:S(2)}, u32[]{:S(2)}) collective-permute-start(bf16[32,1024]{1,0:T(8,128)(2,1)S(1)} %add_convert_fusion.3), channel_id=1, source_target_pairs={{0,32},{8,40},{16,48},{24,56},{32,0},{40,8},{48,16},{56,24},{64,96... | collective-permute-start | bytes 196616 | tf_op jit(solution)/shard_map/ppermute | solution.py:28
  48.7 23.9 %copy-start.9 = (f32[2,64,512]{2,1,0:T(8,128)S(1)}, f32[2,64,512]{2,1,0:T(8,128)}, u32[]{:S(2)}) copy-start(f32[2,64,512]{2,1,0:T(8,128)} %param.15) | copy-start | bytes 786436
  48.7 23.9 %copy-start.10 = (f32[64,512]{1,0:T(8,128)S(1)}, f32[64,512]{1,0:T(8,128)}, u32[]{:S(2)}) copy-start(f32[64,512]{1,0:T(8,128)} %param.14) | copy-start | bytes 393220
  54.8 7.2 %collective-permute-start.5 = (bf16[32,1024]{1,0:T(8,128)(2,1)S(1)}, bf16[32,1024]{1,0:T(8,128)(2,1)S(1)}, u32[]{:S(2)}, u32[]{:S(2)}) collective-permute-start(bf16[32,1024]{1,0:T(8,128)(2,1)S(1)} %add_convert_fusion.2), channel_id=1, source_target_pairs={{0,64},{8,72},{16,80},{24,88},{32,96},{40,104},{48,112},{56,120},{... | collective-permute-start | bytes 196616 | tf_op jit(solution)/shard_map/ppermute | solution.py:28
  62.0 7.3 %collective-permute-start.6 = (bf16[32,1024]{1,0:T(8,128)(2,1)S(1)}, bf16[32,1024]{1,0:T(8,128)(2,1)S(1)}, u32[]{:S(2)}, u32[]{:S(2)}) collective-permute-start(bf16[32,1024]{1,0:T(8,128)(2,1)S(1)} %add_convert_fusion.1), channel_id=1, source_target_pairs={{0,128},{8,136},{16,144},{24,152},{32,160},{40,168},{48,176},{56,1... | collective-permute-start | bytes 196616 | tf_op jit(solution)/shard_map/ppermute | solution.py:28
  69.3 3.2 %collective-permute-start.7 = (f32[32,1024]{1,0:T(8,128)S(1)}, f32[32,1024]{1,0:T(8,128)S(1)}, u32[]{:S(2)}, u32[]{:S(2)}) collective-permute-start(f32[32,1024]{1,0:T(8,128)S(1)} %convert_add_fusion), channel_id=1, source_target_pairs={{0,8},{8,0},{16,24},{24,16},{32,40},{40,32},{48,56},{56,48},{64,72... | collective-permute-start | bytes 393224 | tf_op jit(solution)/shard_map/ppermute | solution.py:28
  79.6 26.8 %all-to-all-start = ((bf16[8,64,768]{2,1,0:T(8,128)(2,1)}), bf16[8,64,768]{2,1,0:T(8,128)(2,1)S(1)}, u32[]{:S(2)}, u32[]{:S(2)}) async-start(bf16[8,64,768]{2,1,0:T(8,128)(2,1)} %long_parts.1), calls=%async_computation | async-start | bytes 1572864 | tf_op jit(solution)/shard_map/all_to_all | solution.py:361
  86.1 2.1 %copy-start.2 = (f32[7680,128]{1,0:T(8,128)S(1)}, f32[7680,128]{1,0:T(8,128)}, u32[]{:S(2)}) copy-start(f32[7680,128]{1,0:T(8,128)} %convert_dynamic-update-slice_fusion) | copy-start | bytes 11796484

commit v5 on v4

--- a/solution.py
+++ b/solution.py
@@ -35,12 +35,15 @@
 
 
 def front_kernel(
-    rows, mix_ref, grad_ref, frac_ref, k_ref, q_ref, whole_ref, pieces_ref, turns_ref, held_ref, sems
+    rows, tile, mix_ref, grad_ref, frac_ref, k_ref,
+    q_ref, whole_ref, pieces_ref, even_ref, odd_ref, held_ref, sems,
 ):
     step, last = pl.program_id(0), pl.num_programs(0) - 1
     slot = lax.rem(step, 2)
     table_ref = held_ref.at[slot]
     block = grad_ref.shape[1]
+    k_count = k_ref.shape[0]
+    turns_refs = (even_ref, odd_ref)
 
     def keep(at, slot):
         columns = pl.ds(pl.multiple_of(at * block, block), block)
@@ -62,25 +65,45 @@
     pieces_ref[0:3, :] = high
     pieces_ref[3:6, :] = middle
     pieces_ref[6:9, :] = rest - middle
-    turns_ref[...] = jnp.dot(k_ref[...], pieces_ref[...].astype(BF16), preferred_element_type=F32)
+    pieces = pieces_ref[...].astype(BF16)
     cot = jnp.dot(mix_ref[...], grad_ref[...], preferred_element_type=F32).astype(BF16)
-    k_count = k_ref.shape[0]
-
-    def fill(i, carry):
-        first = pl.multiple_of(i * rows, rows)
-        turns = turns_ref[pl.ds(first, rows), :]
-        r = turns - jnp.round(turns)
-        u = r * r
-        s = r * (SIN_HALF[0] + u * (SIN_HALF[1] + u * (SIN_HALF[2] + u * SIN_HALF[3])))
-        c = COS_HALF[0] + u * (COS_HALF[1] + u * (COS_HALF[2] + u * COS_HALF[3]))
-        table_ref[pl.ds(first, rows), :] = (1.0 - s * s).astype(BF16)
-        table_ref[pl.ds(first + k_count, rows), :] = (s * c).astype(BF16)
-        return carry
-
-    lax.fori_loop(0, k_count // rows, fill, 0, unroll=2)
-    q_ref[...] += lax.dot_general(
-        cot, table_ref[...], (((1,), (1,)), ((), ())), preferred_element_type=F32
-    )
+
+    def turn(t):
+        k_tile = k_ref[t * tile : (t + 1) * tile, :]
+        turns_refs[t % 2][...] = jnp.dot(k_tile, pieces, preferred_element_type=F32)
+
+    def fill(t):
+        for row in range(0, tile, rows):
+            turns = turns_refs[t % 2][row : row + rows, :]
+            r = turns - jnp.round(turns)
+            u = r * r
+            s = SIN_HALF[-1]
+            for coefficient in SIN_HALF[-2::-1]:
+                s = s * u + coefficient
+            s = s * r
+            c = COS_HALF[-1]
+            for coefficient in COS_HALF[-2::-1]:
+                c = c * u + coefficient
+            first = t * tile + row
+            table_ref[first : first + rows, :] = (1.0 - s * s).astype(BF16)
+            table_ref[k_count + first : k_count + first + rows, :] = (s * c).astype(BF16)
+
+    def add(t):
+        for first in (t * tile, k_count + t * tile):
+            q_ref[:, first : first + tile] += lax.dot_general(
+                cot, table_ref[first : first + tile, :], (((1,), (1,)), ((), ())),
+                preferred_element_type=F32,
+            )
+
+    tiles = k_count // tile
+    turn(0)
+    for t in range(tiles):
+        if t > 0:
+            add(t - 1)
+        if t + 1 < tiles:
+            turn(t + 1)
+        fill(t)
+    add(tiles - 1)
     keep(step, slot).start()
 
     @pl.when(step == last)
@@ -89,11 +112,11 @@
         keep(step, slot).wait()
 
 
-def front(mix, grad, frac, k_triple, rows=16, block=1024):
+def front(mix, grad, frac, k_triple, rows=16, tile=128, block=1024):
     channels, atoms = grad.shape
     k_count = k_triple.shape[0]
     return pl.pallas_call(
-        functools.partial(front_kernel, rows),
+        functools.partial(front_kernel, rows, tile),
         grid=(atoms // block,),
         in_specs=[
             pl.BlockSpec((channels, channels), lambda i: (0, 0)),
@@ -111,7 +134,8 @@
         ],
         scratch_shapes=[
             pltpu.VMEM((16, block), F32),
-            pltpu.VMEM((k_count, block), F32),
+            pltpu.VMEM((tile, block), F32),
+            pltpu.VMEM((tile, block), F32),
             pltpu.VMEM((2, 2 * k_count, block), BF16),
             pltpu.SemaphoreType.DMA((2,)),
         ],
@@ -121,37 +145,22 @@
     )(mix, grad, frac, k_triple)
 
 
-def long_kernel(p_ref, table_ref, out_ref, held_ref, sems):
+def long_kernel(p_ref, table_ref, out_ref):
     parts, _, own = out_ref.shape
-    depth = held_ref.shape[0]
-
-    def fetch(at):
-        columns = slice(at * own, (at + 1) * own)
-        return pltpu.make_async_copy(
-            table_ref.at[:, columns], held_ref.at[at % depth], sems.at[at % depth]
-        )
-
-    for at in range(depth - 1):
-        fetch(at).start()
     for at in range(parts):
-        if at + depth - 1 < parts:
-            fetch(at + depth - 1).start()
-        fetch(at).wait()
         out_ref[at] = jnp.dot(
-            p_ref[...], held_ref[at % depth], preferred_element_type=F32
+            p_ref[...], table_ref[:, at * own : (at + 1) * own], preferred_element_type=F32
         ).astype(BF16)
 
 
 def long_parts(p, table, parts):
-    channels, depth = p.shape
-    own = table.shape[1] // parts
+    whole = pl.BlockSpec(memory_space=pltpu.VMEM)
     return pl.pallas_call(
         long_kernel,
-        in_specs=[pl.BlockSpec(memory_space=pltpu.VMEM), pl.BlockSpec(memory_space=pltpu.HBM)],
-        out_specs=pl.BlockSpec(memory_space=pltpu.VMEM),
-        out_shape=jax.ShapeDtypeStruct((parts, channels, own), BF16),
-        scratch_shapes=[pltpu.VMEM((4, depth, own), BF16), pltpu.SemaphoreType.DMA((4,))],
-        compiler_params=pltpu.CompilerParams(vmem_limit_bytes=12 << 20),
+        in_specs=[whole, whole],
+        out_specs=whole,
+        out_shape=jax.ShapeDtypeStruct((parts, p.shape[0], table.shape[1] // parts), BF16),
+        compiler_params=pltpu.CompilerParams(vmem_limit_bytes=24 << 20),
         cost_estimate=pl.CostEstimate(flops=800_000_000, bytes_accessed=14_000_000, transcendentals=0),
         name="long_parts",
     )(p, table)
@@ -195,7 +204,7 @@
     masked = jnp.where(slot < count_ref[...], weight_ref[...], 0.0)
     for piece, slots_ref in enumerate(slots_refs):
         cut = slice(piece * LANES, (piece + 1) * LANES)
-        slots_ref[...] = index_ref[:, cut]
+        slots_ref[:, : index_ref.shape[0]] = index_ref[:, cut].T
         masked_ref[cut, :] = masked[:, cut].T
     leave.wait()
 
@@ -231,46 +240,63 @@
             jax.ShapeDtypeStruct((2 * per_side, LANES), BF16),
             jax.ShapeDtypeStruct((own, slots), F32),
         ]
-        + [jax.ShapeDtypeStruct((slots, LANES), jnp.int32)] * (own // LANES),
+        + [jax.ShapeDtypeStruct((LANES, LANES), jnp.int32)] * (own // LANES),
         compiler_params=pltpu.CompilerParams(vmem_limit_bytes=12 << 20),
         cost_estimate=pl.CostEstimate(flops=1_000_000_000, bytes_accessed=8_000_000, transcendentals=0),
         name="prepare",
     )(ka, halo, mix_wide, grad, index, weight, count)
 
 
-def short_kernel(index_ref, weight_ref, rows_ref, out_ref, sums_ref):
+def short_kernel(index_ref, weight_ref, rows_ref, out_ref, sums_ref, sems, *windows):
     sublane = lax.broadcasted_iota(jnp.int32, (8, LANES), 0)
-
-    def group(g, carry):
-        first = pl.multiple_of(g * 8, 8)
-        weights = weight_ref[pl.ds(first, 8), :]
-        total = jnp.zeros((8, LANES), F32)
-        for s in range(weight_ref.shape[1]):
-            picked = jnp.broadcast_to(rows_ref[index_ref[s * LANES + first]], (8, LANES))
-            for a in range(1, 8):
-                row = jnp.broadcast_to(rows_ref[index_ref[s * LANES + first + a]], (8, LANES))
-                picked = jnp.where(sublane == a, row, picked)
-            total = total + picked * weights[:, s : s + 1]
-        sums_ref[pl.ds(first, 8), :] = total
+    groups, depth = LANES // 8, len(windows)
+
+    def fetch(g, w):
+        block = index_ref.at[pl.ds(pl.multiple_of(g * 8, 8), 8)]
+        return pltpu.make_async_copy(block, windows[w], sems.at[w])
+
+    for w in range(depth):
+        fetch(w, w).start()
+
+    def round_of_groups(i, carry):
+        for w in range(depth):
+            g = i * depth + w
+            fetch(g, w).wait()
+            first = pl.multiple_of(g * 8, 8)
+            weights = weight_ref[pl.ds(first, 8), :]
+            total = jnp.zeros((8, LANES), F32)
+            for s in range(weight_ref.shape[1]):
+                picked = jnp.broadcast_to(rows_ref[windows[w][0, s]], (8, LANES))
+                for a in range(1, 8):
+                    row = jnp.broadcast_to(rows_ref[windows[w][a, s]], (8, LANES))
+                    picked = jnp.where(sublane == a, row, picked)
+                total = total + picked * weights[:, s : s + 1]
+            sums_ref[pl.ds(first, 8), :] = total
+
+            @pl.when(g + depth < groups)
+            def _(g=g, w=w):
+                fetch(g + depth, w).start()
+
         return carry
 
-    lax.fori_loop(0, LANES // 8, group, 0)
+    lax.fori_loop(0, groups // depth, round_of_groups, 0)
     out_ref[...] = sums_ref[...].T[: out_ref.shape[0], :]
 
 
-def short_sums(piece, channels, index, weight, rows):
+def short_sums(piece, channels, index, weight, rows, depth=4):
     slots = weight.shape[1]
     return pl.pallas_call(
         short_kernel,
         grid=(1,),
         in_specs=[
-            pl.BlockSpec(memory_space=pltpu.SMEM),
+            pl.BlockSpec(memory_space=pltpu.VMEM),
             pl.BlockSpec((LANES, slots), lambda i: (piece, 0)),
             pl.BlockSpec(memory_space=pltpu.VMEM),
         ],
         out_specs=pl.BlockSpec(memory_space=pltpu.VMEM),
         out_shape=jax.ShapeDtypeStruct((channels, LANES), F32),
-        scratch_shapes=[pltpu.VMEM((LANES, LANES), F32)],
+        scratch_shapes=[pltpu.VMEM((LANES, LANES), F32), pltpu.SemaphoreType.DMA((depth,))]
+        + [pltpu.SMEM((8, LANES), jnp.int32)] * depth,
         compiler_params=pltpu.CompilerParams(vmem_limit_bytes=6 << 20),
         cost_estimate=pl.CostEstimate(flops=100_000_000, bytes_accessed=400_000, transcendentals=0),
         name="short_sums",
@@ -313,7 +339,7 @@
 
     def short_piece():
         piece = len(short)
-        short.append(short_sums(piece, channels, slots[piece].reshape(-1), masked, extended))
+        short.append(short_sums(piece, channels, slots[piece], masked, extended))
 
     def beside(value, bit, pieces):
         nonlocal slots
@@ -342,7 +368,7 @@
     bit = 2
     while bit < dom_size:
         rounded = total.astype(BF16)
-        total = rounded.astype(F32) + beside(rounded, bit, 0 if bit == 8 else 1)
+        total = rounded.astype(F32) + beside(rounded, bit, 0 if bit == 16 else 1)
         bit *= 2
     partner = beside(total, 1, 0)
     q = jnp.where(
@@ -355,7 +381,6 @@
     d_filter = (struct_fac[0] * q_cos + struct_fac[1] * q_sin) / atom_total
     p = jnp.concatenate([ewald_filter * q_cos, ewald_filter * q_sin], axis=1).astype(BF16)
 
-    table = pltpu.with_memory_space_constraint(table, pltpu.HBM)
     parts = long_parts(p, table, ka_size)
     parts, slots = lax.optimization_barrier((parts, slots))
     parts = lax.all_to_all(parts, "ka", 0, 0, tiled=True)

time: 108 us -> 95.4 us (0.88)
  Pallas kernels: 67.4 us -> 51.7 us
  local copies, waits for them, and re-layouts: 7.83 us -> 12.4 us
  waiting for transfers between devices: 6.19 us -> 3.81 us
  starting transfers between devices: 22.3 us -> 23.4 us
    pallas_call x6, Pallas kernels: 36.4 us -> 27.1 us  [short_sums(): pl.pallas_call(short_kernel, grid=(1,), in_specs=[pl.BlockSpec(memory_spa...]
    pallas_call x2, Pallas kernels: 23.8 us -> 17.4 us  [the longest x1 14.2 us: front(): pl.pallas_call(functools.partial(front_kernel, rows, tile), grid=(atoms /...]
    unnamed x29 -> x31, local copies, waits for them, and re-layouts: 6.84 us -> 11.4 us
    ppermute x6, waiting for transfers between devices: 6.18 us -> 3.8 us  [swapped(): lax.ppermute(block, axis, [(i, i ^ bit) for i in range(lax.axis_size(axis...]
  transfers between devices with their start and end apart: 9 -> 9, of which waited for: 3 -> 3; matrix products, arithmetic and copies ran while one was open for 1% -> 1% of each run, Pallas kernels for 50% -> 44%
where the time goes in v5:
time: 95.4 us; the launch traced here: 94.9 us
  Pallas kernels  51.7 us (54%)
  starting transfers between devices  23.4 us (25%)
  local copies, waits for them, and re-layouts  12.4 us (13%)
  waiting for transfers between devices  3.81 us (4%)
  other arithmetic  2.63 us (3%)
  between operations  0.98 us (1%)
    pallas_call x6, Pallas kernels, short_sums(): pl.pallas_call(short_kernel, grid=(1,), in_specs=[pl.BlockSpec(memory_spa...  27.1 us
    pallas_call x1, Pallas kernels, front(): pl.pallas_call(functools.partial(front_kernel, rows, tile), grid=(atoms /...  14.2 us
    ppermute x6, starting transfers between devices, swapped(): lax.ppermute(block, axis, [(i, i ^ bit) for i in range(lax.axis_size(axis...  13.3 us
    unnamed x31, local copies, waits for them, and re-layouts  11.4 us
    pallas_call x1, Pallas kernels, prepare(): pl.pallas_call(prepare_kernel, grid_spec=pltpu.PrefetchScalarGridSpec(num...  7.24 us
    all_to_all x1, starting transfers between devices, local(): parts = lax.all_to_all(parts, 'ka', 0, 0, tiled=True)  6.65 us
    ppermute x6, waiting for transfers between devices, swapped(): lax.ppermute(block, axis, [(i, i ^ bit) for i in range(lax.axis_size(axis...  3.8 us
    ppermute x2, starting transfers between devices, shifted(): return lax.ppermute(block, axis, route)  3.41 us
  transfers between devices with their start and end apart: 9, of which 3 were waited for; matrix products, arithmetic and copies ran while one was open for 1% of the time, Pallas kernels for 44%

profile of v5, /device:TPU:1, one launch (start us, length us, event | category | flops | bytes accessed | tf_op | source)
XLA Modules:
  0.0 94.9 jit_solution(15928799975874623058)
XLA Ops:
  0.6 0.0 copy-start.12
  0.6 0.0 copy-start.8
  0.7 0.7 pad.4.mix_ref
  1.4 0.0 copy-start.4
  1.4 1.1 %copy-done.4 = bf16[64,6144]{1,0:T(8,128)(2,1)S(1)} copy-done((bf16[64,6144]{1,0:T(8,128)(2,1)S(1)}, bf16[64,6144]{1,0:T(8,128)(2,1)}, u32[]{:S(2)}) %copy-start.4) | copy-done | bytes 786456
  2.5 0.0 copy-start.7
  2.5 0.7 copy-done.7
  3.3 0.0 copy-start.9
  3.3 0.7 copy-done.9
  4.0 0.0 copy-start.5
  4.0 0.0 copy-start.6
  4.0 7.2 %prepare.1 = (f32[7680,128]{1,0:T(8,128)}, bf16[1536,128]{1,0:T(8,128)(2,1)S(1)}, f32[768,48]{1,0:T(8,128)S(1)}, s32[128,128]{1,0:T(8,128)S(1)}, s32[128,128]{1,...) custom-call(s32[1]{0:T(128)} %bitcast.ka_ref, ...), custom_call_target="tpu_custom_call" | custom-call | flops 1000000000 | bytes 8000000 | tf_op jit(solution)/shard_map/prepare/pallas_call | solution.py:218
  11.2 3.1 %collective-permute-start = (bf16[768,128]{1,0:T(8,128)(2,1)S(1)}, bf16[768,128]{1,0:T(8,128)(2,1)S(1)}, u32[]{:S(2)}, u32[]{:S(2)}) collective-permute-start(bf16[768,128]{1,0:T(8,128)(2,1)S(1)} %get-tuple-element.121), channel_id=1, source_target_pairs={{248,0},{0,8},{8,16},{16,24},{24,32},{32,40},{40,48},{48,56},{56,6... | collective-permute-start | bytes 589832 | tf_op jit(solution)/shard_map/ppermute | solution.py:34
  14.3 0.3 collective-permute-start.1
  14.6 0.0 copy-done.12
  14.7 0.1 pad.16.clone
  14.7 0.1 maximum_maximum_fusion
  14.8 0.1 copy.14.k_ref
  14.9 0.0 copy-done.8
  15.0 0.0 copy-done.5
  15.0 0.0 copy-done.6
  15.0 14.2 %structure_sums.1 = (f32[64,1024]{1,0:T(8,128)S(1)}, bf16[1024,6144]{1,0:T(8,128)(2,1)}) custom-call(bf16[64,64]{1,0:T(8,128)(2,1)S(1)} %copy-done.8, bf16[64,6144]{1,0:T(8,128)(2,1)S(1)} %copy-done.5, f32[3,6144]{1,0:T(4,128)S(1)} %copy-done.6, bf16[512,16]{1,0:T(8,128)(2,1)S(1)} %copy.14.k_ref), custom_call_target="tpu_custom_call" | custom-call | flops 20000000000 | bytes 14000000 | tf_op jit(solution)/shard_map/structure_sums/pallas_call | solution.py:118
  29.2 0.0 collective-permute-done
  29.2 0.0 collective-permute-done.1
  29.3 4.6 %collective-permute-start.2 = (bf16[32,1024]{1,0:T(8,128)(2,1)S(1)}, bf16[32,1024]{1,0:T(8,128)(2,1)S(1)}, u32[]{:S(2)}, u32[]{:S(2)}) collective-permute-start(bf16[32,1024]{1,0:T(8,128)(2,1)S(1)} %dynamic-slice_convert_fusion), channel_id=1, source_target_pairs={{0,8},{8,0},{16,24},{24,16},{32,40},{40,32},{48,56},{56,48},{64,72... | collective-permute-start | bytes 196616 | tf_op jit(solution)/shard_map/ppermute | solution.py:28
  33.9 0.9 collective-permute-done.2
  34.8 0.1 collective-permute-start.3
  34.9 0.9 convert_dynamic-update-slice_fusion
  35.8 0.0 copy-start
  35.8 2.1 %copy-done = f32[7680,128]{1,0:T(8,128)S(1)} copy-done((f32[7680,128]{1,0:T(8,128)S(1)}, f32[7680,128]{1,0:T(8,128)}, u32[]{:S(2)}) %copy-start) | copy-done | bytes 3932184
  37.9 0.0 copy-start.1
  37.9 4.5 %short_sums.6 = f32[64,128]{1,0:T(8,128)S(1)} custom-call(s32[128,128]{1,0:T(8,128)S(1)} %get-tuple-element.78.index_ref, f32[768,48]{1,0:T(8,128)S(1)} %get-tuple-element.79.weight_ref, f32[7680,1,128]{2,1,0:T(1,128)S(1)} %bitcast.15), custom_call_target="tpu_custom_call" | custom-call | flops 100000000 | bytes 400000 | tf_op jit(solution)/shard_map/short_sums/pallas_call | solution.py:288
  42.5 0.0 collective-permute-done.3
  42.5 0.0 copy-start.10
  42.5 0.0 copy-start.11
  42.5 1.5 %collective-permute-start.4 = (bf16[32,1024]{1,0:T(8,128)(2,1)S(1)}, bf16[32,1024]{1,0:T(8,128)(2,1)S(1)}, u32[]{:S(2)}, u32[]{:S(2)}) collective-permute-start(bf16[32,1024]{1,0:T(8,128)(2,1)S(1)} %add_convert_fusion.3), channel_id=1, source_target_pairs={{0,32},{8,40},{16,48},{24,56},{32,0},{40,8},{48,16},{56,24},{64,96... | collective-permute-start | bytes 196616 | tf_op jit(solution)/shard_map/ppermute | solution.py:28
  44.0 0.0 copy-done.1
  44.0 4.5 %short_sums.7 = f32[64,128]{1,0:T(8,128)S(1)} custom-call(s32[128,128]{1,0:T(8,128)S(1)} %get-tuple-element.90.index_ref, f32[768,48]{1,0:T(8,128)S(1)} %get-tuple-element.79.weight_ref, f32[7680,1,128]{2,1,0:T(1,128)S(1)} %bitcast.16), custom_call_target="tpu_custom_call" | custom-call | flops 100000000 | bytes 400000 | tf_op jit(solution)/shard_map/short_sums/pallas_call | solution.py:288
  48.5 0.0 collective-permute-done.4
  48.6 3.0 %collective-permute-start.5 = (bf16[32,1024]{1,0:T(8,128)(2,1)S(1)}, bf16[32,1024]{1,0:T(8,128)(2,1)S(1)}, u32[]{:S(2)}, u32[]{:S(2)}) collective-permute-start(bf16[32,1024]{1,0:T(8,128)(2,1)S(1)} %add_convert_fusion.2), channel_id=1, source_target_pairs={{0,64},{8,72},{16,80},{24,88},{32,96},{40,104},{48,112},{56,120},{... | collective-permute-start | bytes 196616 | tf_op jit(solution)/shard_map/ppermute | solution.py:28
  51.5 4.5 %short_sums.8 = f32[64,128]{1,0:T(8,128)S(1)} custom-call(s32[128,128]{1,0:T(8,128)S(1)} %get-tuple-element.97.index_ref, f32[768,48]{1,0:T(8,128)S(1)} %get-tuple-element.79.weight_ref, f32[7680,1,128]{2,1,0:T(1,128)S(1)} %bitcast.17), custom_call_target="tpu_custom_call" | custom-call | flops 100000000 | bytes 400000 | tf_op jit(solution)/shard_map/short_sums/pallas_call | solution.py:288
  56.0 0.0 collective-permute-done.5
  56.1 1.3 %collective-permute-start.6 = (bf16[32,1024]{1,0:T(8,128)(2,1)S(1)}, bf16[32,1024]{1,0:T(8,128)(2,1)S(1)}, u32[]{:S(2)}, u32[]{:S(2)}) collective-permute-start(bf16[32,1024]{1,0:T(8,128)(2,1)S(1)} %add_convert_fusion.1), channel_id=1, source_target_pairs={{0,128},{8,136},{16,144},{24,152},{32,160},{40,168},{48,176},{56,1... | collective-permute-start | bytes 196616 | tf_op jit(solution)/shard_map/ppermute | solution.py:28
  57.4 1.9 %collective-permute-done.6 = bf16[32,1024]{1,0:T(8,128)(2,1)S(1)} collective-permute-done((bf16[32,1024]{1,0:T(8,128)(2,1)S(1)}, bf16[32,1024]{1,0:T(8,128)(2,1)S(1)}, u32[]{:S(2)}, u32[]{:S(2)}) %collective-permute-start.6) | collective-permute-done | bytes 65568 | tf_op jit(solution)/shard_map/ppermute | solution.py:28
  59.3 2.9 %collective-permute-start.7 = (f32[32,1024]{1,0:T(8,128)S(1)}, f32[32,1024]{1,0:T(8,128)S(1)}, u32[]{:S(2)}, u32[]{:S(2)}) collective-permute-start(f32[32,1024]{1,0:T(8,128)S(1)} %convert_add_fusion), channel_id=1, source_target_pairs={{0,8},{8,0},{16,24},{24,16},{32,40},{40,32},{48,56},{56,48},{64,72... | collective-permute-start | bytes 393224 | tf_op jit(solution)/shard_map/ppermute | solution.py:28
  62.2 1.0 %collective-permute-done.7 = f32[32,1024]{1,0:T(8,128)S(1)} collective-permute-done((f32[32,1024]{1,0:T(8,128)S(1)}, f32[32,1024]{1,0:T(8,128)S(1)}, u32[]{:S(2)}, u32[]{:S(2)}) %collective-permute-start.7) | collective-permute-done | bytes 131104 | tf_op jit(solution)/shard_map/ppermute | solution.py:28
  63.2 0.0 copy-done.10
  63.2 0.0 copy-done.11
  63.2 0.7 multiply_convert_fusion.1
  64.0 0.0 copy-start.3
  64.0 4.6 %copy-done.3 = bf16[1024,6144]{1,0:T(8,128)(2,1)S(1)} copy-done((bf16[1024,6144]{1,0:T(8,128)(2,1)S(1)}, bf16[1024,6144]{1,0:T(8,128)(2,1)}, u32[]{:S(2)}) %copy-start.3) | copy-done | bytes 12582936
  68.5 3.2 %long_parts.1 = bf16[8,64,768]{2,1,0:T(8,128)(2,1)} custom-call(bf16[64,1024]{1,0:T(8,128)(2,1)S(1)} %pad_maximum_fusion.p_ref, bf16[1024,6144]{1,0:T(8,128)(2,1)S(1)} %copy-done.3), custom_call_target="tpu_custom_call" | custom-call | flops 800000000 | bytes 14000000 | tf_op jit(solution)/shard_map/long_parts/pallas_call | solution.py:158
  71.7 6.6 %all-to-all-start = ((bf16[8,64,768]{2,1,0:T(8,128)(2,1)}), bf16[8,64,768]{2,1,0:T(8,128)(2,1)S(1)}, u32[]{:S(2)}, u32[]{:S(2)}) async-start(bf16[8,64,768]{2,1,0:T(8,128)(2,1)} %long_parts.1), calls=%async_computation | async-start | bytes 1572864 | tf_op jit(solution)/shard_map/all_to_all | solution.py:386
  78.4 0.0 copy-start.2
  78.4 2.1 %copy-done.2 = f32[7680,128]{1,0:T(8,128)S(1)} copy-done((f32[7680,128]{1,0:T(8,128)S(1)}, f32[7680,128]{1,0:T(8,128)}, u32[]{:S(2)}) %copy-start.2) | copy-done | bytes 3932184
  80.5 4.5 %short_sums.11 = f32[64,128]{1,0:T(8,128)S(1)} custom-call(s32[128,128]{1,0:T(8,128)S(1)} %get-tuple-element.117.index_ref, f32[768,48]{1,0:T(8,128)S(1)} %get-tuple-element.79.weight_ref, f32[7680,1,128]{2,1,0:T(1,128)S(1)} %bitcast.18), custom_call_target="tpu_custom_call" | custom-call | flops 100000000 | bytes 400000 | tf_op jit(solution)/shard_map/short_sums/pallas_call | solution.py:288
  85.0 4.5 %short_sums.10 = f32[64,128]{1,0:T(8,128)S(1)} custom-call(s32[128,128]{1,0:T(8,128)S(1)} %get-tuple-element.116.index_ref, f32[768,48]{1,0:T(8,128)S(1)} %get-tuple-element.79.weight_ref, f32[7680,1,128]{2,1,0:T(1,128)S(1)} %bitcast.19), custom_call_target="tpu_custom_call" | custom-call | flops 100000000 | bytes 400000 | tf_op jit(solution)/shard_map/short_sums/pallas_call | solution.py:288
  89.5 4.5 %short_sums.9 = f32[64,128]{1,0:T(8,128)S(1)} custom-call(s32[128,128]{1,0:T(8,128)S(1)} %get-tuple-element.115.index_ref, f32[768,48]{1,0:T(8,128)S(1)} %get-tuple-element.79.weight_ref, f32[7680,1,128]{2,1,0:T(1,128)S(1)} %bitcast.20), custom_call_target="tpu_custom_call" | custom-call | flops 100000000 | bytes 400000 | tf_op jit(solution)/shard_map/short_sums/pallas_call | solution.py:288
  94.1 0.0 all-to-all-done
  94.1 0.1 convert_reduce_fusion
  94.2 0.7 add_convert_fusion
  (17 shorter events, 0.2 us)
Async XLA Ops:
  0.6 14.0 %copy-start.12 = (s32[3,512]{1,0:T(4,128)S(1)}, s32[3,512]{1,0:T(4,128)}, u32[]{:S(2)}) copy-start(s32[3,512]{1,0:T(4,128)} %param.13) | copy-start | bytes 18436
  0.6 14.3 %copy-start.8 = (bf16[64,64]{1,0:T(8,128)(2,1)S(1)}, bf16[64,64]{1,0:T(8,128)(2,1)}, u32[]{:S(2)}) copy-start(bf16[64,64]{1,0:T(8,128)(2,1)} %mix_ref.1) | copy-start | bytes 24580
  1.4 1.1 %copy-start.4 = (bf16[64,6144]{1,0:T(8,128)(2,1)S(1)}, bf16[64,6144]{1,0:T(8,128)(2,1)}, u32[]{:S(2)}) copy-start(bf16[64,6144]{1,0:T(8,128)(2,1)} %grad_ref.3) | copy-start | bytes 2359300
  2.5 0.7 copy-start.7
  3.3 0.7 copy-start.9
  4.0 11.0 %copy-start.5 = (bf16[64,6144]{1,0:T(8,128)(2,1)S(1)}, bf16[64,6144]{1,0:T(8,128)(2,1)}, u32[]{:S(2)}) copy-start(bf16[64,6144]{1,0:T(8,128)(2,1)} %grad_ref.3) | copy-start | bytes 2359300
  4.0 11.0 %copy-start.6 = (f32[3,6144]{1,0:T(4,128)S(1)}, f32[3,6144]{1,0:T(4,128)}, u32[]{:S(2)}) copy-start(f32[3,6144]{1,0:T(4,128)} %frac_ref) | copy-start | bytes 221188
  11.2 18.0 %collective-permute-start = (bf16[768,128]{1,0:T(8,128)(2,1)S(1)}, bf16[768,128]{1,0:T(8,128)(2,1)S(1)}, u32[]{:S(2)}, u32[]{:S(2)}) collective-permute-start(bf16[768,128]{1,0:T(8,128)(2,1)S(1)} %get-tuple-element.121), channel_id=1, source_target_pairs={{248,0},{0,8},{8,16},{16,24},{24,32},{32,40},{40,48},{48,56},{56,6... | collective-permute-start | bytes 589832 | tf_op jit(solution)/shard_map/ppermute | solution.py:34
  14.3 14.9 %collective-permute-start.1 = (bf16[768,128]{1,0:T(8,128)(2,1)S(1)}, bf16[768,128]{1,0:T(8,128)(2,1)S(1)}, u32[]{:S(2)}, u32[]{:S(2)}) collective-permute-start(bf16[768,128]{1,0:T(8,128)(2,1)S(1)} %get-tuple-element.120), channel_id=1, source_target_pairs={{8,0},{16,8},{24,16},{32,24},{40,32},{48,40},{56,48},{64,56},{72,6... | collective-permute-start | bytes 589832 | tf_op jit(solution)/shard_map/ppermute | solution.py:34
  29.3 5.5 %collective-permute-start.2 = (bf16[32,1024]{1,0:T(8,128)(2,1)S(1)}, bf16[32,1024]{1,0:T(8,128)(2,1)S(1)}, u32[]{:S(2)}, u32[]{:S(2)}) collective-permute-start(bf16[32,1024]{1,0:T(8,128)(2,1)S(1)} %dynamic-slice_convert_fusion), channel_id=1, source_target_pairs={{0,8},{8,0},{16,24},{24,16},{32,40},{40,32},{48,56},{56,48},{64,72... | collective-permute-start | bytes 196616 | tf_op jit(solution)/shard_map/ppermute | solution.py:28
  34.8 7.7 %collective-permute-start.3 = (bf16[32,1024]{1,0:T(8,128)(2,1)S(1)}, bf16[32,1024]{1,0:T(8,128)(2,1)S(1)}, u32[]{:S(2)}, u32[]{:S(2)}) collective-permute-start(bf16[32,1024]{1,0:T(8,128)(2,1)S(1)} %add_convert_fusion.4), channel_id=1, source_target_pairs={{0,16},{8,24},{16,0},{24,8},{32,48},{40,56},{48,32},{56,40},{64,80... | collective-permute-start | bytes 196616 | tf_op jit(solution)/shard_map/ppermute | solution.py:28
  35.8 2.1 %copy-start = (f32[7680,128]{1,0:T(8,128)S(1)}, f32[7680,128]{1,0:T(8,128)}, u32[]{:S(2)}) copy-start(f32[7680,128]{1,0:T(8,128)} %convert_dynamic-update-slice_fusion) | copy-start | bytes 11796484
  37.9 6.1 %copy-start.1 = (f32[7680,128]{1,0:T(8,128)S(1)}, f32[7680,128]{1,0:T(8,128)}, u32[]{:S(2)}) copy-start(f32[7680,128]{1,0:T(8,128)} %convert_dynamic-update-slice_fusion) | copy-start | bytes 11796484
  42.5 20.7 %copy-start.10 = (f32[2,64,512]{2,1,0:T(8,128)S(1)}, f32[2,64,512]{2,1,0:T(8,128)}, u32[]{:S(2)}) copy-start(f32[2,64,512]{2,1,0:T(8,128)} %param.15) | copy-start | bytes 786436
  42.5 20.7 %copy-start.11 = (f32[64,512]{1,0:T(8,128)S(1)}, f32[64,512]{1,0:T(8,128)}, u32[]{:S(2)}) copy-start(f32[64,512]{1,0:T(8,128)} %param.14) | copy-start | bytes 393220
  42.5 6.0 %collective-permute-start.4 = (bf16[32,1024]{1,0:T(8,128)(2,1)S(1)}, bf16[32,1024]{1,0:T(8,128)(2,1)S(1)}, u32[]{:S(2)}, u32[]{:S(2)}) collective-permute-start(bf16[32,1024]{1,0:T(8,128)(2,1)S(1)} %add_convert_fusion.3), channel_id=1, source_target_pairs={{0,32},{8,40},{16,48},{24,56},{32,0},{40,8},{48,16},{56,24},{64,96... | collective-permute-start | bytes 196616 | tf_op jit(solution)/shard_map/ppermute | solution.py:28
  48.6 7.5 %collective-permute-start.5 = (bf16[32,1024]{1,0:T(8,128)(2,1)S(1)}, bf16[32,1024]{1,0:T(8,128)(2,1)S(1)}, u32[]{:S(2)}, u32[]{:S(2)}) collective-permute-start(bf16[32,1024]{1,0:T(8,128)(2,1)S(1)} %add_convert_fusion.2), channel_id=1, source_target_pairs={{0,64},{8,72},{16,80},{24,88},{32,96},{40,104},{48,112},{56,120},{... | collective-permute-start | bytes 196616 | tf_op jit(solution)/shard_map/ppermute | solution.py:28
  56.1 3.2 %collective-permute-start.6 = (bf16[32,1024]{1,0:T(8,128)(2,1)S(1)}, bf16[32,1024]{1,0:T(8,128)(2,1)S(1)}, u32[]{:S(2)}, u32[]{:S(2)}) collective-permute-start(bf16[32,1024]{1,0:T(8,128)(2,1)S(1)} %add_convert_fusion.1), channel_id=1, source_target_pairs={{0,128},{8,136},{16,144},{24,152},{32,160},{40,168},{48,176},{56,1... | collective-permute-start | bytes 196616 | tf_op jit(solution)/shard_map/ppermute | solution.py:28
  59.3 3.9 %collective-permute-start.7 = (f32[32,1024]{1,0:T(8,128)S(1)}, f32[32,1024]{1,0:T(8,128)S(1)}, u32[]{:S(2)}, u32[]{:S(2)}) collective-permute-start(f32[32,1024]{1,0:T(8,128)S(1)} %convert_add_fusion), channel_id=1, source_target_pairs={{0,8},{8,0},{16,24},{24,16},{32,40},{40,32},{48,56},{56,48},{64,72... | collective-permute-start | bytes 393224 | tf_op jit(solution)/shard_map/ppermute | solution.py:28
  64.0 4.6 %copy-start.3 = (bf16[1024,6144]{1,0:T(8,128)(2,1)S(1)}, bf16[1024,6144]{1,0:T(8,128)(2,1)}, u32[]{:S(2)}) copy-start(bf16[1024,6144]{1,0:T(8,128)(2,1)} %get-tuple-element.107.table_ref) | copy-start | bytes 37748740
  71.7 22.4 %all-to-all-start = ((bf16[8,64,768]{2,1,0:T(8,128)(2,1)}), bf16[8,64,768]{2,1,0:T(8,128)(2,1)S(1)}, u32[]{:S(2)}, u32[]{:S(2)}) async-start(bf16[8,64,768]{2,1,0:T(8,128)(2,1)} %long_parts.1), calls=%async_computation | async-start | bytes 1572864 | tf_op jit(solution)/shard_map/all_to_all | solution.py:386
  78.4 2.1 %copy-start.2 = (f32[7680,128]{1,0:T(8,128)S(1)}, f32[7680,128]{1,0:T(8,128)}, u32[]{:S(2)}) copy-start(f32[7680,128]{1,0:T(8,128)} %convert_dynamic-update-slice_fusion) | copy-start | bytes 11796484

commit v6 on v5

--- a/solution.py
+++ b/solution.py
@@ -145,32 +145,44 @@
     )(mix, grad, frac, k_triple)
 
 
-def long_kernel(p_ref, table_ref, out_ref):
+def long_kernel(p_ref, table_ref, out_ref, held_ref, sems):
     parts, _, own = out_ref.shape
-    for at in range(parts):
-        out_ref[at] = jnp.dot(
-            p_ref[...], table_ref[:, at * own : (at + 1) * own], preferred_element_type=F32
-        ).astype(BF16)
+    fetches = [
+        pltpu.make_async_copy(
+            table_ref.at[:, at * own : (at + 1) * own], held_ref.at[at], sems.at[at]
+        )
+        for at in range(parts)
+    ]
+    for fetch in fetches:
+        fetch.start()
+    for at, fetch in enumerate(fetches):
+        fetch.wait()
+        out_ref[at] = jnp.dot(p_ref[...], held_ref[at], preferred_element_type=F32).astype(BF16)
 
 
 def long_parts(p, table, parts):
-    whole = pl.BlockSpec(memory_space=pltpu.VMEM)
+    channels, depth = p.shape
+    own = table.shape[1] // parts
     return pl.pallas_call(
         long_kernel,
-        in_specs=[whole, whole],
-        out_specs=whole,
-        out_shape=jax.ShapeDtypeStruct((parts, p.shape[0], table.shape[1] // parts), BF16),
-        compiler_params=pltpu.CompilerParams(vmem_limit_bytes=24 << 20),
+        in_specs=[pl.BlockSpec(memory_space=pltpu.VMEM), pl.BlockSpec(memory_space=pltpu.HBM)],
+        out_specs=pl.BlockSpec(memory_space=pltpu.VMEM),
+        out_shape=jax.ShapeDtypeStruct((parts, channels, own), BF16),
+        scratch_shapes=[pltpu.VMEM((parts, depth, own), BF16), pltpu.SemaphoreType.DMA((parts,))],
+        compiler_params=pltpu.CompilerParams(vmem_limit_bytes=18 << 20),
         cost_estimate=pl.CostEstimate(flops=800_000_000, bytes_accessed=14_000_000, transcendentals=0),
         name="long_parts",
-    )(p, table)
+    )(p, pltpu.with_memory_space_constraint(table, pltpu.HBM))
 
 
 def prepare_kernel(
     ka_ref, halo_ref, mix_ref, grad_ref, index_ref, weight_ref, count_ref,
     rows_ref, send_ref, masked_ref, *refs,
 ):
-    *slots_refs, picked_ref, held_ref, sem = refs
+    *slots_refs, picked_ref, held_ref, wide_ref, sem = refs
+    channels = mix_ref.shape[0]
+    wide_ref[channels:, :] = jnp.zeros((LANES - channels, channels), BF16)
+    wide_ref[:channels, :] = mix_ref[...]
     atoms = grad_ref.shape[1]
     block = math.gcd(atoms, 512)
     sends, per_side = send_ref.shape[0], halo_ref.shape[1]
@@ -178,7 +190,7 @@
     def mix(i, carry):
         first = pl.multiple_of(i * block, block)
         mixed = lax.dot_general(
-            grad_ref[:, pl.ds(first, block)], mix_ref[...], (((0,), (1,)), ((), ())),
+            grad_ref[:, pl.ds(first, block)], wide_ref[...], (((0,), (1,)), ((), ())),
             preferred_element_type=F32,
         )
         held_ref[pl.ds(first, block), :] = mixed.astype(BF16).astype(F32)
@@ -189,15 +201,8 @@
     leave.start()
 
     for side in range(2):
-        def pick(i, carry, side=side):
-            first = pl.multiple_of(i * 32, 32)
-            for j in range(32):
-                picked_ref[pl.ds(side * per_side + first + j, 1), :] = held_ref[
-                    pl.ds(halo_ref[side, first + j], 1), :
-                ]
-            return carry
-
-        lax.fori_loop(0, per_side // 32, pick, 0)
+        for j in range(per_side):
+            picked_ref[side * per_side + j, :] = held_ref[halo_ref[side, j], :]
     send_ref[...] = picked_ref[...].astype(BF16)
 
     slot = lax.broadcasted_iota(jnp.int32, weight_ref.shape, 0)
@@ -209,7 +214,7 @@
     leave.wait()
 
 
-def prepare(ka, mix_wide, grad, index, weight, count, halo):
+def prepare(ka, mix, grad, index, weight, count, halo):
     channels, atoms = grad.shape
     slots = index.shape[0]
     per_side = halo.shape[1]
@@ -232,6 +237,7 @@
             scratch_shapes=[
                 pltpu.VMEM((2 * per_side, LANES), F32),
                 pltpu.VMEM((atoms, LANES), F32),
+                pltpu.VMEM((LANES, channels), BF16),
                 pltpu.SemaphoreType.DMA(()),
             ],
         ),
@@ -244,7 +250,7 @@
         compiler_params=pltpu.CompilerParams(vmem_limit_bytes=12 << 20),
         cost_estimate=pl.CostEstimate(flops=1_000_000_000, bytes_accessed=8_000_000, transcendentals=0),
         name="prepare",
-    )(ka, halo, mix_wide, grad, index, weight, count)
+    )(ka, halo, mix, grad, index, weight, count)
 
 
 def short_kernel(index_ref, weight_ref, rows_ref, out_ref, sums_ref, sems, *windows):
@@ -283,7 +289,7 @@
     out_ref[...] = sums_ref[...].T[: out_ref.shape[0], :]
 
 
-def short_sums(piece, channels, index, weight, rows, depth=4):
+def short_sums(piece, channels, index, weight, rows, flops, depth=4):
     slots = weight.shape[1]
     return pl.pallas_call(
         short_kernel,
@@ -298,7 +304,7 @@
         scratch_shapes=[pltpu.VMEM((LANES, LANES), F32), pltpu.SemaphoreType.DMA((depth,))]
         + [pltpu.SMEM((8, LANES), jnp.int32)] * depth,
         compiler_params=pltpu.CompilerParams(vmem_limit_bytes=6 << 20),
-        cost_estimate=pl.CostEstimate(flops=100_000_000, bytes_accessed=400_000, transcendentals=0),
+        cost_estimate=pl.CostEstimate(flops=flops, bytes_accessed=400_000, transcendentals=0),
         name="short_sums",
     )(index, weight, rows)
 
@@ -322,24 +328,22 @@
     k_count = k_index.shape[1]
 
     ka = lax.axis_index("ka").astype(jnp.int32)
-    mix_wide = jnp.pad(pair_mix, ((0, LANES - channels), (0, 0)))
     rows, send, masked, *slots = prepare(
         ka[None],
-        mix_wide,
-        grad_out,
-        pltpu.with_memory_space_constraint(nbr_index, pltpu.HBM),
-        pltpu.with_memory_space_constraint(pair_weight, pltpu.HBM),
-        nbr_count[None, :],
-        halo_send,
+        pair_mix,
+        *(
+            pltpu.with_memory_space_constraint(a, pltpu.HBM)
+            for a in (grad_out, nbr_index, pair_weight, nbr_count[None, :], halo_send)
+        ),
     )
     per_side = halo_send.shape[1]
     from_left = shifted(send[:per_side], "dom", 1)
     from_right = shifted(send[per_side:], "dom", -1)
     short = []
 
-    def short_piece():
+    def short_piece(flops):
         piece = len(short)
-        short.append(short_sums(piece, channels, slots[piece], masked, extended))
+        short.append(short_sums(piece, channels, slots[piece], masked, extended, flops))
 
     def beside(value, bit, pieces):
         nonlocal slots
@@ -347,7 +351,7 @@
         received = swapped(value, "dom", bit)
         start = len(short)
         for _ in range(pieces):
-            short_piece()
+            short_piece(4_000_000_000)
         received, short[start:] = lax.optimization_barrier((received, short[start:]))
         return received.astype(F32)
 
@@ -368,7 +372,7 @@
     bit = 2
     while bit < dom_size:
         rounded = total.astype(BF16)
-        total = rounded.astype(F32) + beside(rounded, bit, 0 if bit == 16 else 1)
+        total = rounded.astype(F32) + beside(rounded, bit, 0 if bit == 2 else 1)
         bit *= 2
     partner = beside(total, 1, 0)
     q = jnp.where(
@@ -385,7 +389,7 @@
     parts, slots = lax.optimization_barrier((parts, slots))
     parts = lax.all_to_all(parts, "ka", 0, 0, tiled=True)
     while len(short) < own_rows // LANES:
-        short_piece()
+        short_piece(100_000_000)
     long_own = jnp.sum(parts.astype(F32), axis=0)
     own_grad = lax.dynamic_slice_in_dim(grad_out, ka * own_rows, own_rows, 1).astype(F32)
     d_feat = (own_grad + long_own + jnp.concatenate(short, axis=1)).astype(BF16)

time: 95.4 us -> 88.4 us (0.927)
  local copies, waits for them, and re-layouts: 12.4 us -> 5.31 us
  Pallas kernels: 51.7 us -> 53.1 us
  starting transfers between devices: 23.4 us -> 22.1 us
    unnamed x31 -> x25, local copies, waits for them, and re-layouts: 11.4 us -> 5.06 us
    pallas_call x1, Pallas kernels: 3.18 us -> 6.12 us  [long_parts(): pl.pallas_call(long_kernel, in_specs=[pl.BlockSpec(memory_space=pltpu.VME...]
    pallas_call x1, Pallas kernels: 7.24 us -> 5.69 us  [prepare(): pl.pallas_call(prepare_kernel, grid_spec=pltpu.PrefetchScalarGridSpec(num...]
    ppermute x6, starting transfers between devices: 13.3 us -> 12.3 us  [swapped(): lax.ppermute(block, axis, [(i, i ^ bit) for i in range(lax.axis_size(axis...]
  transfers between devices with their start and end apart: 9 -> 9, of which waited for: 3 -> 3; matrix products, arithmetic and copies ran while one was open for 1% -> 1% of each run, Pallas kernels for 44% -> 47%
where the time goes in v6:
time: 88.4 us; the launch traced here: 88.2 us
  Pallas kernels  53.1 us (60%)
  starting transfers between devices  22.1 us (25%)
  local copies, waits for them, and re-layouts  5.31 us (6%)
  waiting for transfers between devices  4.07 us (5%)
  other arithmetic  2.63 us (3%)
  between operations  0.99 us (1%)
    pallas_call x6, Pallas kernels, short_sums(): pl.pallas_call(short_kernel, grid=(1,), in_specs=[pl.BlockSpec(memory_spa...  27.1 us
    pallas_call x1, Pallas kernels, front(): pl.pallas_call(functools.partial(front_kernel, rows, tile), grid=(atoms /...  14.2 us
    ppermute x6, starting transfers between devices, swapped(): lax.ppermute(block, axis, [(i, i ^ bit) for i in range(lax.axis_size(axis...  12.3 us
    all_to_all x1, starting transfers between devices, local(): parts = lax.all_to_all(parts, 'ka', 0, 0, tiled=True)  6.37 us
    pallas_call x1, Pallas kernels, long_parts(): pl.pallas_call(long_kernel, in_specs=[pl.BlockSpec(memory_space=pltpu.VME...  6.12 us
    pallas_call x1, Pallas kernels, prepare(): pl.pallas_call(prepare_kernel, grid_spec=pltpu.PrefetchScalarGridSpec(num...  5.69 us
    unnamed x25, local copies, waits for them, and re-layouts  5.06 us
    ppermute x6, waiting for transfers between devices, swapped(): lax.ppermute(block, axis, [(i, i ^ bit) for i in range(lax.axis_size(axis...  4.06 us
  transfers between devices with their start and end apart: 9, of which 3 were waited for; matrix products, arithmetic and copies ran while one was open for 1% of the time, Pallas kernels for 47%

profile of v6, /device:TPU:1, one launch (start us, length us, event | category | flops | bytes accessed | tf_op | source)
XLA Modules:
  0.0 88.2 jit_solution(2228623627091508024)
XLA Ops:
  0.6 0.0 copy-start.3
  0.6 0.0 copy-start.4
  0.7 0.0 copy-start.5
  0.7 0.8 copy-done.5
  1.5 0.0 copy-start.9
  1.5 0.0 copy-start.6
  1.5 5.7 %prepare.1 = (f32[7680,128]{1,0:T(8,128)}, bf16[1536,128]{1,0:T(8,128)(2,1)S(1)}, f32[768,48]{1,0:T(8,128)S(1)}, s32[128,128]{1,0:T(8,128)S(1)}, s32[128,128]{1,...) custom-call(s32[1]{0:T(128)} %bitcast.ka_ref, ...), custom_call_target="tpu_custom_call" | custom-call | flops 1000000000 | bytes 8000000 | tf_op jit(solution)/shard_map/prepare/pallas_call | solution.py:223
  7.2 3.1 %collective-permute-start = (bf16[768,128]{1,0:T(8,128)(2,1)S(1)}, bf16[768,128]{1,0:T(8,128)(2,1)S(1)}, u32[]{:S(2)}, u32[]{:S(2)}) collective-permute-start(bf16[768,128]{1,0:T(8,128)(2,1)S(1)} %get-tuple-element.127), channel_id=1, source_target_pairs={{248,0},{0,8},{8,16},{16,24},{24,32},{32,40},{40,48},{48,56},{56,6... | collective-permute-start | bytes 589832 | tf_op jit(solution)/shard_map/ppermute | solution.py:34
  10.3 0.3 collective-permute-start.1
  10.6 0.0 copy-done.9
  10.6 0.1 pad.11.clone
  10.7 0.1 maximum_maximum_fusion
  10.8 0.1 copy.14.k_ref
  10.9 0.0 copy-done.3
  10.9 0.0 copy-done.4
  10.9 0.0 copy-done.6
  10.9 14.2 %structure_sums.1 = (f32[64,1024]{1,0:T(8,128)S(1)}, bf16[1024,6144]{1,0:T(8,128)(2,1)}) custom-call(bf16[64,64]{1,0:T(8,128)(2,1)S(1)} %copy-done.6, bf16[64,6144]{1,0:T(8,128)(2,1)S(1)} %copy-done.3, f32[3,6144]{1,0:T(4,128)S(1)} %copy-done.4, bf16[512,16]{1,0:T(8,128)(2,1)S(1)} %copy.14.k_ref), custom_call_target="tpu_custom_call" | custom-call | flops 20000000000 | bytes 14000000 | tf_op jit(solution)/shard_map/structure_sums/pallas_call | solution.py:118
  25.2 0.0 collective-permute-done
  25.2 0.0 collective-permute-done.1
  25.2 4.6 %collective-permute-start.2 = (bf16[32,1024]{1,0:T(8,128)(2,1)S(1)}, bf16[32,1024]{1,0:T(8,128)(2,1)S(1)}, u32[]{:S(2)}, u32[]{:S(2)}) collective-permute-start(bf16[32,1024]{1,0:T(8,128)(2,1)S(1)} %dynamic-slice_convert_fusion), channel_id=1, source_target_pairs={{0,8},{8,0},{16,24},{24,16},{32,40},{40,32},{48,56},{56,48},{64,72... | collective-permute-start | bytes 196616 | tf_op jit(solution)/shard_map/ppermute | solution.py:28
  29.8 0.9 %collective-permute-done.2 = bf16[32,1024]{1,0:T(8,128)(2,1)S(1)} collective-permute-done((bf16[32,1024]{1,0:T(8,128)(2,1)S(1)}, bf16[32,1024]{1,0:T(8,128)(2,1)S(1)}, u32[]{:S(2)}, u32[]{:S(2)}) %collective-permute-start.2) | collective-permute-done | bytes 65568 | tf_op jit(solution)/shard_map/ppermute | solution.py:28
  30.7 0.1 collective-permute-start.3
  30.8 0.9 %convert_dynamic-update-slice_fusion = f32[7680,128]{1,0:T(8,128)} fusion(f32[7680,128]{1,0:T(8,128)} %get-tuple-element.90, bf16[768,128]{1,0:T(8,128)(2,1)S(1)} %collective-permute-done.1, bf16[768,128]{1,0:T(8,128)(2,1)S(1)} %collective-permute-done), kind=kLoop, calls=%fused_computation.1 | loop fusion | flops 786432 | bytes 1179648 | tf_op jit(solution)/shard_map/dynamic_update_slice | solution.py:364
  31.7 2.2 %collective-permute-done.3 = bf16[32,1024]{1,0:T(8,128)(2,1)S(1)} collective-permute-done((bf16[32,1024]{1,0:T(8,128)(2,1)S(1)}, bf16[32,1024]{1,0:T(8,128)(2,1)S(1)}, u32[]{:S(2)}, u32[]{:S(2)}) %collective-permute-start.3) | collective-permute-done | bytes 65568 | tf_op jit(solution)/shard_map/ppermute | solution.py:28
  33.9 0.7 collective-permute-start.4
  34.6 0.0 copy-start
  34.6 2.1 %copy-done = f32[7680,128]{1,0:T(8,128)S(1)} copy-done((f32[7680,128]{1,0:T(8,128)S(1)}, f32[7680,128]{1,0:T(8,128)}, u32[]{:S(2)}) %copy-start) | copy-done | bytes 3932184
  36.7 0.0 copy-start.1
  36.7 4.5 %short_sums.6 = f32[64,128]{1,0:T(8,128)S(1)} custom-call(s32[128,128]{1,0:T(8,128)S(1)} %get-tuple-element.88.index_ref, f32[768,48]{1,0:T(8,128)S(1)} %get-tuple-element.89.weight_ref, f32[7680,1,128]{2,1,0:T(1,128)S(1)} %bitcast.15), custom_call_target="tpu_custom_call" | custom-call | flops 4000000000 | bytes 400000 | tf_op jit(solution)/shard_map/short_sums/pallas_call | solution.py:294
  41.3 0.0 collective-permute-done.4
  41.3 3.1 %collective-permute-start.5 = (bf16[32,1024]{1,0:T(8,128)(2,1)S(1)}, bf16[32,1024]{1,0:T(8,128)(2,1)S(1)}, u32[]{:S(2)}, u32[]{:S(2)}) collective-permute-start(bf16[32,1024]{1,0:T(8,128)(2,1)S(1)} %add_convert_fusion.2), channel_id=1, source_target_pairs={{0,64},{8,72},{16,80},{24,88},{32,96},{40,104},{48,112},{56,120},{... | collective-permute-start | bytes 196616 | tf_op jit(solution)/shard_map/ppermute | solution.py:28
  44.4 0.0 copy-done.1
  44.4 4.5 %short_sums.7 = f32[64,128]{1,0:T(8,128)S(1)} custom-call(s32[128,128]{1,0:T(8,128)S(1)} %get-tuple-element.100.index_ref, f32[768,48]{1,0:T(8,128)S(1)} %get-tuple-element.89.weight_ref, f32[7680,1,128]{2,1,0:T(1,128)S(1)} %bitcast.16), custom_call_target="tpu_custom_call" | custom-call | flops 4000000000 | bytes 400000 | tf_op jit(solution)/shard_map/short_sums/pallas_call | solution.py:294
  48.9 0.0 collective-permute-done.5
  48.9 0.0 copy-start.7
  48.9 0.0 copy-start.8
  48.9 1.3 %collective-permute-start.6 = (bf16[32,1024]{1,0:T(8,128)(2,1)S(1)}, bf16[32,1024]{1,0:T(8,128)(2,1)S(1)}, u32[]{:S(2)}, u32[]{:S(2)}) collective-permute-start(bf16[32,1024]{1,0:T(8,128)(2,1)S(1)} %add_convert_fusion.1), channel_id=1, source_target_pairs={{0,128},{8,136},{16,144},{24,152},{32,160},{40,168},{48,176},{56,1... | collective-permute-start | bytes 196616 | tf_op jit(solution)/shard_map/ppermute | solution.py:28
  50.2 4.5 %short_sums.8 = f32[64,128]{1,0:T(8,128)S(1)} custom-call(s32[128,128]{1,0:T(8,128)S(1)} %get-tuple-element.107.index_ref, f32[768,48]{1,0:T(8,128)S(1)} %get-tuple-element.89.weight_ref, f32[7680,1,128]{2,1,0:T(1,128)S(1)} %bitcast.17), custom_call_target="tpu_custom_call" | custom-call | flops 4000000000 | bytes 400000 | tf_op jit(solution)/shard_map/short_sums/pallas_call | solution.py:294
  54.8 0.0 collective-permute-done.6
  54.8 2.6 %collective-permute-start.7 = (f32[32,1024]{1,0:T(8,128)S(1)}, f32[32,1024]{1,0:T(8,128)S(1)}, u32[]{:S(2)}, u32[]{:S(2)}) collective-permute-start(f32[32,1024]{1,0:T(8,128)S(1)} %convert_add_fusion), channel_id=1, source_target_pairs={{0,8},{8,0},{16,24},{24,16},{32,40},{40,32},{48,56},{56,48},{64,72... | collective-permute-start | bytes 393224 | tf_op jit(solution)/shard_map/ppermute | solution.py:28
  57.4 1.0 %collective-permute-done.7 = f32[32,1024]{1,0:T(8,128)S(1)} collective-permute-done((f32[32,1024]{1,0:T(8,128)S(1)}, f32[32,1024]{1,0:T(8,128)S(1)}, u32[]{:S(2)}, u32[]{:S(2)}) %collective-permute-start.7) | collective-permute-done | bytes 131104 | tf_op jit(solution)/shard_map/ppermute | solution.py:28
  58.4 0.0 copy-done.7
  58.4 0.0 copy-done.8
  58.4 0.7 multiply_convert_fusion.1
  59.1 6.1 %long_parts.1 = bf16[8,64,768]{2,1,0:T(8,128)(2,1)} custom-call(bf16[64,1024]{1,0:T(8,128)(2,1)S(1)} %pad_maximum_fusion.p_ref, bf16[1024,6144]{1,0:T(8,128)(2,1)} %get-tuple-element.113.table_ref), custom_call_target="tpu_custom_call" | custom-call | flops 800000000 | bytes 14000000 | tf_op jit(solution)/shard_map/long_parts/pallas_call | solution.py:166
  65.2 6.4 %all-to-all-start = ((bf16[8,64,768]{2,1,0:T(8,128)(2,1)}), bf16[8,64,768]{2,1,0:T(8,128)(2,1)S(1)}, u32[]{:S(2)}, u32[]{:S(2)}) async-start(bf16[8,64,768]{2,1,0:T(8,128)(2,1)} %long_parts.1), calls=%async_computation | async-start | bytes 1572864 | tf_op jit(solution)/shard_map/all_to_all | solution.py:390
  71.6 0.0 copy-start.2
  71.7 2.1 %copy-done.2 = f32[7680,128]{1,0:T(8,128)S(1)} copy-done((f32[7680,128]{1,0:T(8,128)S(1)}, f32[7680,128]{1,0:T(8,128)}, u32[]{:S(2)}) %copy-start.2) | copy-done | bytes 3932184
  73.8 4.5 %short_sums.11 = f32[64,128]{1,0:T(8,128)S(1)} custom-call(s32[128,128]{1,0:T(8,128)S(1)} %get-tuple-element.123.index_ref, f32[768,48]{1,0:T(8,128)S(1)} %get-tuple-element.89.weight_ref, f32[7680,1,128]{2,1,0:T(1,128)S(1)} %bitcast.18), custom_call_target="tpu_custom_call" | custom-call | flops 100000000 | bytes 400000 | tf_op jit(solution)/shard_map/short_sums/pallas_call | solution.py:294
  78.3 4.5 %short_sums.10 = f32[64,128]{1,0:T(8,128)S(1)} custom-call(s32[128,128]{1,0:T(8,128)S(1)} %get-tuple-element.122.index_ref, f32[768,48]{1,0:T(8,128)S(1)} %get-tuple-element.89.weight_ref, f32[7680,1,128]{2,1,0:T(1,128)S(1)} %bitcast.19), custom_call_target="tpu_custom_call" | custom-call | flops 100000000 | bytes 400000 | tf_op jit(solution)/shard_map/short_sums/pallas_call | solution.py:294
  82.8 4.5 %short_sums.9 = f32[64,128]{1,0:T(8,128)S(1)} custom-call(s32[128,128]{1,0:T(8,128)S(1)} %get-tuple-element.121.index_ref, f32[768,48]{1,0:T(8,128)S(1)} %get-tuple-element.89.weight_ref, f32[7680,1,128]{2,1,0:T(1,128)S(1)} %bitcast.20), custom_call_target="tpu_custom_call" | custom-call | flops 100000000 | bytes 400000 | tf_op jit(solution)/shard_map/short_sums/pallas_call | solution.py:294
  87.4 0.0 all-to-all-done
  87.4 0.1 convert_reduce_fusion
  87.5 0.7 add_convert_fusion
  (17 shorter events, 0.2 us)
Async XLA Ops:
  0.6 10.3 %copy-start.3 = (bf16[64,6144]{1,0:T(8,128)(2,1)S(1)}, bf16[64,6144]{1,0:T(8,128)(2,1)}, u32[]{:S(2)}) copy-start(bf16[64,6144]{1,0:T(8,128)(2,1)} %grad_ref.3) | copy-start | bytes 2359300
  0.6 10.3 %copy-start.4 = (f32[3,6144]{1,0:T(4,128)S(1)}, f32[3,6144]{1,0:T(4,128)}, u32[]{:S(2)}) copy-start(f32[3,6144]{1,0:T(4,128)} %frac_ref) | copy-start | bytes 221188
  0.7 0.8 copy-start.5
  1.5 9.1 %copy-start.9 = (s32[3,512]{1,0:T(4,128)S(1)}, s32[3,512]{1,0:T(4,128)}, u32[]{:S(2)}) copy-start(s32[3,512]{1,0:T(4,128)} %param.13) | copy-start | bytes 18436
  1.5 9.5 %copy-start.6 = (bf16[64,64]{1,0:T(8,128)(2,1)S(1)}, bf16[64,64]{1,0:T(8,128)(2,1)}, u32[]{:S(2)}) copy-start(bf16[64,64]{1,0:T(8,128)(2,1)} %mix_ref.3) | copy-start | bytes 24580
  7.2 18.0 %collective-permute-start = (bf16[768,128]{1,0:T(8,128)(2,1)S(1)}, bf16[768,128]{1,0:T(8,128)(2,1)S(1)}, u32[]{:S(2)}, u32[]{:S(2)}) collective-permute-start(bf16[768,128]{1,0:T(8,128)(2,1)S(1)} %get-tuple-element.127), channel_id=1, source_target_pairs={{248,0},{0,8},{8,16},{16,24},{24,32},{32,40},{40,48},{48,56},{56,6... | collective-permute-start | bytes 589832 | tf_op jit(solution)/shard_map/ppermute | solution.py:34
  10.3 14.9 %collective-permute-start.1 = (bf16[768,128]{1,0:T(8,128)(2,1)S(1)}, bf16[768,128]{1,0:T(8,128)(2,1)S(1)}, u32[]{:S(2)}, u32[]{:S(2)}) collective-permute-start(bf16[768,128]{1,0:T(8,128)(2,1)S(1)} %get-tuple-element.126), channel_id=1, source_target_pairs={{8,0},{16,8},{24,16},{32,24},{40,32},{48,40},{56,48},{64,56},{72,6... | collective-permute-start | bytes 589832 | tf_op jit(solution)/shard_map/ppermute | solution.py:34
  25.2 5.5 %collective-permute-start.2 = (bf16[32,1024]{1,0:T(8,128)(2,1)S(1)}, bf16[32,1024]{1,0:T(8,128)(2,1)S(1)}, u32[]{:S(2)}, u32[]{:S(2)}) collective-permute-start(bf16[32,1024]{1,0:T(8,128)(2,1)S(1)} %dynamic-slice_convert_fusion), channel_id=1, source_target_pairs={{0,8},{8,0},{16,24},{24,16},{32,40},{40,32},{48,56},{56,48},{64,72... | collective-permute-start | bytes 196616 | tf_op jit(solution)/shard_map/ppermute | solution.py:28
  30.7 3.2 %collective-permute-start.3 = (bf16[32,1024]{1,0:T(8,128)(2,1)S(1)}, bf16[32,1024]{1,0:T(8,128)(2,1)S(1)}, u32[]{:S(2)}, u32[]{:S(2)}) collective-permute-start(bf16[32,1024]{1,0:T(8,128)(2,1)S(1)} %add_convert_fusion.4), channel_id=1, source_target_pairs={{0,16},{8,24},{16,0},{24,8},{32,48},{40,56},{48,32},{56,40},{64,80... | collective-permute-start | bytes 196616 | tf_op jit(solution)/shard_map/ppermute | solution.py:28
  33.9 7.3 %collective-permute-start.4 = (bf16[32,1024]{1,0:T(8,128)(2,1)S(1)}, bf16[32,1024]{1,0:T(8,128)(2,1)S(1)}, u32[]{:S(2)}, u32[]{:S(2)}) collective-permute-start(bf16[32,1024]{1,0:T(8,128)(2,1)S(1)} %add_convert_fusion.3), channel_id=1, source_target_pairs={{0,32},{8,40},{16,48},{24,56},{32,0},{40,8},{48,16},{56,24},{64,96... | collective-permute-start | bytes 196616 | tf_op jit(solution)/shard_map/ppermute | solution.py:28
  34.6 2.1 %copy-start = (f32[7680,128]{1,0:T(8,128)S(1)}, f32[7680,128]{1,0:T(8,128)}, u32[]{:S(2)}) copy-start(f32[7680,128]{1,0:T(8,128)} %convert_dynamic-update-slice_fusion) | copy-start | bytes 11796484
  36.7 7.6 %copy-start.1 = (f32[7680,128]{1,0:T(8,128)S(1)}, f32[7680,128]{1,0:T(8,128)}, u32[]{:S(2)}) copy-start(f32[7680,128]{1,0:T(8,128)} %convert_dynamic-update-slice_fusion) | copy-start | bytes 11796484
  41.3 7.6 %collective-permute-start.5 = (bf16[32,1024]{1,0:T(8,128)(2,1)S(1)}, bf16[32,1024]{1,0:T(8,128)(2,1)S(1)}, u32[]{:S(2)}, u32[]{:S(2)}) collective-permute-start(bf16[32,1024]{1,0:T(8,128)(2,1)S(1)} %add_convert_fusion.2), channel_id=1, source_target_pairs={{0,64},{8,72},{16,80},{24,88},{32,96},{40,104},{48,112},{56,120},{... | collective-permute-start | bytes 196616 | tf_op jit(solution)/shard_map/ppermute | solution.py:28
  48.9 9.5 %copy-start.7 = (f32[2,64,512]{2,1,0:T(8,128)S(1)}, f32[2,64,512]{2,1,0:T(8,128)}, u32[]{:S(2)}) copy-start(f32[2,64,512]{2,1,0:T(8,128)} %param.15) | copy-start | bytes 786436
  48.9 9.5 %copy-start.8 = (f32[64,512]{1,0:T(8,128)S(1)}, f32[64,512]{1,0:T(8,128)}, u32[]{:S(2)}) copy-start(f32[64,512]{1,0:T(8,128)} %param.14) | copy-start | bytes 393220
  48.9 5.8 %collective-permute-start.6 = (bf16[32,1024]{1,0:T(8,128)(2,1)S(1)}, bf16[32,1024]{1,0:T(8,128)(2,1)S(1)}, u32[]{:S(2)}, u32[]{:S(2)}) collective-permute-start(bf16[32,1024]{1,0:T(8,128)(2,1)S(1)} %add_convert_fusion.1), channel_id=1, source_target_pairs={{0,128},{8,136},{16,144},{24,152},{32,160},{40,168},{48,176},{56,1... | collective-permute-start | bytes 196616 | tf_op jit(solution)/shard_map/ppermute | solution.py:28
  54.8 3.6 %collective-permute-start.7 = (f32[32,1024]{1,0:T(8,128)S(1)}, f32[32,1024]{1,0:T(8,128)S(1)}, u32[]{:S(2)}, u32[]{:S(2)}) collective-permute-start(f32[32,1024]{1,0:T(8,128)S(1)} %convert_add_fusion), channel_id=1, source_target_pairs={{0,8},{8,0},{16,24},{24,16},{32,40},{40,32},{48,56},{56,48},{64,72... | collective-permute-start | bytes 393224 | tf_op jit(solution)/shard_map/ppermute | solution.py:28
  65.2 22.1 %all-to-all-start = ((bf16[8,64,768]{2,1,0:T(8,128)(2,1)}), bf16[8,64,768]{2,1,0:T(8,128)(2,1)S(1)}, u32[]{:S(2)}, u32[]{:S(2)}) async-start(bf16[8,64,768]{2,1,0:T(8,128)(2,1)} %long_parts.1), calls=%async_computation | async-start | bytes 1572864 | tf_op jit(solution)/shard_map/all_to_all | solution.py:390
  71.6 2.1 %copy-start.2 = (f32[7680,128]{1,0:T(8,128)S(1)}, f32[7680,128]{1,0:T(8,128)}, u32[]{:S(2)}) copy-start(f32[7680,128]{1,0:T(8,128)} %convert_dynamic-update-slice_fusion) | copy-start | bytes 11796484

commit v7 on v6

--- a/solution.py
+++ b/solution.py
@@ -20,7 +20,7 @@
     return [float(c) for c in fitted.convert(kind=np.polynomial.Polynomial).coef]
 
 
-SIN_HALF = even_fit(lambda r: math.sqrt(2) * np.sin(np.pi * r) / r, 4)
+SIN_HALF = even_fit(lambda r: math.sqrt(2) * np.sin(np.pi * r) / r, 3)
 COS_HALF = even_fit(lambda r: math.sqrt(2) * np.cos(np.pi * r), 4)
 
 
@@ -309,6 +309,22 @@
     )(index, weight, rows)
 
 
+def near_kernel(index_ref, rows_ref, out_ref):
+    out_ref[...] = index_ref[...]
+
+
+def near(index, rows):
+    return pl.pallas_call(
+        near_kernel,
+        in_specs=[pl.BlockSpec(memory_space=pltpu.VMEM)] * 2,
+        out_specs=pl.BlockSpec(memory_space=pltpu.VMEM),
+        out_shape=jax.ShapeDtypeStruct(index.shape, index.dtype),
+        compiler_params=pltpu.CompilerParams(vmem_limit_bytes=6 << 20),
+        cost_estimate=pl.CostEstimate(flops=1_000_000_000, bytes_accessed=400_000, transcendentals=0),
+        name="near",
+    )(index, rows)
+
+
 def local(
     grad_out,
     frac_pos,
@@ -350,6 +366,9 @@
         value, slots = lax.optimization_barrier((value, slots))
         received = swapped(value, "dom", bit)
         start = len(short)
+        if not pieces and bit == 2:
+            slots[0] = near(slots[0], extended)
+            received, slots[0] = lax.optimization_barrier((received, slots[0]))
         for _ in range(pieces):
             short_piece(4_000_000_000)
         received, short[start:] = lax.optimization_barrier((received, short[start:]))

time: 88.4 us -> 86.3 us (0.976)
  waiting for transfers between devices: 4.07 us -> 1.98 us
    ppermute x6, waiting for transfers between devices: 4.06 us -> 1.98 us  [swapped(): lax.ppermute(block, axis, [(i, i ^ bit) for i in range(lax.axis_size(axis...]
  transfers between devices with their start and end apart: 9 -> 9, of which waited for: 3 -> 2; matrix products, arithmetic and copies ran while one was open for 1% -> 1% of each run, Pallas kernels for 47% -> 47%
where the time goes in v7:
time: 86.3 us; the launch traced here: 86 us
  Pallas kernels  52.3 us (61%)
  starting transfers between devices  22.4 us (26%)
  local copies, waits for them, and re-layouts  5.7 us (7%)
  other arithmetic  2.62 us (3%)
  waiting for transfers between devices  1.98 us (2%)
  between operations  1 us (1%)
    pallas_call x6, Pallas kernels, short_sums(): pl.pallas_call(short_kernel, grid=(1,), in_specs=[pl.BlockSpec(memory_spa...  27.1 us
    pallas_call x1, Pallas kernels, front(): pl.pallas_call(functools.partial(front_kernel, rows, tile), grid=(atoms /...  13.5 us
    ppermute x6, starting transfers between devices, swapped(): lax.ppermute(block, axis, [(i, i ^ bit) for i in range(lax.axis_size(axis...  12.6 us
    all_to_all x1, starting transfers between devices, local(): parts = lax.all_to_all(parts, 'ka', 0, 0, tiled=True)  6.37 us
    pallas_call x1, Pallas kernels, long_parts(): pl.pallas_call(long_kernel, in_specs=[pl.BlockSpec(memory_space=pltpu.VME...  6.11 us
    pallas_call x1, Pallas kernels, prepare(): pl.pallas_call(prepare_kernel, grid_spec=pltpu.PrefetchScalarGridSpec(num...  5.69 us
    unnamed x25, local copies, waits for them, and re-layouts  5.44 us
    ppermute x2, starting transfers between devices, shifted(): return lax.ppermute(block, axis, route)  3.41 us
  transfers between devices with their start and end apart: 9, of which 2 were waited for; matrix products, arithmetic and copies ran while one was open for 1% of the time, Pallas kernels for 47%

profile of v7, /device:TPU:1, one launch (start us, length us, event | category | flops | bytes accessed | tf_op | source)
XLA Modules:
  0.0 86.0 jit_solution(2484141645805223909)
XLA Ops:
  0.6 0.0 copy-start.3
  0.6 0.0 copy-start.4
  0.7 0.0 copy-start.5
  0.7 0.8 copy-done.5
  1.5 0.0 copy-start.9
  1.5 0.0 copy-start.6
  1.5 5.7 %prepare.1 = (f32[7680,128]{1,0:T(8,128)}, bf16[1536,128]{1,0:T(8,128)(2,1)S(1)}, f32[768,48]{1,0:T(8,128)S(1)}, s32[128,128]{1,0:T(8,128)S(1)}, s32[128,128]{1,...) custom-call(s32[1]{0:T(128)} %bitcast.ka_ref, ...), custom_call_target="tpu_custom_call" | custom-call | flops 1000000000 | bytes 8000000 | tf_op jit(solution)/shard_map/prepare/pallas_call | solution.py:223
  7.2 3.1 %collective-permute-start = (bf16[768,128]{1,0:T(8,128)(2,1)S(1)}, bf16[768,128]{1,0:T(8,128)(2,1)S(1)}, u32[]{:S(2)}, u32[]{:S(2)}) collective-permute-start(bf16[768,128]{1,0:T(8,128)(2,1)S(1)} %get-tuple-element.131), channel_id=1, source_target_pairs={{248,0},{0,8},{8,16},{16,24},{24,32},{32,40},{40,48},{48,56},{56,6... | collective-permute-start | bytes 589832 | tf_op jit(solution)/shard_map/ppermute | solution.py:34
  10.3 0.3 collective-permute-start.1
  10.6 0.0 copy-done.9
  10.6 0.1 pad.11.clone
  10.7 0.1 maximum_maximum_fusion
  10.8 0.1 copy.14.k_ref
  10.9 0.0 copy-done.3
  10.9 0.0 copy-done.4
  10.9 0.0 copy-done.6
  10.9 13.5 %structure_sums.1 = (f32[64,1024]{1,0:T(8,128)S(1)}, bf16[1024,6144]{1,0:T(8,128)(2,1)}) custom-call(bf16[64,64]{1,0:T(8,128)(2,1)S(1)} %copy-done.6, bf16[64,6144]{1,0:T(8,128)(2,1)S(1)} %copy-done.3, f32[3,6144]{1,0:T(4,128)S(1)} %copy-done.4, bf16[512,16]{1,0:T(8,128)(2,1)S(1)} %copy.14.k_ref), custom_call_target="tpu_custom_call" | custom-call | flops 20000000000 | bytes 14000000 | tf_op jit(solution)/shard_map/structure_sums/pallas_call | solution.py:118
  24.4 0.0 collective-permute-done
  24.4 0.0 collective-permute-done.1
  24.5 4.6 %collective-permute-start.2 = (bf16[32,1024]{1,0:T(8,128)(2,1)S(1)}, bf16[32,1024]{1,0:T(8,128)(2,1)S(1)}, u32[]{:S(2)}, u32[]{:S(2)}) collective-permute-start(bf16[32,1024]{1,0:T(8,128)(2,1)S(1)} %dynamic-slice_convert_fusion), channel_id=1, source_target_pairs={{0,8},{8,0},{16,24},{24,16},{32,40},{40,32},{48,56},{56,48},{64,72... | collective-permute-start | bytes 196616 | tf_op jit(solution)/shard_map/ppermute | solution.py:28
  29.0 0.9 %convert_dynamic-update-slice_fusion = f32[7680,128]{1,0:T(8,128)} fusion(f32[7680,128]{1,0:T(8,128)} %get-tuple-element.84, bf16[768,128]{1,0:T(8,128)(2,1)S(1)} %collective-permute-done.1, bf16[768,128]{1,0:T(8,128)(2,1)S(1)} %collective-permute-done), kind=kLoop, calls=%fused_computation.1 | loop fusion | flops 786432 | bytes 1179648 | tf_op jit(solution)/shard_map/dynamic_update_slice | solution.py:383
  30.0 0.0 collective-permute-done.2
  30.0 0.1 collective-permute-start.3
  30.1 0.0 copy-start
  30.1 2.1 %copy-done = f32[7680,128]{1,0:T(8,128)S(1)} copy-done((f32[7680,128]{1,0:T(8,128)S(1)}, f32[7680,128]{1,0:T(8,128)}, u32[]{:S(2)}) %copy-start) | copy-done | bytes 3932184
  32.2 0.0 copy-start.1
  32.2 1.0 %collective-permute-done.3 = bf16[32,1024]{1,0:T(8,128)(2,1)S(1)} collective-permute-done((bf16[32,1024]{1,0:T(8,128)(2,1)S(1)}, bf16[32,1024]{1,0:T(8,128)(2,1)S(1)}, u32[]{:S(2)}, u32[]{:S(2)}) %collective-permute-start.3) | collective-permute-done | bytes 65568 | tf_op jit(solution)/shard_map/ppermute | solution.py:28
  33.2 0.7 collective-permute-start.4
  33.9 0.4 copy-done.1
  34.3 4.5 %short_sums.6 = f32[64,128]{1,0:T(8,128)S(1)} custom-call(s32[128,128]{1,0:T(8,128)S(1)} %near.1.index_ref, f32[768,48]{1,0:T(8,128)S(1)} %get-tuple-element.96.weight_ref, f32[7680,1,128]{2,1,0:T(1,128)S(1)} %bitcast.16), custom_call_target="tpu_custom_call" | custom-call | flops 4000000000 | bytes 400000 | tf_op jit(solution)/shard_map/short_sums/pallas_call | solution.py:294
  38.8 0.0 collective-permute-done.4
  38.9 3.6 %collective-permute-start.5 = (bf16[32,1024]{1,0:T(8,128)(2,1)S(1)}, bf16[32,1024]{1,0:T(8,128)(2,1)S(1)}, u32[]{:S(2)}, u32[]{:S(2)}) collective-permute-start(bf16[32,1024]{1,0:T(8,128)(2,1)S(1)} %add_convert_fusion.2), channel_id=1, source_target_pairs={{0,64},{8,72},{16,80},{24,88},{32,96},{40,104},{48,112},{56,120},{... | collective-permute-start | bytes 196616 | tf_op jit(solution)/shard_map/ppermute | solution.py:28
  42.5 4.5 %short_sums.7 = f32[64,128]{1,0:T(8,128)S(1)} custom-call(s32[128,128]{1,0:T(8,128)S(1)} %get-tuple-element.104.index_ref, f32[768,48]{1,0:T(8,128)S(1)} %get-tuple-element.96.weight_ref, f32[7680,1,128]{2,1,0:T(1,128)S(1)} %bitcast.17), custom_call_target="tpu_custom_call" | custom-call | flops 4000000000 | bytes 400000 | tf_op jit(solution)/shard_map/short_sums/pallas_call | solution.py:294
  47.0 0.0 collective-permute-done.5
  47.1 0.0 copy-start.7
  47.1 0.0 copy-start.8
  47.1 1.3 %collective-permute-start.6 = (bf16[32,1024]{1,0:T(8,128)(2,1)S(1)}, bf16[32,1024]{1,0:T(8,128)(2,1)S(1)}, u32[]{:S(2)}, u32[]{:S(2)}) collective-permute-start(bf16[32,1024]{1,0:T(8,128)(2,1)S(1)} %add_convert_fusion.1), channel_id=1, source_target_pairs={{0,128},{8,136},{16,144},{24,152},{32,160},{40,168},{48,176},{56,1... | collective-permute-start | bytes 196616 | tf_op jit(solution)/shard_map/ppermute | solution.py:28
  48.4 4.5 %short_sums.8 = f32[64,128]{1,0:T(8,128)S(1)} custom-call(s32[128,128]{1,0:T(8,128)S(1)} %get-tuple-element.111.index_ref, f32[768,48]{1,0:T(8,128)S(1)} %get-tuple-element.96.weight_ref, f32[7680,1,128]{2,1,0:T(1,128)S(1)} %bitcast.18), custom_call_target="tpu_custom_call" | custom-call | flops 4000000000 | bytes 400000 | tf_op jit(solution)/shard_map/short_sums/pallas_call | solution.py:294
  52.9 0.0 collective-permute-done.6
  53.0 2.3 %collective-permute-start.7 = (f32[32,1024]{1,0:T(8,128)S(1)}, f32[32,1024]{1,0:T(8,128)S(1)}, u32[]{:S(2)}, u32[]{:S(2)}) collective-permute-start(f32[32,1024]{1,0:T(8,128)S(1)} %convert_add_fusion), channel_id=1, source_target_pairs={{0,8},{8,0},{16,24},{24,16},{32,40},{40,32},{48,56},{56,48},{64,72... | collective-permute-start | bytes 393224 | tf_op jit(solution)/shard_map/ppermute | solution.py:28
  55.2 1.0 %collective-permute-done.7 = f32[32,1024]{1,0:T(8,128)S(1)} collective-permute-done((f32[32,1024]{1,0:T(8,128)S(1)}, f32[32,1024]{1,0:T(8,128)S(1)}, u32[]{:S(2)}, u32[]{:S(2)}) %collective-permute-start.7) | collective-permute-done | bytes 131104 | tf_op jit(solution)/shard_map/ppermute | solution.py:28
  56.2 0.0 copy-done.7
  56.2 0.0 copy-done.8
  56.2 0.7 multiply_convert_fusion.1
  57.0 6.1 %long_parts.1 = bf16[8,64,768]{2,1,0:T(8,128)(2,1)} custom-call(bf16[64,1024]{1,0:T(8,128)(2,1)S(1)} %pad_maximum_fusion.p_ref, bf16[1024,6144]{1,0:T(8,128)(2,1)} %get-tuple-element.117.table_ref), custom_call_target="tpu_custom_call" | custom-call | flops 800000000 | bytes 14000000 | tf_op jit(solution)/shard_map/long_parts/pallas_call | solution.py:166
  63.1 6.4 %all-to-all-start = ((bf16[8,64,768]{2,1,0:T(8,128)(2,1)}), bf16[8,64,768]{2,1,0:T(8,128)(2,1)S(1)}, u32[]{:S(2)}, u32[]{:S(2)}) async-start(bf16[8,64,768]{2,1,0:T(8,128)(2,1)} %long_parts.1), calls=%async_computation | async-start | bytes 1572864 | tf_op jit(solution)/shard_map/all_to_all | solution.py:409
  69.5 0.0 copy-start.2
  69.5 2.1 %copy-done.2 = f32[7680,128]{1,0:T(8,128)S(1)} copy-done((f32[7680,128]{1,0:T(8,128)S(1)}, f32[7680,128]{1,0:T(8,128)}, u32[]{:S(2)}) %copy-start.2) | copy-done | bytes 3932184
  71.6 4.5 %short_sums.11 = f32[64,128]{1,0:T(8,128)S(1)} custom-call(s32[128,128]{1,0:T(8,128)S(1)} %get-tuple-element.127.index_ref, f32[768,48]{1,0:T(8,128)S(1)} %get-tuple-element.96.weight_ref, f32[7680,1,128]{2,1,0:T(1,128)S(1)} %bitcast.19), custom_call_target="tpu_custom_call" | custom-call | flops 100000000 | bytes 400000 | tf_op jit(solution)/shard_map/short_sums/pallas_call | solution.py:294
  76.1 4.5 %short_sums.10 = f32[64,128]{1,0:T(8,128)S(1)} custom-call(s32[128,128]{1,0:T(8,128)S(1)} %get-tuple-element.126.index_ref, f32[768,48]{1,0:T(8,128)S(1)} %get-tuple-element.96.weight_ref, f32[7680,1,128]{2,1,0:T(1,128)S(1)} %bitcast.20), custom_call_target="tpu_custom_call" | custom-call | flops 100000000 | bytes 400000 | tf_op jit(solution)/shard_map/short_sums/pallas_call | solution.py:294
  80.6 4.5 %short_sums.9 = f32[64,128]{1,0:T(8,128)S(1)} custom-call(s32[128,128]{1,0:T(8,128)S(1)} %get-tuple-element.125.index_ref, f32[768,48]{1,0:T(8,128)S(1)} %get-tuple-element.96.weight_ref, f32[7680,1,128]{2,1,0:T(1,128)S(1)} %bitcast.21), custom_call_target="tpu_custom_call" | custom-call | flops 100000000 | bytes 400000 | tf_op jit(solution)/shard_map/short_sums/pallas_call | solution.py:294
  85.2 0.0 all-to-all-done
  85.2 0.1 convert_reduce_fusion
  85.3 0.7 add_convert_fusion
  (18 shorter events, 0.2 us)
Async XLA Ops:
  0.6 10.3 %copy-start.3 = (bf16[64,6144]{1,0:T(8,128)(2,1)S(1)}, bf16[64,6144]{1,0:T(8,128)(2,1)}, u32[]{:S(2)}) copy-start(bf16[64,6144]{1,0:T(8,128)(2,1)} %grad_ref.3) | copy-start | bytes 2359300
  0.6 10.3 %copy-start.4 = (f32[3,6144]{1,0:T(4,128)S(1)}, f32[3,6144]{1,0:T(4,128)}, u32[]{:S(2)}) copy-start(f32[3,6144]{1,0:T(4,128)} %frac_ref) | copy-start | bytes 221188
  0.7 0.8 copy-start.5
  1.5 9.1 %copy-start.9 = (s32[3,512]{1,0:T(4,128)S(1)}, s32[3,512]{1,0:T(4,128)}, u32[]{:S(2)}) copy-start(s32[3,512]{1,0:T(4,128)} %param.13) | copy-start | bytes 18436
  1.5 9.5 %copy-start.6 = (bf16[64,64]{1,0:T(8,128)(2,1)S(1)}, bf16[64,64]{1,0:T(8,128)(2,1)}, u32[]{:S(2)}) copy-start(bf16[64,64]{1,0:T(8,128)(2,1)} %mix_ref.3) | copy-start | bytes 24580
  7.2 17.2 %collective-permute-start = (bf16[768,128]{1,0:T(8,128)(2,1)S(1)}, bf16[768,128]{1,0:T(8,128)(2,1)S(1)}, u32[]{:S(2)}, u32[]{:S(2)}) collective-permute-start(bf16[768,128]{1,0:T(8,128)(2,1)S(1)} %get-tuple-element.131), channel_id=1, source_target_pairs={{248,0},{0,8},{8,16},{16,24},{24,32},{32,40},{40,48},{48,56},{56,6... | collective-permute-start | bytes 589832 | tf_op jit(solution)/shard_map/ppermute | solution.py:34
  10.3 14.1 %collective-permute-start.1 = (bf16[768,128]{1,0:T(8,128)(2,1)S(1)}, bf16[768,128]{1,0:T(8,128)(2,1)S(1)}, u32[]{:S(2)}, u32[]{:S(2)}) collective-permute-start(bf16[768,128]{1,0:T(8,128)(2,1)S(1)} %get-tuple-element.130), channel_id=1, source_target_pairs={{8,0},{16,8},{24,16},{32,24},{40,32},{48,40},{56,48},{64,56},{72,6... | collective-permute-start | bytes 589832 | tf_op jit(solution)/shard_map/ppermute | solution.py:34
  24.5 5.5 %collective-permute-start.2 = (bf16[32,1024]{1,0:T(8,128)(2,1)S(1)}, bf16[32,1024]{1,0:T(8,128)(2,1)S(1)}, u32[]{:S(2)}, u32[]{:S(2)}) collective-permute-start(bf16[32,1024]{1,0:T(8,128)(2,1)S(1)} %dynamic-slice_convert_fusion), channel_id=1, source_target_pairs={{0,8},{8,0},{16,24},{24,16},{32,40},{40,32},{48,56},{56,48},{64,72... | collective-permute-start | bytes 196616 | tf_op jit(solution)/shard_map/ppermute | solution.py:28
  30.0 3.2 %collective-permute-start.3 = (bf16[32,1024]{1,0:T(8,128)(2,1)S(1)}, bf16[32,1024]{1,0:T(8,128)(2,1)S(1)}, u32[]{:S(2)}, u32[]{:S(2)}) collective-permute-start(bf16[32,1024]{1,0:T(8,128)(2,1)S(1)} %add_convert_fusion.4), channel_id=1, source_target_pairs={{0,16},{8,24},{16,0},{24,8},{32,48},{40,56},{48,32},{56,40},{64,80... | collective-permute-start | bytes 196616 | tf_op jit(solution)/shard_map/ppermute | solution.py:28
  30.1 2.1 %copy-start = (f32[7680,128]{1,0:T(8,128)S(1)}, f32[7680,128]{1,0:T(8,128)}, u32[]{:S(2)}) copy-start(f32[7680,128]{1,0:T(8,128)} %convert_dynamic-update-slice_fusion) | copy-start | bytes 11796484
  32.2 2.1 %copy-start.1 = (f32[7680,128]{1,0:T(8,128)S(1)}, f32[7680,128]{1,0:T(8,128)}, u32[]{:S(2)}) copy-start(f32[7680,128]{1,0:T(8,128)} %convert_dynamic-update-slice_fusion) | copy-start | bytes 11796484
  33.2 5.6 %collective-permute-start.4 = (bf16[32,1024]{1,0:T(8,128)(2,1)S(1)}, bf16[32,1024]{1,0:T(8,128)(2,1)S(1)}, u32[]{:S(2)}, u32[]{:S(2)}) collective-permute-start(bf16[32,1024]{1,0:T(8,128)(2,1)S(1)} %add_convert_fusion.3), channel_id=1, source_target_pairs={{0,32},{8,40},{16,48},{24,56},{32,0},{40,8},{48,16},{56,24},{64,96... | collective-permute-start | bytes 196616 | tf_op jit(solution)/shard_map/ppermute | solution.py:28
  38.9 8.2 %collective-permute-start.5 = (bf16[32,1024]{1,0:T(8,128)(2,1)S(1)}, bf16[32,1024]{1,0:T(8,128)(2,1)S(1)}, u32[]{:S(2)}, u32[]{:S(2)}) collective-permute-start(bf16[32,1024]{1,0:T(8,128)(2,1)S(1)} %add_convert_fusion.2), channel_id=1, source_target_pairs={{0,64},{8,72},{16,80},{24,88},{32,96},{40,104},{48,112},{56,120},{... | collective-permute-start | bytes 196616 | tf_op jit(solution)/shard_map/ppermute | solution.py:28
  47.1 9.1 %copy-start.7 = (f32[2,64,512]{2,1,0:T(8,128)S(1)}, f32[2,64,512]{2,1,0:T(8,128)}, u32[]{:S(2)}) copy-start(f32[2,64,512]{2,1,0:T(8,128)} %param.15) | copy-start | bytes 786436
  47.1 9.1 %copy-start.8 = (f32[64,512]{1,0:T(8,128)S(1)}, f32[64,512]{1,0:T(8,128)}, u32[]{:S(2)}) copy-start(f32[64,512]{1,0:T(8,128)} %param.14) | copy-start | bytes 393220
  47.1 5.8 %collective-permute-start.6 = (bf16[32,1024]{1,0:T(8,128)(2,1)S(1)}, bf16[32,1024]{1,0:T(8,128)(2,1)S(1)}, u32[]{:S(2)}, u32[]{:S(2)}) collective-permute-start(bf16[32,1024]{1,0:T(8,128)(2,1)S(1)} %add_convert_fusion.1), channel_id=1, source_target_pairs={{0,128},{8,136},{16,144},{24,152},{32,160},{40,168},{48,176},{56,1... | collective-permute-start | bytes 196616 | tf_op jit(solution)/shard_map/ppermute | solution.py:28
  53.0 3.2 %collective-permute-start.7 = (f32[32,1024]{1,0:T(8,128)S(1)}, f32[32,1024]{1,0:T(8,128)S(1)}, u32[]{:S(2)}, u32[]{:S(2)}) collective-permute-start(f32[32,1024]{1,0:T(8,128)S(1)} %convert_add_fusion), channel_id=1, source_target_pairs={{0,8},{8,0},{16,24},{24,16},{32,40},{40,32},{48,56},{56,48},{64,72... | collective-permute-start | bytes 393224 | tf_op jit(solution)/shard_map/ppermute | solution.py:28
  63.1 22.1 %all-to-all-start = ((bf16[8,64,768]{2,1,0:T(8,128)(2,1)}), bf16[8,64,768]{2,1,0:T(8,128)(2,1)S(1)}, u32[]{:S(2)}, u32[]{:S(2)}) async-start(bf16[8,64,768]{2,1,0:T(8,128)(2,1)} %long_parts.1), calls=%async_computation | async-start | bytes 1572864 | tf_op jit(solution)/shard_map/all_to_all | solution.py:409
  69.5 2.1 %copy-start.2 = (f32[7680,128]{1,0:T(8,128)S(1)}, f32[7680,128]{1,0:T(8,128)}, u32[]{:S(2)}) copy-start(f32[7680,128]{1,0:T(8,128)} %convert_dynamic-update-slice_fusion) | copy-start | bytes 11796484

commit v8 on v6

--- a/solution.py
+++ b/solution.py
@@ -20,7 +20,7 @@
     return [float(c) for c in fitted.convert(kind=np.polynomial.Polynomial).coef]
 
 
-SIN_HALF = even_fit(lambda r: math.sqrt(2) * np.sin(np.pi * r) / r, 4)
+SIN_HALF = even_fit(lambda r: math.sqrt(2) * np.sin(np.pi * r) / r, 3)
 COS_HALF = even_fit(lambda r: math.sqrt(2) * np.cos(np.pi * r), 4)
 
 
@@ -345,15 +345,15 @@
         piece = len(short)
         short.append(short_sums(piece, channels, slots[piece], masked, extended, flops))
 
-    def beside(value, bit, pieces):
+    def beside(value, flips, pieces):
         nonlocal slots
         value, slots = lax.optimization_barrier((value, slots))
-        received = swapped(value, "dom", bit)
+        received = [swapped(value, "dom", flip) for flip in flips]
         start = len(short)
         for _ in range(pieces):
             short_piece(4_000_000_000)
         received, short[start:] = lax.optimization_barrier((received, short[start:]))
-        return received.astype(F32)
+        return [r.astype(F32) for r in received]
 
     k_rows = k_index.astype(BF16).T
     k_triple = jnp.concatenate([k_rows, k_rows, k_rows, jnp.zeros((k_count, 7), BF16)], axis=1)
@@ -368,13 +368,18 @@
     core = lax.axis_index("dom") % 2
     mine = lax.dynamic_slice_in_dim(q, core * half, half, 0)
     other = lax.dynamic_slice_in_dim(q, (1 - core) * half, half, 0)
-    total = mine + beside(other.astype(BF16), 1, 0)
+    total = mine + beside(other.astype(BF16), [1], 0)[0]
     bit = 2
     while bit < dom_size:
         rounded = total.astype(BF16)
-        total = rounded.astype(F32) + beside(rounded, bit, 0 if bit == 2 else 1)
-        bit *= 2
-    partner = beside(total, 1, 0)
+        total = rounded.astype(F32)
+        if 2 * bit < dom_size:
+            first, second, third = beside(rounded, [bit, 2 * bit, 3 * bit], 1 if bit == 2 else 2)
+            total = (total + first) + (second + third)
+        else:
+            total = total + beside(rounded, [bit], 1)[0]
+        bit *= 4
+    partner = beside(total, [1], 0)[0]
     q = jnp.where(
         core == 0,
         jnp.concatenate([total, partner], axis=0),

time: 88.4 us -> 89.4 us (1.011)
  starting transfers between devices: 22.1 us -> 26.9 us
  waiting for transfers between devices: 4.07 us -> 1.01 us
    ppermute x6 -> x8, starting transfers between devices: 12.3 us -> 17.1 us  [swapped(): lax.ppermute(block, axis, [(i, i ^ bit) for i in range(lax.axis_size(axis...]
    ppermute x6 -> x8, waiting for transfers between devices: 4.06 us -> 1 us  [swapped(): lax.ppermute(block, axis, [(i, i ^ bit) for i in range(lax.axis_size(axis...]
  transfers between devices with their start and end apart: 9 -> 11, of which waited for: 3 -> 1; matrix products, arithmetic and copies ran while one was open for 1% -> 1% of each run, Pallas kernels for 47% -> 45%
where the time goes in v8:
time: 89.4 us; the launch traced here: 89.2 us
  Pallas kernels  52.3 us (59%)
  starting transfers between devices  26.9 us (30%)
  local copies, waits for them, and re-layouts  5.31 us (6%)
  other arithmetic  2.63 us (3%)
  waiting for transfers between devices  1.01 us (1%)
  between operations  1.01 us (1%)
    pallas_call x6, Pallas kernels, short_sums(): pl.pallas_call(short_kernel, grid=(1,), in_specs=[pl.BlockSpec(memory_spa...  27.1 us
    ppermute x8, starting transfers between devices, swapped(): lax.ppermute(block, axis, [(i, i ^ bit) for i in range(lax.axis_size(axis...  17.1 us
    pallas_call x1, Pallas kernels, front(): pl.pallas_call(functools.partial(front_kernel, rows, tile), grid=(atoms /...  13.5 us
    all_to_all x1, starting transfers between devices, local(): parts = lax.all_to_all(parts, 'ka', 0, 0, tiled=True)  6.37 us
    pallas_call x1, Pallas kernels, long_parts(): pl.pallas_call(long_kernel, in_specs=[pl.BlockSpec(memory_space=pltpu.VME...  6.1 us
    pallas_call x1, Pallas kernels, prepare(): pl.pallas_call(prepare_kernel, grid_spec=pltpu.PrefetchScalarGridSpec(num...  5.69 us
    unnamed x25, local copies, waits for them, and re-layouts  5.06 us
    ppermute x2, starting transfers between devices, shifted(): return lax.ppermute(block, axis, route)  3.41 us
  transfers between devices with their start and end apart: 11, of which 1 were waited for; matrix products, arithmetic and copies ran while one was open for 1% of the time, Pallas kernels for 45%

profile of v8, /device:TPU:1, one launch (start us, length us, event | category | flops | bytes accessed | tf_op | source)
XLA Modules:
  0.0 89.2 jit_solution(14527866480645732771)
XLA Ops:
  0.6 0.0 copy-start.3
  0.6 0.0 copy-start.4
  0.7 0.0 copy-start.5
  0.7 0.8 copy-done.5
  1.5 0.0 copy-start.9
  1.5 0.0 copy-start.6
  1.5 5.7 %prepare.1 = (f32[7680,128]{1,0:T(8,128)}, bf16[1536,128]{1,0:T(8,128)(2,1)S(1)}, f32[768,48]{1,0:T(8,128)S(1)}, s32[128,128]{1,0:T(8,128)S(1)}, s32[128,128]{1,...) custom-call(s32[1]{0:T(128)} %bitcast.ka_ref, ...), custom_call_target="tpu_custom_call" | custom-call | flops 1000000000 | bytes 8000000 | tf_op jit(solution)/shard_map/prepare/pallas_call | solution.py:223
  7.2 3.1 %collective-permute-start = (bf16[768,128]{1,0:T(8,128)(2,1)S(1)}, bf16[768,128]{1,0:T(8,128)(2,1)S(1)}, u32[]{:S(2)}, u32[]{:S(2)}) collective-permute-start(bf16[768,128]{1,0:T(8,128)(2,1)S(1)} %get-tuple-element.109), channel_id=1, source_target_pairs={{248,0},{0,8},{8,16},{16,24},{24,32},{32,40},{40,48},{48,56},{56,6... | collective-permute-start | bytes 589832 | tf_op jit(solution)/shard_map/ppermute | solution.py:34
  10.3 0.3 collective-permute-start.1
  10.6 0.0 copy-done.9
  10.6 0.1 pad.11.clone
  10.7 0.1 maximum_maximum_fusion
  10.8 0.1 copy.14.k_ref
  10.9 0.0 copy-done.3
  10.9 0.0 copy-done.4
  10.9 0.0 copy-done.6
  10.9 13.5 %structure_sums.1 = (f32[64,1024]{1,0:T(8,128)S(1)}, bf16[1024,6144]{1,0:T(8,128)(2,1)}) custom-call(bf16[64,64]{1,0:T(8,128)(2,1)S(1)} %copy-done.6, bf16[64,6144]{1,0:T(8,128)(2,1)S(1)} %copy-done.3, f32[3,6144]{1,0:T(4,128)S(1)} %copy-done.4, bf16[512,16]{1,0:T(8,128)(2,1)S(1)} %copy.14.k_ref), custom_call_target="tpu_custom_call" | custom-call | flops 20000000000 | bytes 14000000 | tf_op jit(solution)/shard_map/structure_sums/pallas_call | solution.py:118
  24.4 0.0 collective-permute-done
  24.4 0.0 collective-permute-done.1
  24.5 4.6 %collective-permute-start.2 = (bf16[32,1024]{1,0:T(8,128)(2,1)S(1)}, bf16[32,1024]{1,0:T(8,128)(2,1)S(1)}, u32[]{:S(2)}, u32[]{:S(2)}) collective-permute-start(bf16[32,1024]{1,0:T(8,128)(2,1)S(1)} %dynamic-slice_convert_fusion), channel_id=1, source_target_pairs={{0,8},{8,0},{16,24},{24,16},{32,40},{40,32},{48,56},{56,48},{64,72... | collective-permute-start | bytes 196616 | tf_op jit(solution)/shard_map/ppermute | solution.py:28
  29.0 0.9 %convert_dynamic-update-slice_fusion = f32[7680,128]{1,0:T(8,128)} fusion(f32[7680,128]{1,0:T(8,128)} %get-tuple-element.74, bf16[768,128]{1,0:T(8,128)(2,1)S(1)} %collective-permute-done.1, bf16[768,128]{1,0:T(8,128)(2,1)S(1)} %collective-permute-done), kind=kLoop, calls=%fused_computation.1 | loop fusion | flops 786432 | bytes 1179648 | tf_op jit(solution)/shard_map/dynamic_update_slice | solution.py:364
  30.0 0.0 collective-permute-done.2
  30.0 0.1 collective-permute-start.3
  30.1 1.4 %collective-permute-start.4 = (bf16[32,1024]{1,0:T(8,128)(2,1)S(1)}, bf16[32,1024]{1,0:T(8,128)(2,1)S(1)}, u32[]{:S(2)}, u32[]{:S(2)}) collective-permute-start(bf16[32,1024]{1,0:T(8,128)(2,1)S(1)} %add_convert_fusion.2), channel_id=1, source_target_pairs={{0,32},{8,40},{16,48},{24,56},{32,0},{40,8},{48,16},{56,24},{64,96... | collective-permute-start | bytes 196616 | tf_op jit(solution)/shard_map/ppermute | solution.py:28
  31.5 2.2 %collective-permute-start.5 = (bf16[32,1024]{1,0:T(8,128)(2,1)S(1)}, bf16[32,1024]{1,0:T(8,128)(2,1)S(1)}, u32[]{:S(2)}, u32[]{:S(2)}) collective-permute-start(bf16[32,1024]{1,0:T(8,128)(2,1)S(1)} %add_convert_fusion.2), channel_id=1, source_target_pairs={{0,48},{8,56},{16,32},{24,40},{32,16},{40,24},{48,0},{56,8},{64,11... | collective-permute-start | bytes 196616 | tf_op jit(solution)/shard_map/ppermute | solution.py:28
  33.6 0.0 copy-start
  33.6 2.1 %copy-done = f32[7680,128]{1,0:T(8,128)S(1)} copy-done((f32[7680,128]{1,0:T(8,128)S(1)}, f32[7680,128]{1,0:T(8,128)}, u32[]{:S(2)}) %copy-start) | copy-done | bytes 3932184
  35.7 0.0 copy-start.1
  35.7 4.5 %short_sums.6 = f32[64,128]{1,0:T(8,128)S(1)} custom-call(s32[128,128]{1,0:T(8,128)S(1)} %get-tuple-element.72.index_ref, f32[768,48]{1,0:T(8,128)S(1)} %get-tuple-element.73.weight_ref, f32[7680,1,128]{2,1,0:T(1,128)S(1)} %bitcast.15), custom_call_target="tpu_custom_call" | custom-call | flops 4000000000 | bytes 400000 | tf_op jit(solution)/shard_map/short_sums/pallas_call | solution.py:294
  40.3 0.0 collective-permute-done.3
  40.3 0.0 collective-permute-done.4
  40.3 0.0 collective-permute-done.5
  40.3 3.6 %collective-permute-start.6 = (bf16[32,1024]{1,0:T(8,128)(2,1)S(1)}, bf16[32,1024]{1,0:T(8,128)(2,1)S(1)}, u32[]{:S(2)}, u32[]{:S(2)}) collective-permute-start(bf16[32,1024]{1,0:T(8,128)(2,1)S(1)} %add_convert_fusion.1), channel_id=1, source_target_pairs={{0,64},{8,72},{16,80},{24,88},{32,96},{40,104},{48,112},{56,120},{... | collective-permute-start | bytes 196616 | tf_op jit(solution)/shard_map/ppermute | solution.py:28
  44.0 1.2 %collective-permute-start.7 = (bf16[32,1024]{1,0:T(8,128)(2,1)S(1)}, bf16[32,1024]{1,0:T(8,128)(2,1)S(1)}, u32[]{:S(2)}, u32[]{:S(2)}) collective-permute-start(bf16[32,1024]{1,0:T(8,128)(2,1)S(1)} %add_convert_fusion.1), channel_id=1, source_target_pairs={{0,128},{8,136},{16,144},{24,152},{32,160},{40,168},{48,176},{56,1... | collective-permute-start | bytes 196616 | tf_op jit(solution)/shard_map/ppermute | solution.py:28
  45.2 1.8 %collective-permute-start.8 = (bf16[32,1024]{1,0:T(8,128)(2,1)S(1)}, bf16[32,1024]{1,0:T(8,128)(2,1)S(1)}, u32[]{:S(2)}, u32[]{:S(2)}) collective-permute-start(bf16[32,1024]{1,0:T(8,128)(2,1)S(1)} %add_convert_fusion.1), channel_id=1, source_target_pairs={{0,192},{8,200},{16,208},{24,216},{32,224},{40,232},{48,240},{56,2... | collective-permute-start | bytes 196616 | tf_op jit(solution)/shard_map/ppermute | solution.py:28
  47.0 0.0 copy-done.1
  47.0 4.5 %short_sums.8 = f32[64,128]{1,0:T(8,128)S(1)} custom-call(s32[128,128]{1,0:T(8,128)S(1)} %get-tuple-element.87.index_ref, f32[768,48]{1,0:T(8,128)S(1)} %get-tuple-element.73.weight_ref, f32[7680,1,128]{2,1,0:T(1,128)S(1)} %bitcast.16), custom_call_target="tpu_custom_call" | custom-call | flops 4000000000 | bytes 400000 | tf_op jit(solution)/shard_map/short_sums/pallas_call | solution.py:294
  51.5 0.0 copy-start.7
  51.5 0.0 copy-start.8
  51.5 4.5 %short_sums.7 = f32[64,128]{1,0:T(8,128)S(1)} custom-call(s32[128,128]{1,0:T(8,128)S(1)} %get-tuple-element.86.index_ref, f32[768,48]{1,0:T(8,128)S(1)} %get-tuple-element.73.weight_ref, f32[7680,1,128]{2,1,0:T(1,128)S(1)} %bitcast.17), custom_call_target="tpu_custom_call" | custom-call | flops 4000000000 | bytes 400000 | tf_op jit(solution)/shard_map/short_sums/pallas_call | solution.py:294
  56.1 0.0 collective-permute-done.6
  56.1 0.0 collective-permute-done.7
  56.1 0.0 collective-permute-done.8
  56.1 2.3 %collective-permute-start.9 = (f32[32,1024]{1,0:T(8,128)S(1)}, f32[32,1024]{1,0:T(8,128)S(1)}, u32[]{:S(2)}, u32[]{:S(2)}) collective-permute-start(f32[32,1024]{1,0:T(8,128)S(1)} %add_add_fusion), channel_id=1, source_target_pairs={{0,8},{8,0},{16,24},{24,16},{32,40},{40,32},{48,56},{56,48},{64,72... | collective-permute-start | bytes 393224 | tf_op jit(solution)/shard_map/ppermute | solution.py:28
  58.4 1.0 %collective-permute-done.9 = f32[32,1024]{1,0:T(8,128)S(1)} collective-permute-done((f32[32,1024]{1,0:T(8,128)S(1)}, f32[32,1024]{1,0:T(8,128)S(1)}, u32[]{:S(2)}, u32[]{:S(2)}) %collective-permute-start.9) | collective-permute-done | bytes 131104 | tf_op jit(solution)/shard_map/ppermute | solution.py:28
  59.4 0.0 copy-done.7
  59.4 0.0 copy-done.8
  59.4 0.7 multiply_convert_fusion.1
  60.1 6.1 %long_parts.1 = bf16[8,64,768]{2,1,0:T(8,128)(2,1)} custom-call(bf16[64,1024]{1,0:T(8,128)(2,1)S(1)} %pad_maximum_fusion.p_ref, bf16[1024,6144]{1,0:T(8,128)(2,1)} %get-tuple-element.95.table_ref), custom_call_target="tpu_custom_call" | custom-call | flops 800000000 | bytes 14000000 | tf_op jit(solution)/shard_map/long_parts/pallas_call | solution.py:166
  66.2 6.4 %all-to-all-start = ((bf16[8,64,768]{2,1,0:T(8,128)(2,1)}), bf16[8,64,768]{2,1,0:T(8,128)(2,1)S(1)}, u32[]{:S(2)}, u32[]{:S(2)}) async-start(bf16[8,64,768]{2,1,0:T(8,128)(2,1)} %long_parts.1), calls=%async_computation | async-start | bytes 1572864 | tf_op jit(solution)/shard_map/all_to_all | solution.py:395
  72.6 0.0 copy-start.2
  72.7 2.1 %copy-done.2 = f32[7680,128]{1,0:T(8,128)S(1)} copy-done((f32[7680,128]{1,0:T(8,128)S(1)}, f32[7680,128]{1,0:T(8,128)}, u32[]{:S(2)}) %copy-start.2) | copy-done | bytes 3932184
  74.8 4.5 %short_sums.11 = f32[64,128]{1,0:T(8,128)S(1)} custom-call(s32[128,128]{1,0:T(8,128)S(1)} %get-tuple-element.105.index_ref, f32[768,48]{1,0:T(8,128)S(1)} %get-tuple-element.73.weight_ref, f32[7680,1,128]{2,1,0:T(1,128)S(1)} %bitcast.18), custom_call_target="tpu_custom_call" | custom-call | flops 100000000 | bytes 400000 | tf_op jit(solution)/shard_map/short_sums/pallas_call | solution.py:294
  79.3 4.5 %short_sums.10 = f32[64,128]{1,0:T(8,128)S(1)} custom-call(s32[128,128]{1,0:T(8,128)S(1)} %get-tuple-element.104.index_ref, f32[768,48]{1,0:T(8,128)S(1)} %get-tuple-element.73.weight_ref, f32[7680,1,128]{2,1,0:T(1,128)S(1)} %bitcast.19), custom_call_target="tpu_custom_call" | custom-call | flops 100000000 | bytes 400000 | tf_op jit(solution)/shard_map/short_sums/pallas_call | solution.py:294
  83.8 4.5 %short_sums.9 = f32[64,128]{1,0:T(8,128)S(1)} custom-call(s32[128,128]{1,0:T(8,128)S(1)} %get-tuple-element.103.index_ref, f32[768,48]{1,0:T(8,128)S(1)} %get-tuple-element.73.weight_ref, f32[7680,1,128]{2,1,0:T(1,128)S(1)} %bitcast.20), custom_call_target="tpu_custom_call" | custom-call | flops 100000000 | bytes 400000 | tf_op jit(solution)/shard_map/short_sums/pallas_call | solution.py:294
  88.4 0.0 all-to-all-done
  88.4 0.1 convert_reduce_fusion
  88.5 0.7 add_convert_fusion
  (15 shorter events, 0.2 us)
Async XLA Ops:
  0.6 10.3 %copy-start.3 = (bf16[64,6144]{1,0:T(8,128)(2,1)S(1)}, bf16[64,6144]{1,0:T(8,128)(2,1)}, u32[]{:S(2)}) copy-start(bf16[64,6144]{1,0:T(8,128)(2,1)} %grad_ref.3) | copy-start | bytes 2359300
  0.6 10.3 %copy-start.4 = (f32[3,6144]{1,0:T(4,128)S(1)}, f32[3,6144]{1,0:T(4,128)}, u32[]{:S(2)}) copy-start(f32[3,6144]{1,0:T(4,128)} %frac_ref) | copy-start | bytes 221188
  0.7 0.8 copy-start.5
  1.5 9.1 %copy-start.9 = (s32[3,512]{1,0:T(4,128)S(1)}, s32[3,512]{1,0:T(4,128)}, u32[]{:S(2)}) copy-start(s32[3,512]{1,0:T(4,128)} %param.13) | copy-start | bytes 18436
  1.5 9.5 %copy-start.6 = (bf16[64,64]{1,0:T(8,128)(2,1)S(1)}, bf16[64,64]{1,0:T(8,128)(2,1)}, u32[]{:S(2)}) copy-start(bf16[64,64]{1,0:T(8,128)(2,1)} %mix_ref.3) | copy-start | bytes 24580
  7.2 17.2 %collective-permute-start = (bf16[768,128]{1,0:T(8,128)(2,1)S(1)}, bf16[768,128]{1,0:T(8,128)(2,1)S(1)}, u32[]{:S(2)}, u32[]{:S(2)}) collective-permute-start(bf16[768,128]{1,0:T(8,128)(2,1)S(1)} %get-tuple-element.109), channel_id=1, source_target_pairs={{248,0},{0,8},{8,16},{16,24},{24,32},{32,40},{40,48},{48,56},{56,6... | collective-permute-start | bytes 589832 | tf_op jit(solution)/shard_map/ppermute | solution.py:34
  10.3 14.1 %collective-permute-start.1 = (bf16[768,128]{1,0:T(8,128)(2,1)S(1)}, bf16[768,128]{1,0:T(8,128)(2,1)S(1)}, u32[]{:S(2)}, u32[]{:S(2)}) collective-permute-start(bf16[768,128]{1,0:T(8,128)(2,1)S(1)} %get-tuple-element.108), channel_id=1, source_target_pairs={{8,0},{16,8},{24,16},{32,24},{40,32},{48,40},{56,48},{64,56},{72,6... | collective-permute-start | bytes 589832 | tf_op jit(solution)/shard_map/ppermute | solution.py:34
  24.5 5.5 %collective-permute-start.2 = (bf16[32,1024]{1,0:T(8,128)(2,1)S(1)}, bf16[32,1024]{1,0:T(8,128)(2,1)S(1)}, u32[]{:S(2)}, u32[]{:S(2)}) collective-permute-start(bf16[32,1024]{1,0:T(8,128)(2,1)S(1)} %dynamic-slice_convert_fusion), channel_id=1, source_target_pairs={{0,8},{8,0},{16,24},{24,16},{32,40},{40,32},{48,56},{56,48},{64,72... | collective-permute-start | bytes 196616 | tf_op jit(solution)/shard_map/ppermute | solution.py:28
  30.0 10.3 %collective-permute-start.3 = (bf16[32,1024]{1,0:T(8,128)(2,1)S(1)}, bf16[32,1024]{1,0:T(8,128)(2,1)S(1)}, u32[]{:S(2)}, u32[]{:S(2)}) collective-permute-start(bf16[32,1024]{1,0:T(8,128)(2,1)S(1)} %add_convert_fusion.2), channel_id=1, source_target_pairs={{0,16},{8,24},{16,0},{24,8},{32,48},{40,56},{48,32},{56,40},{64,80... | collective-permute-start | bytes 196616 | tf_op jit(solution)/shard_map/ppermute | solution.py:28
  30.1 10.2 %collective-permute-start.4 = (bf16[32,1024]{1,0:T(8,128)(2,1)S(1)}, bf16[32,1024]{1,0:T(8,128)(2,1)S(1)}, u32[]{:S(2)}, u32[]{:S(2)}) collective-permute-start(bf16[32,1024]{1,0:T(8,128)(2,1)S(1)} %add_convert_fusion.2), channel_id=1, source_target_pairs={{0,32},{8,40},{16,48},{24,56},{32,0},{40,8},{48,16},{56,24},{64,96... | collective-permute-start | bytes 196616 | tf_op jit(solution)/shard_map/ppermute | solution.py:28
  31.5 8.8 %collective-permute-start.5 = (bf16[32,1024]{1,0:T(8,128)(2,1)S(1)}, bf16[32,1024]{1,0:T(8,128)(2,1)S(1)}, u32[]{:S(2)}, u32[]{:S(2)}) collective-permute-start(bf16[32,1024]{1,0:T(8,128)(2,1)S(1)} %add_convert_fusion.2), channel_id=1, source_target_pairs={{0,48},{8,56},{16,32},{24,40},{32,16},{40,24},{48,0},{56,8},{64,11... | collective-permute-start | bytes 196616 | tf_op jit(solution)/shard_map/ppermute | solution.py:28
  33.6 2.1 %copy-start = (f32[7680,128]{1,0:T(8,128)S(1)}, f32[7680,128]{1,0:T(8,128)}, u32[]{:S(2)}) copy-start(f32[7680,128]{1,0:T(8,128)} %convert_dynamic-update-slice_fusion) | copy-start | bytes 11796484
  35.7 11.2 %copy-start.1 = (f32[7680,128]{1,0:T(8,128)S(1)}, f32[7680,128]{1,0:T(8,128)}, u32[]{:S(2)}) copy-start(f32[7680,128]{1,0:T(8,128)} %convert_dynamic-update-slice_fusion) | copy-start | bytes 11796484
  40.3 15.7 %collective-permute-start.6 = (bf16[32,1024]{1,0:T(8,128)(2,1)S(1)}, bf16[32,1024]{1,0:T(8,128)(2,1)S(1)}, u32[]{:S(2)}, u32[]{:S(2)}) collective-permute-start(bf16[32,1024]{1,0:T(8,128)(2,1)S(1)} %add_convert_fusion.1), channel_id=1, source_target_pairs={{0,64},{8,72},{16,80},{24,88},{32,96},{40,104},{48,112},{56,120},{... | collective-permute-start | bytes 196616 | tf_op jit(solution)/shard_map/ppermute | solution.py:28
  44.0 12.1 %collective-permute-start.7 = (bf16[32,1024]{1,0:T(8,128)(2,1)S(1)}, bf16[32,1024]{1,0:T(8,128)(2,1)S(1)}, u32[]{:S(2)}, u32[]{:S(2)}) collective-permute-start(bf16[32,1024]{1,0:T(8,128)(2,1)S(1)} %add_convert_fusion.1), channel_id=1, source_target_pairs={{0,128},{8,136},{16,144},{24,152},{32,160},{40,168},{48,176},{56,1... | collective-permute-start | bytes 196616 | tf_op jit(solution)/shard_map/ppermute | solution.py:28
  45.2 10.9 %collective-permute-start.8 = (bf16[32,1024]{1,0:T(8,128)(2,1)S(1)}, bf16[32,1024]{1,0:T(8,128)(2,1)S(1)}, u32[]{:S(2)}, u32[]{:S(2)}) collective-permute-start(bf16[32,1024]{1,0:T(8,128)(2,1)S(1)} %add_convert_fusion.1), channel_id=1, source_target_pairs={{0,192},{8,200},{16,208},{24,216},{32,224},{40,232},{48,240},{56,2... | collective-permute-start | bytes 196616 | tf_op jit(solution)/shard_map/ppermute | solution.py:28
  51.5 7.9 %copy-start.7 = (f32[2,64,512]{2,1,0:T(8,128)S(1)}, f32[2,64,512]{2,1,0:T(8,128)}, u32[]{:S(2)}) copy-start(f32[2,64,512]{2,1,0:T(8,128)} %param.15) | copy-start | bytes 786436
  51.5 7.9 %copy-start.8 = (f32[64,512]{1,0:T(8,128)S(1)}, f32[64,512]{1,0:T(8,128)}, u32[]{:S(2)}) copy-start(f32[64,512]{1,0:T(8,128)} %param.14) | copy-start | bytes 393220
  56.1 3.2 %collective-permute-start.9 = (f32[32,1024]{1,0:T(8,128)S(1)}, f32[32,1024]{1,0:T(8,128)S(1)}, u32[]{:S(2)}, u32[]{:S(2)}) collective-permute-start(f32[32,1024]{1,0:T(8,128)S(1)} %add_add_fusion), channel_id=1, source_target_pairs={{0,8},{8,0},{16,24},{24,16},{32,40},{40,32},{48,56},{56,48},{64,72... | collective-permute-start | bytes 393224 | tf_op jit(solution)/shard_map/ppermute | solution.py:28
  66.2 22.1 %all-to-all-start = ((bf16[8,64,768]{2,1,0:T(8,128)(2,1)}), bf16[8,64,768]{2,1,0:T(8,128)(2,1)S(1)}, u32[]{:S(2)}, u32[]{:S(2)}) async-start(bf16[8,64,768]{2,1,0:T(8,128)(2,1)} %long_parts.1), calls=%async_computation | async-start | bytes 1572864 | tf_op jit(solution)/shard_map/all_to_all | solution.py:395
  72.6 2.1 %copy-start.2 = (f32[7680,128]{1,0:T(8,128)S(1)}, f32[7680,128]{1,0:T(8,128)}, u32[]{:S(2)}) copy-start(f32[7680,128]{1,0:T(8,128)} %convert_dynamic-update-slice_fusion) | copy-start | bytes 11796484

commit v9 on v7

--- a/solution.py
+++ b/solution.py
@@ -253,7 +253,7 @@
     )(ka, halo, mix, grad, index, weight, count)
 
 
-def short_kernel(index_ref, weight_ref, rows_ref, out_ref, sums_ref, sems, *windows):
+def short_kernel(start, index_ref, weight_ref, rows_ref, out_ref, sums_ref, sems, *windows):
     sublane = lax.broadcasted_iota(jnp.int32, (8, LANES), 0)
     groups, depth = LANES // 8, len(windows)
 
@@ -269,7 +269,7 @@
             g = i * depth + w
             fetch(g, w).wait()
             first = pl.multiple_of(g * 8, 8)
-            weights = weight_ref[pl.ds(first, 8), :]
+            weights = weight_ref[pl.ds(start + first, 8), :]
             total = jnp.zeros((8, LANES), F32)
             for s in range(weight_ref.shape[1]):
                 picked = jnp.broadcast_to(rows_ref[windows[w][0, s]], (8, LANES))
@@ -290,15 +290,9 @@
 
 
 def short_sums(piece, channels, index, weight, rows, flops, depth=4):
-    slots = weight.shape[1]
     return pl.pallas_call(
-        short_kernel,
-        grid=(1,),
-        in_specs=[
-            pl.BlockSpec(memory_space=pltpu.VMEM),
-            pl.BlockSpec((LANES, slots), lambda i: (piece, 0)),
-            pl.BlockSpec(memory_space=pltpu.VMEM),
-        ],
+        functools.partial(short_kernel, piece * LANES),
+        in_specs=[pl.BlockSpec(memory_space=pltpu.VMEM)] * 3,
         out_specs=pl.BlockSpec(memory_space=pltpu.VMEM),
         out_shape=jax.ShapeDtypeStruct((channels, LANES), F32),
         scratch_shapes=[pltpu.VMEM((LANES, LANES), F32), pltpu.SemaphoreType.DMA((depth,))]

time: 86.3 us -> 86.3 us (level)
  no operation moved by 1% of the time
where the time goes in v9:
time: 86.3 us; the launch traced here: 86 us
  Pallas kernels  52.3 us (61%)
  starting transfers between devices  22.4 us (26%)
  local copies, waits for them, and re-layouts  5.7 us (7%)
  other arithmetic  2.62 us (3%)
  waiting for transfers between devices  1.98 us (2%)
  between operations  1 us (1%)
    pallas_call x6, Pallas kernels, short_sums(): pl.pallas_call(functools.partial(short_kernel, piece * LANES), in_specs=[...  27.1 us
    pallas_call x1, Pallas kernels, front(): pl.pallas_call(functools.partial(front_kernel, rows, tile), grid=(atoms /...  13.5 us
    ppermute x6, starting transfers between devices, swapped(): lax.ppermute(block, axis, [(i, i ^ bit) for i in range(lax.axis_size(axis...  12.6 us
    all_to_all x1, starting transfers between devices, local(): parts = lax.all_to_all(parts, 'ka', 0, 0, tiled=True)  6.37 us
    pallas_call x1, Pallas kernels, long_parts(): pl.pallas_call(long_kernel, in_specs=[pl.BlockSpec(memory_space=pltpu.VME...  6.11 us
    pallas_call x1, Pallas kernels, prepare(): pl.pallas_call(prepare_kernel, grid_spec=pltpu.PrefetchScalarGridSpec(num...  5.69 us
    unnamed x25, local copies, waits for them, and re-layouts  5.44 us
    ppermute x2, starting transfers between devices, shifted(): return lax.ppermute(block, axis, route)  3.41 us
  transfers between devices with their start and end apart: 9, of which 2 were waited for; matrix products, arithmetic and copies ran while one was open for 1% of the time, Pallas kernels for 47%

profile of v9, /device:TPU:1, one launch (start us, length us, event | category | flops | bytes accessed | tf_op | source)
XLA Modules:
  0.0 86.0 jit_solution(2484141645805223909)
XLA Ops:
  0.6 0.0 copy-start.3
  0.6 0.0 copy-start.4
  0.7 0.0 copy-start.5
  0.7 0.8 copy-done.5
  1.5 0.0 copy-start.9
  1.5 0.0 copy-start.6
  1.5 5.7 %prepare.1 = (f32[7680,128]{1,0:T(8,128)}, bf16[1536,128]{1,0:T(8,128)(2,1)S(1)}, f32[768,48]{1,0:T(8,128)S(1)}, s32[128,128]{1,0:T(8,128)S(1)}, s32[128,128]{1,...) custom-call(s32[1]{0:T(128)} %bitcast.ka_ref, ...), custom_call_target="tpu_custom_call" | custom-call | flops 1000000000 | bytes 8000000 | tf_op jit(solution)/shard_map/prepare/pallas_call | solution.py:223
  7.2 3.1 %collective-permute-start = (bf16[768,128]{1,0:T(8,128)(2,1)S(1)}, bf16[768,128]{1,0:T(8,128)(2,1)S(1)}, u32[]{:S(2)}, u32[]{:S(2)}) collective-permute-start(bf16[768,128]{1,0:T(8,128)(2,1)S(1)} %get-tuple-element.131), channel_id=1, source_target_pairs={{248,0},{0,8},{8,16},{16,24},{24,32},{32,40},{40,48},{48,56},{56,6... | collective-permute-start | bytes 589832 | tf_op jit(solution)/shard_map/ppermute | solution.py:34
  10.3 0.3 collective-permute-start.1
  10.6 0.0 copy-done.9
  10.6 0.1 pad.11.clone
  10.7 0.1 maximum_maximum_fusion
  10.8 0.1 copy.14.k_ref
  10.9 0.0 copy-done.3
  10.9 0.0 copy-done.4
  10.9 0.0 copy-done.6
  10.9 13.5 %structure_sums.1 = (f32[64,1024]{1,0:T(8,128)S(1)}, bf16[1024,6144]{1,0:T(8,128)(2,1)}) custom-call(bf16[64,64]{1,0:T(8,128)(2,1)S(1)} %copy-done.6, bf16[64,6144]{1,0:T(8,128)(2,1)S(1)} %copy-done.3, f32[3,6144]{1,0:T(4,128)S(1)} %copy-done.4, bf16[512,16]{1,0:T(8,128)(2,1)S(1)} %copy.14.k_ref), custom_call_target="tpu_custom_call" | custom-call | flops 20000000000 | bytes 14000000 | tf_op jit(solution)/shard_map/structure_sums/pallas_call | solution.py:118
  24.4 0.0 collective-permute-done
  24.4 0.0 collective-permute-done.1
  24.5 4.6 %collective-permute-start.2 = (bf16[32,1024]{1,0:T(8,128)(2,1)S(1)}, bf16[32,1024]{1,0:T(8,128)(2,1)S(1)}, u32[]{:S(2)}, u32[]{:S(2)}) collective-permute-start(bf16[32,1024]{1,0:T(8,128)(2,1)S(1)} %dynamic-slice_convert_fusion), channel_id=1, source_target_pairs={{0,8},{8,0},{16,24},{24,16},{32,40},{40,32},{48,56},{56,48},{64,72... | collective-permute-start | bytes 196616 | tf_op jit(solution)/shard_map/ppermute | solution.py:28
  29.0 0.9 %convert_dynamic-update-slice_fusion = f32[7680,128]{1,0:T(8,128)} fusion(f32[7680,128]{1,0:T(8,128)} %get-tuple-element.84, bf16[768,128]{1,0:T(8,128)(2,1)S(1)} %collective-permute-done.1, bf16[768,128]{1,0:T(8,128)(2,1)S(1)} %collective-permute-done), kind=kLoop, calls=%fused_computation.1 | loop fusion | flops 786432 | bytes 1179648 | tf_op jit(solution)/shard_map/dynamic_update_slice | solution.py:377
  30.0 0.0 collective-permute-done.2
  30.0 0.1 collective-permute-start.3
  30.1 0.0 copy-start
  30.1 2.1 %copy-done = f32[7680,128]{1,0:T(8,128)S(1)} copy-done((f32[7680,128]{1,0:T(8,128)S(1)}, f32[7680,128]{1,0:T(8,128)}, u32[]{:S(2)}) %copy-start) | copy-done | bytes 3932184
  32.2 0.0 copy-start.1
  32.2 1.0 %collective-permute-done.3 = bf16[32,1024]{1,0:T(8,128)(2,1)S(1)} collective-permute-done((bf16[32,1024]{1,0:T(8,128)(2,1)S(1)}, bf16[32,1024]{1,0:T(8,128)(2,1)S(1)}, u32[]{:S(2)}, u32[]{:S(2)}) %collective-permute-start.3) | collective-permute-done | bytes 65568 | tf_op jit(solution)/shard_map/ppermute | solution.py:28
  33.2 0.7 collective-permute-start.4
  33.9 0.4 copy-done.1
  34.3 4.5 %short_sums.6 = f32[64,128]{1,0:T(8,128)S(1)} custom-call(s32[128,128]{1,0:T(8,128)S(1)} %near.1.index_ref, f32[768,48]{1,0:T(8,128)S(1)} %get-tuple-element.96.weight_ref, f32[7680,1,128]{2,1,0:T(1,128)S(1)} %bitcast.16), custom_call_target="tpu_custom_call" | custom-call | flops 4000000000 | bytes 400000 | tf_op jit(solution)/shard_map/short_sums/pallas_call | solution.py:293
  38.8 0.0 collective-permute-done.4
  38.9 3.6 %collective-permute-start.5 = (bf16[32,1024]{1,0:T(8,128)(2,1)S(1)}, bf16[32,1024]{1,0:T(8,128)(2,1)S(1)}, u32[]{:S(2)}, u32[]{:S(2)}) collective-permute-start(bf16[32,1024]{1,0:T(8,128)(2,1)S(1)} %add_convert_fusion.2), channel_id=1, source_target_pairs={{0,64},{8,72},{16,80},{24,88},{32,96},{40,104},{48,112},{56,120},{... | collective-permute-start | bytes 196616 | tf_op jit(solution)/shard_map/ppermute | solution.py:28
  42.5 4.5 %short_sums.7 = f32[64,128]{1,0:T(8,128)S(1)} custom-call(s32[128,128]{1,0:T(8,128)S(1)} %get-tuple-element.104.index_ref, f32[768,48]{1,0:T(8,128)S(1)} %get-tuple-element.96.weight_ref, f32[7680,1,128]{2,1,0:T(1,128)S(1)} %bitcast.17), custom_call_target="tpu_custom_call" | custom-call | flops 4000000000 | bytes 400000 | tf_op jit(solution)/shard_map/short_sums/pallas_call | solution.py:293
  47.0 0.0 collective-permute-done.5
  47.1 0.0 copy-start.7
  47.1 0.0 copy-start.8
  47.1 1.3 %collective-permute-start.6 = (bf16[32,1024]{1,0:T(8,128)(2,1)S(1)}, bf16[32,1024]{1,0:T(8,128)(2,1)S(1)}, u32[]{:S(2)}, u32[]{:S(2)}) collective-permute-start(bf16[32,1024]{1,0:T(8,128)(2,1)S(1)} %add_convert_fusion.1), channel_id=1, source_target_pairs={{0,128},{8,136},{16,144},{24,152},{32,160},{40,168},{48,176},{56,1... | collective-permute-start | bytes 196616 | tf_op jit(solution)/shard_map/ppermute | solution.py:28
  48.4 4.5 %short_sums.8 = f32[64,128]{1,0:T(8,128)S(1)} custom-call(s32[128,128]{1,0:T(8,128)S(1)} %get-tuple-element.111.index_ref, f32[768,48]{1,0:T(8,128)S(1)} %get-tuple-element.96.weight_ref, f32[7680,1,128]{2,1,0:T(1,128)S(1)} %bitcast.18), custom_call_target="tpu_custom_call" | custom-call | flops 4000000000 | bytes 400000 | tf_op jit(solution)/shard_map/short_sums/pallas_call | solution.py:293
  52.9 0.0 collective-permute-done.6
  53.0 2.3 %collective-permute-start.7 = (f32[32,1024]{1,0:T(8,128)S(1)}, f32[32,1024]{1,0:T(8,128)S(1)}, u32[]{:S(2)}, u32[]{:S(2)}) collective-permute-start(f32[32,1024]{1,0:T(8,128)S(1)} %convert_add_fusion), channel_id=1, source_target_pairs={{0,8},{8,0},{16,24},{24,16},{32,40},{40,32},{48,56},{56,48},{64,72... | collective-permute-start | bytes 393224 | tf_op jit(solution)/shard_map/ppermute | solution.py:28
  55.2 1.0 %collective-permute-done.7 = f32[32,1024]{1,0:T(8,128)S(1)} collective-permute-done((f32[32,1024]{1,0:T(8,128)S(1)}, f32[32,1024]{1,0:T(8,128)S(1)}, u32[]{:S(2)}, u32[]{:S(2)}) %collective-permute-start.7) | collective-permute-done | bytes 131104 | tf_op jit(solution)/shard_map/ppermute | solution.py:28
  56.2 0.0 copy-done.7
  56.2 0.0 copy-done.8
  56.2 0.7 multiply_convert_fusion.1
  57.0 6.1 %long_parts.1 = bf16[8,64,768]{2,1,0:T(8,128)(2,1)} custom-call(bf16[64,1024]{1,0:T(8,128)(2,1)S(1)} %pad_maximum_fusion.p_ref, bf16[1024,6144]{1,0:T(8,128)(2,1)} %get-tuple-element.117.table_ref), custom_call_target="tpu_custom_call" | custom-call | flops 800000000 | bytes 14000000 | tf_op jit(solution)/shard_map/long_parts/pallas_call | solution.py:166
  63.1 6.4 %all-to-all-start = ((bf16[8,64,768]{2,1,0:T(8,128)(2,1)}), bf16[8,64,768]{2,1,0:T(8,128)(2,1)S(1)}, u32[]{:S(2)}, u32[]{:S(2)}) async-start(bf16[8,64,768]{2,1,0:T(8,128)(2,1)} %long_parts.1), calls=%async_computation | async-start | bytes 1572864 | tf_op jit(solution)/shard_map/all_to_all | solution.py:403
  69.5 0.0 copy-start.2
  69.5 2.1 %copy-done.2 = f32[7680,128]{1,0:T(8,128)S(1)} copy-done((f32[7680,128]{1,0:T(8,128)S(1)}, f32[7680,128]{1,0:T(8,128)}, u32[]{:S(2)}) %copy-start.2) | copy-done | bytes 3932184
  71.6 4.5 %short_sums.11 = f32[64,128]{1,0:T(8,128)S(1)} custom-call(s32[128,128]{1,0:T(8,128)S(1)} %get-tuple-element.127.index_ref, f32[768,48]{1,0:T(8,128)S(1)} %get-tuple-element.96.weight_ref, f32[7680,1,128]{2,1,0:T(1,128)S(1)} %bitcast.19), custom_call_target="tpu_custom_call" | custom-call | flops 100000000 | bytes 400000 | tf_op jit(solution)/shard_map/short_sums/pallas_call | solution.py:293
  76.1 4.5 %short_sums.10 = f32[64,128]{1,0:T(8,128)S(1)} custom-call(s32[128,128]{1,0:T(8,128)S(1)} %get-tuple-element.126.index_ref, f32[768,48]{1,0:T(8,128)S(1)} %get-tuple-element.96.weight_ref, f32[7680,1,128]{2,1,0:T(1,128)S(1)} %bitcast.20), custom_call_target="tpu_custom_call" | custom-call | flops 100000000 | bytes 400000 | tf_op jit(solution)/shard_map/short_sums/pallas_call | solution.py:293
  80.6 4.5 %short_sums.9 = f32[64,128]{1,0:T(8,128)S(1)} custom-call(s32[128,128]{1,0:T(8,128)S(1)} %get-tuple-element.125.index_ref, f32[768,48]{1,0:T(8,128)S(1)} %get-tuple-element.96.weight_ref, f32[7680,1,128]{2,1,0:T(1,128)S(1)} %bitcast.21), custom_call_target="tpu_custom_call" | custom-call | flops 100000000 | bytes 400000 | tf_op jit(solution)/shard_map/short_sums/pallas_call | solution.py:293
  85.2 0.0 all-to-all-done
  85.2 0.1 convert_reduce_fusion
  85.3 0.7 add_convert_fusion
  (18 shorter events, 0.2 us)
Async XLA Ops:
  0.6 10.3 %copy-start.3 = (bf16[64,6144]{1,0:T(8,128)(2,1)S(1)}, bf16[64,6144]{1,0:T(8,128)(2,1)}, u32[]{:S(2)}) copy-start(bf16[64,6144]{1,0:T(8,128)(2,1)} %grad_ref.3) | copy-start | bytes 2359300
  0.6 10.3 %copy-start.4 = (f32[3,6144]{1,0:T(4,128)S(1)}, f32[3,6144]{1,0:T(4,128)}, u32[]{:S(2)}) copy-start(f32[3,6144]{1,0:T(4,128)} %frac_ref) | copy-start | bytes 221188
  0.7 0.8 copy-start.5
  1.5 9.1 %copy-start.9 = (s32[3,512]{1,0:T(4,128)S(1)}, s32[3,512]{1,0:T(4,128)}, u32[]{:S(2)}) copy-start(s32[3,512]{1,0:T(4,128)} %param.13) | copy-start | bytes 18436
  1.5 9.5 %copy-start.6 = (bf16[64,64]{1,0:T(8,128)(2,1)S(1)}, bf16[64,64]{1,0:T(8,128)(2,1)}, u32[]{:S(2)}) copy-start(bf16[64,64]{1,0:T(8,128)(2,1)} %mix_ref.3) | copy-start | bytes 24580
  7.2 17.2 %collective-permute-start = (bf16[768,128]{1,0:T(8,128)(2,1)S(1)}, bf16[768,128]{1,0:T(8,128)(2,1)S(1)}, u32[]{:S(2)}, u32[]{:S(2)}) collective-permute-start(bf16[768,128]{1,0:T(8,128)(2,1)S(1)} %get-tuple-element.131), channel_id=1, source_target_pairs={{248,0},{0,8},{8,16},{16,24},{24,32},{32,40},{40,48},{48,56},{56,6... | collective-permute-start | bytes 589832 | tf_op jit(solution)/shard_map/ppermute | solution.py:34
  10.3 14.1 %collective-permute-start.1 = (bf16[768,128]{1,0:T(8,128)(2,1)S(1)}, bf16[768,128]{1,0:T(8,128)(2,1)S(1)}, u32[]{:S(2)}, u32[]{:S(2)}) collective-permute-start(bf16[768,128]{1,0:T(8,128)(2,1)S(1)} %get-tuple-element.130), channel_id=1, source_target_pairs={{8,0},{16,8},{24,16},{32,24},{40,32},{48,40},{56,48},{64,56},{72,6... | collective-permute-start | bytes 589832 | tf_op jit(solution)/shard_map/ppermute | solution.py:34
  24.5 5.5 %collective-permute-start.2 = (bf16[32,1024]{1,0:T(8,128)(2,1)S(1)}, bf16[32,1024]{1,0:T(8,128)(2,1)S(1)}, u32[]{:S(2)}, u32[]{:S(2)}) collective-permute-start(bf16[32,1024]{1,0:T(8,128)(2,1)S(1)} %dynamic-slice_convert_fusion), channel_id=1, source_target_pairs={{0,8},{8,0},{16,24},{24,16},{32,40},{40,32},{48,56},{56,48},{64,72... | collective-permute-start | bytes 196616 | tf_op jit(solution)/shard_map/ppermute | solution.py:28
  30.0 3.2 %collective-permute-start.3 = (bf16[32,1024]{1,0:T(8,128)(2,1)S(1)}, bf16[32,1024]{1,0:T(8,128)(2,1)S(1)}, u32[]{:S(2)}, u32[]{:S(2)}) collective-permute-start(bf16[32,1024]{1,0:T(8,128)(2,1)S(1)} %add_convert_fusion.4), channel_id=1, source_target_pairs={{0,16},{8,24},{16,0},{24,8},{32,48},{40,56},{48,32},{56,40},{64,80... | collective-permute-start | bytes 196616 | tf_op jit(solution)/shard_map/ppermute | solution.py:28
  30.1 2.1 %copy-start = (f32[7680,128]{1,0:T(8,128)S(1)}, f32[7680,128]{1,0:T(8,128)}, u32[]{:S(2)}) copy-start(f32[7680,128]{1,0:T(8,128)} %convert_dynamic-update-slice_fusion) | copy-start | bytes 11796484
  32.2 2.1 %copy-start.1 = (f32[7680,128]{1,0:T(8,128)S(1)}, f32[7680,128]{1,0:T(8,128)}, u32[]{:S(2)}) copy-start(f32[7680,128]{1,0:T(8,128)} %convert_dynamic-update-slice_fusion) | copy-start | bytes 11796484
  33.2 5.6 %collective-permute-start.4 = (bf16[32,1024]{1,0:T(8,128)(2,1)S(1)}, bf16[32,1024]{1,0:T(8,128)(2,1)S(1)}, u32[]{:S(2)}, u32[]{:S(2)}) collective-permute-start(bf16[32,1024]{1,0:T(8,128)(2,1)S(1)} %add_convert_fusion.3), channel_id=1, source_target_pairs={{0,32},{8,40},{16,48},{24,56},{32,0},{40,8},{48,16},{56,24},{64,96... | collective-permute-start | bytes 196616 | tf_op jit(solution)/shard_map/ppermute | solution.py:28
  38.9 8.2 %collective-permute-start.5 = (bf16[32,1024]{1,0:T(8,128)(2,1)S(1)}, bf16[32,1024]{1,0:T(8,128)(2,1)S(1)}, u32[]{:S(2)}, u32[]{:S(2)}) collective-permute-start(bf16[32,1024]{1,0:T(8,128)(2,1)S(1)} %add_convert_fusion.2), channel_id=1, source_target_pairs={{0,64},{8,72},{16,80},{24,88},{32,96},{40,104},{48,112},{56,120},{... | collective-permute-start | bytes 196616 | tf_op jit(solution)/shard_map/ppermute | solution.py:28
  47.1 9.1 %copy-start.7 = (f32[2,64,512]{2,1,0:T(8,128)S(1)}, f32[2,64,512]{2,1,0:T(8,128)}, u32[]{:S(2)}) copy-start(f32[2,64,512]{2,1,0:T(8,128)} %param.15) | copy-start | bytes 786436
  47.1 9.1 %copy-start.8 = (f32[64,512]{1,0:T(8,128)S(1)}, f32[64,512]{1,0:T(8,128)}, u32[]{:S(2)}) copy-start(f32[64,512]{1,0:T(8,128)} %param.14) | copy-start | bytes 393220
  47.1 5.8 %collective-permute-start.6 = (bf16[32,1024]{1,0:T(8,128)(2,1)S(1)}, bf16[32,1024]{1,0:T(8,128)(2,1)S(1)}, u32[]{:S(2)}, u32[]{:S(2)}) collective-permute-start(bf16[32,1024]{1,0:T(8,128)(2,1)S(1)} %add_convert_fusion.1), channel_id=1, source_target_pairs={{0,128},{8,136},{16,144},{24,152},{32,160},{40,168},{48,176},{56,1... | collective-permute-start | bytes 196616 | tf_op jit(solution)/shard_map/ppermute | solution.py:28
  53.0 3.2 %collective-permute-start.7 = (f32[32,1024]{1,0:T(8,128)S(1)}, f32[32,1024]{1,0:T(8,128)S(1)}, u32[]{:S(2)}, u32[]{:S(2)}) collective-permute-start(f32[32,1024]{1,0:T(8,128)S(1)} %convert_add_fusion), channel_id=1, source_target_pairs={{0,8},{8,0},{16,24},{24,16},{32,40},{40,32},{48,56},{56,48},{64,72... | collective-permute-start | bytes 393224 | tf_op jit(solution)/shard_map/ppermute | solution.py:28
  63.1 22.1 %all-to-all-start = ((bf16[8,64,768]{2,1,0:T(8,128)(2,1)}), bf16[8,64,768]{2,1,0:T(8,128)(2,1)S(1)}, u32[]{:S(2)}, u32[]{:S(2)}) async-start(bf16[8,64,768]{2,1,0:T(8,128)(2,1)} %long_parts.1), calls=%async_computation | async-start | bytes 1572864 | tf_op jit(solution)/shard_map/all_to_all | solution.py:403
  69.5 2.1 %copy-start.2 = (f32[7680,128]{1,0:T(8,128)S(1)}, f32[7680,128]{1,0:T(8,128)}, u32[]{:S(2)}) copy-start(f32[7680,128]{1,0:T(8,128)} %convert_dynamic-update-slice_fusion) | copy-start | bytes 11796484

commit v10 on v9

--- a/solution.py
+++ b/solution.py
@@ -289,7 +289,7 @@
     out_ref[...] = sums_ref[...].T[: out_ref.shape[0], :]
 
 
-def short_sums(piece, channels, index, weight, rows, flops, depth=4):
+def short_sums(piece, channels, index, weight, rows, flops, depth=8):
     return pl.pallas_call(
         functools.partial(short_kernel, piece * LANES),
         in_specs=[pl.BlockSpec(memory_space=pltpu.VMEM)] * 3,

time: 86.3 us -> 86.3 us (level)
  no operation moved by 1% of the time
where the time goes in v10:
time: 86.3 us; the launch traced here: 86 us
  Pallas kernels  52.4 us (61%)
  starting transfers between devices  22.3 us (26%)
  local copies, waits for them, and re-layouts  5.7 us (7%)
  other arithmetic  2.62 us (3%)
  waiting for transfers between devices  1.98 us (2%)
  between operations  1 us (1%)
    pallas_call x6, Pallas kernels, short_sums(): pl.pallas_call(functools.partial(short_kernel, piece * LANES), in_specs=[...  27.1 us
    pallas_call x1, Pallas kernels, front(): pl.pallas_call(functools.partial(front_kernel, rows, tile), grid=(atoms /...  13.5 us
    ppermute x6, starting transfers between devices, swapped(): lax.ppermute(block, axis, [(i, i ^ bit) for i in range(lax.axis_size(axis...  12.6 us
    all_to_all x1, starting transfers between devices, local(): parts = lax.all_to_all(parts, 'ka', 0, 0, tiled=True)  6.37 us
    pallas_call x1, Pallas kernels, long_parts(): pl.pallas_call(long_kernel, in_specs=[pl.BlockSpec(memory_space=pltpu.VME...  6.12 us
    pallas_call x1, Pallas kernels, prepare(): pl.pallas_call(prepare_kernel, grid_spec=pltpu.PrefetchScalarGridSpec(num...  5.69 us
    unnamed x25, local copies, waits for them, and re-layouts  5.44 us
    ppermute x2, starting transfers between devices, shifted(): return lax.ppermute(block, axis, route)  3.41 us
  transfers between devices with their start and end apart: 9, of which 2 were waited for; matrix products, arithmetic and copies ran while one was open for 1% of the time, Pallas kernels for 47%

profile of v10, /device:TPU:1, one launch (start us, length us, event | category | flops | bytes accessed | tf_op | source)
XLA Modules:
  0.0 86.0 jit_solution(14717337916289775793)
XLA Ops:
  0.6 0.0 copy-start.3
  0.6 0.0 copy-start.4
  0.7 0.0 copy-start.5
  0.7 0.8 copy-done.5
  1.5 0.0 copy-start.9
  1.5 0.0 copy-start.6
  1.5 5.7 %prepare.1 = (f32[7680,128]{1,0:T(8,128)}, bf16[1536,128]{1,0:T(8,128)(2,1)S(1)}, f32[768,48]{1,0:T(8,128)S(1)}, s32[128,128]{1,0:T(8,128)S(1)}, s32[128,128]{1,...) custom-call(s32[1]{0:T(128)} %bitcast.ka_ref, ...), custom_call_target="tpu_custom_call" | custom-call | flops 1000000000 | bytes 8000000 | tf_op jit(solution)/shard_map/prepare/pallas_call | solution.py:223
  7.2 3.1 %collective-permute-start = (bf16[768,128]{1,0:T(8,128)(2,1)S(1)}, bf16[768,128]{1,0:T(8,128)(2,1)S(1)}, u32[]{:S(2)}, u32[]{:S(2)}) collective-permute-start(bf16[768,128]{1,0:T(8,128)(2,1)S(1)} %get-tuple-element.131), channel_id=1, source_target_pairs={{248,0},{0,8},{8,16},{16,24},{24,32},{32,40},{40,48},{48,56},{56,6... | collective-permute-start | bytes 589832 | tf_op jit(solution)/shard_map/ppermute | solution.py:34
  10.3 0.3 collective-permute-start.1
  10.6 0.0 copy-done.9
  10.6 0.1 pad.11.clone
  10.7 0.1 maximum_maximum_fusion
  10.8 0.1 copy.14.k_ref
  10.9 0.0 copy-done.3
  10.9 0.0 copy-done.4
  10.9 0.0 copy-done.6
  10.9 13.5 %structure_sums.1 = (f32[64,1024]{1,0:T(8,128)S(1)}, bf16[1024,6144]{1,0:T(8,128)(2,1)}) custom-call(bf16[64,64]{1,0:T(8,128)(2,1)S(1)} %copy-done.6, bf16[64,6144]{1,0:T(8,128)(2,1)S(1)} %copy-done.3, f32[3,6144]{1,0:T(4,128)S(1)} %copy-done.4, bf16[512,16]{1,0:T(8,128)(2,1)S(1)} %copy.14.k_ref), custom_call_target="tpu_custom_call" | custom-call | flops 20000000000 | bytes 14000000 | tf_op jit(solution)/shard_map/structure_sums/pallas_call | solution.py:118
  24.4 0.0 collective-permute-done
  24.4 0.0 collective-permute-done.1
  24.5 4.6 %collective-permute-start.2 = (bf16[32,1024]{1,0:T(8,128)(2,1)S(1)}, bf16[32,1024]{1,0:T(8,128)(2,1)S(1)}, u32[]{:S(2)}, u32[]{:S(2)}) collective-permute-start(bf16[32,1024]{1,0:T(8,128)(2,1)S(1)} %dynamic-slice_convert_fusion), channel_id=1, source_target_pairs={{0,8},{8,0},{16,24},{24,16},{32,40},{40,32},{48,56},{56,48},{64,72... | collective-permute-start | bytes 196616 | tf_op jit(solution)/shard_map/ppermute | solution.py:28
  29.0 0.9 %convert_dynamic-update-slice_fusion = f32[7680,128]{1,0:T(8,128)} fusion(f32[7680,128]{1,0:T(8,128)} %get-tuple-element.84, bf16[768,128]{1,0:T(8,128)(2,1)S(1)} %collective-permute-done.1, bf16[768,128]{1,0:T(8,128)(2,1)S(1)} %collective-permute-done), kind=kLoop, calls=%fused_computation.1 | loop fusion | flops 786432 | bytes 1179648 | tf_op jit(solution)/shard_map/dynamic_update_slice | solution.py:377
  30.0 0.0 collective-permute-done.2
  30.0 0.1 collective-permute-start.3
  30.1 0.0 copy-start
  30.1 2.1 %copy-done = f32[7680,128]{1,0:T(8,128)S(1)} copy-done((f32[7680,128]{1,0:T(8,128)S(1)}, f32[7680,128]{1,0:T(8,128)}, u32[]{:S(2)}) %copy-start) | copy-done | bytes 3932184
  32.2 0.0 copy-start.1
  32.2 1.0 %collective-permute-done.3 = bf16[32,1024]{1,0:T(8,128)(2,1)S(1)} collective-permute-done((bf16[32,1024]{1,0:T(8,128)(2,1)S(1)}, bf16[32,1024]{1,0:T(8,128)(2,1)S(1)}, u32[]{:S(2)}, u32[]{:S(2)}) %collective-permute-start.3) | collective-permute-done | bytes 65568 | tf_op jit(solution)/shard_map/ppermute | solution.py:28
  33.2 0.7 collective-permute-start.4
  33.9 0.4 copy-done.1
  34.3 4.5 %short_sums.6 = f32[64,128]{1,0:T(8,128)S(1)} custom-call(s32[128,128]{1,0:T(8,128)S(1)} %near.1.index_ref, f32[768,48]{1,0:T(8,128)S(1)} %get-tuple-element.96.weight_ref, f32[7680,1,128]{2,1,0:T(1,128)S(1)} %bitcast.16), custom_call_target="tpu_custom_call" | custom-call | flops 4000000000 | bytes 400000 | tf_op jit(solution)/shard_map/short_sums/pallas_call | solution.py:293
  38.9 0.0 collective-permute-done.4
  38.9 3.6 %collective-permute-start.5 = (bf16[32,1024]{1,0:T(8,128)(2,1)S(1)}, bf16[32,1024]{1,0:T(8,128)(2,1)S(1)}, u32[]{:S(2)}, u32[]{:S(2)}) collective-permute-start(bf16[32,1024]{1,0:T(8,128)(2,1)S(1)} %add_convert_fusion.2), channel_id=1, source_target_pairs={{0,64},{8,72},{16,80},{24,88},{32,96},{40,104},{48,112},{56,120},{... | collective-permute-start | bytes 196616 | tf_op jit(solution)/shard_map/ppermute | solution.py:28
  42.5 4.5 %short_sums.7 = f32[64,128]{1,0:T(8,128)S(1)} custom-call(s32[128,128]{1,0:T(8,128)S(1)} %get-tuple-element.104.index_ref, f32[768,48]{1,0:T(8,128)S(1)} %get-tuple-element.96.weight_ref, f32[7680,1,128]{2,1,0:T(1,128)S(1)} %bitcast.17), custom_call_target="tpu_custom_call" | custom-call | flops 4000000000 | bytes 400000 | tf_op jit(solution)/shard_map/short_sums/pallas_call | solution.py:293
  47.1 0.0 collective-permute-done.5
  47.1 0.0 copy-start.7
  47.1 0.0 copy-start.8
  47.1 1.5 %collective-permute-start.6 = (bf16[32,1024]{1,0:T(8,128)(2,1)S(1)}, bf16[32,1024]{1,0:T(8,128)(2,1)S(1)}, u32[]{:S(2)}, u32[]{:S(2)}) collective-permute-start(bf16[32,1024]{1,0:T(8,128)(2,1)S(1)} %add_convert_fusion.1), channel_id=1, source_target_pairs={{0,128},{8,136},{16,144},{24,152},{32,160},{40,168},{48,176},{56,1... | collective-permute-start | bytes 196616 | tf_op jit(solution)/shard_map/ppermute | solution.py:28
  48.6 4.5 %short_sums.8 = f32[64,128]{1,0:T(8,128)S(1)} custom-call(s32[128,128]{1,0:T(8,128)S(1)} %get-tuple-element.111.index_ref, f32[768,48]{1,0:T(8,128)S(1)} %get-tuple-element.96.weight_ref, f32[7680,1,128]{2,1,0:T(1,128)S(1)} %bitcast.18), custom_call_target="tpu_custom_call" | custom-call | flops 4000000000 | bytes 400000 | tf_op jit(solution)/shard_map/short_sums/pallas_call | solution.py:293
  53.1 0.0 collective-permute-done.6
  53.2 2.1 %collective-permute-start.7 = (f32[32,1024]{1,0:T(8,128)S(1)}, f32[32,1024]{1,0:T(8,128)S(1)}, u32[]{:S(2)}, u32[]{:S(2)}) collective-permute-start(f32[32,1024]{1,0:T(8,128)S(1)} %convert_add_fusion), channel_id=1, source_target_pairs={{0,8},{8,0},{16,24},{24,16},{32,40},{40,32},{48,56},{56,48},{64,72... | collective-permute-start | bytes 393224 | tf_op jit(solution)/shard_map/ppermute | solution.py:28
  55.2 1.0 %collective-permute-done.7 = f32[32,1024]{1,0:T(8,128)S(1)} collective-permute-done((f32[32,1024]{1,0:T(8,128)S(1)}, f32[32,1024]{1,0:T(8,128)S(1)}, u32[]{:S(2)}, u32[]{:S(2)}) %collective-permute-start.7) | collective-permute-done | bytes 131104 | tf_op jit(solution)/shard_map/ppermute | solution.py:28
  56.2 0.0 copy-done.7
  56.2 0.0 copy-done.8
  56.3 0.7 multiply_convert_fusion.1
  57.0 6.1 %long_parts.1 = bf16[8,64,768]{2,1,0:T(8,128)(2,1)} custom-call(bf16[64,1024]{1,0:T(8,128)(2,1)S(1)} %pad_maximum_fusion.p_ref, bf16[1024,6144]{1,0:T(8,128)(2,1)} %get-tuple-element.117.table_ref), custom_call_target="tpu_custom_call" | custom-call | flops 800000000 | bytes 14000000 | tf_op jit(solution)/shard_map/long_parts/pallas_call | solution.py:166
  63.1 6.4 %all-to-all-start = ((bf16[8,64,768]{2,1,0:T(8,128)(2,1)}), bf16[8,64,768]{2,1,0:T(8,128)(2,1)S(1)}, u32[]{:S(2)}, u32[]{:S(2)}) async-start(bf16[8,64,768]{2,1,0:T(8,128)(2,1)} %long_parts.1), calls=%async_computation | async-start | bytes 1572864 | tf_op jit(solution)/shard_map/all_to_all | solution.py:403
  69.5 0.0 copy-start.2
  69.5 2.1 %copy-done.2 = f32[7680,128]{1,0:T(8,128)S(1)} copy-done((f32[7680,128]{1,0:T(8,128)S(1)}, f32[7680,128]{1,0:T(8,128)}, u32[]{:S(2)}) %copy-start.2) | copy-done | bytes 3932184
  71.6 4.5 %short_sums.11 = f32[64,128]{1,0:T(8,128)S(1)} custom-call(s32[128,128]{1,0:T(8,128)S(1)} %get-tuple-element.127.index_ref, f32[768,48]{1,0:T(8,128)S(1)} %get-tuple-element.96.weight_ref, f32[7680,1,128]{2,1,0:T(1,128)S(1)} %bitcast.19), custom_call_target="tpu_custom_call" | custom-call | flops 100000000 | bytes 400000 | tf_op jit(solution)/shard_map/short_sums/pallas_call | solution.py:293
  76.2 4.5 %short_sums.10 = f32[64,128]{1,0:T(8,128)S(1)} custom-call(s32[128,128]{1,0:T(8,128)S(1)} %get-tuple-element.126.index_ref, f32[768,48]{1,0:T(8,128)S(1)} %get-tuple-element.96.weight_ref, f32[7680,1,128]{2,1,0:T(1,128)S(1)} %bitcast.20), custom_call_target="tpu_custom_call" | custom-call | flops 100000000 | bytes 400000 | tf_op jit(solution)/shard_map/short_sums/pallas_call | solution.py:293
  80.7 4.5 %short_sums.9 = f32[64,128]{1,0:T(8,128)S(1)} custom-call(s32[128,128]{1,0:T(8,128)S(1)} %get-tuple-element.125.index_ref, f32[768,48]{1,0:T(8,128)S(1)} %get-tuple-element.96.weight_ref, f32[7680,1,128]{2,1,0:T(1,128)S(1)} %bitcast.21), custom_call_target="tpu_custom_call" | custom-call | flops 100000000 | bytes 400000 | tf_op jit(solution)/shard_map/short_sums/pallas_call | solution.py:293
  85.3 0.0 all-to-all-done
  85.3 0.1 convert_reduce_fusion
  85.4 0.7 add_convert_fusion
  (18 shorter events, 0.2 us)
Async XLA Ops:
  0.6 10.3 %copy-start.3 = (bf16[64,6144]{1,0:T(8,128)(2,1)S(1)}, bf16[64,6144]{1,0:T(8,128)(2,1)}, u32[]{:S(2)}) copy-start(bf16[64,6144]{1,0:T(8,128)(2,1)} %grad_ref.3) | copy-start | bytes 2359300
  0.6 10.3 %copy-start.4 = (f32[3,6144]{1,0:T(4,128)S(1)}, f32[3,6144]{1,0:T(4,128)}, u32[]{:S(2)}) copy-start(f32[3,6144]{1,0:T(4,128)} %frac_ref) | copy-start | bytes 221188
  0.7 0.8 copy-start.5
  1.5 9.1 %copy-start.9 = (s32[3,512]{1,0:T(4,128)S(1)}, s32[3,512]{1,0:T(4,128)}, u32[]{:S(2)}) copy-start(s32[3,512]{1,0:T(4,128)} %param.13) | copy-start | bytes 18436
  1.5 9.5 %copy-start.6 = (bf16[64,64]{1,0:T(8,128)(2,1)S(1)}, bf16[64,64]{1,0:T(8,128)(2,1)}, u32[]{:S(2)}) copy-start(bf16[64,64]{1,0:T(8,128)(2,1)} %mix_ref.3) | copy-start | bytes 24580
  7.2 17.2 %collective-permute-start = (bf16[768,128]{1,0:T(8,128)(2,1)S(1)}, bf16[768,128]{1,0:T(8,128)(2,1)S(1)}, u32[]{:S(2)}, u32[]{:S(2)}) collective-permute-start(bf16[768,128]{1,0:T(8,128)(2,1)S(1)} %get-tuple-element.131), channel_id=1, source_target_pairs={{248,0},{0,8},{8,16},{16,24},{24,32},{32,40},{40,48},{48,56},{56,6... | collective-permute-start | bytes 589832 | tf_op jit(solution)/shard_map/ppermute | solution.py:34
  10.3 14.1 %collective-permute-start.1 = (bf16[768,128]{1,0:T(8,128)(2,1)S(1)}, bf16[768,128]{1,0:T(8,128)(2,1)S(1)}, u32[]{:S(2)}, u32[]{:S(2)}) collective-permute-start(bf16[768,128]{1,0:T(8,128)(2,1)S(1)} %get-tuple-element.130), channel_id=1, source_target_pairs={{8,0},{16,8},{24,16},{32,24},{40,32},{48,40},{56,48},{64,56},{72,6... | collective-permute-start | bytes 589832 | tf_op jit(solution)/shard_map/ppermute | solution.py:34
  24.5 5.5 %collective-permute-start.2 = (bf16[32,1024]{1,0:T(8,128)(2,1)S(1)}, bf16[32,1024]{1,0:T(8,128)(2,1)S(1)}, u32[]{:S(2)}, u32[]{:S(2)}) collective-permute-start(bf16[32,1024]{1,0:T(8,128)(2,1)S(1)} %dynamic-slice_convert_fusion), channel_id=1, source_target_pairs={{0,8},{8,0},{16,24},{24,16},{32,40},{40,32},{48,56},{56,48},{64,72... | collective-permute-start | bytes 196616 | tf_op jit(solution)/shard_map/ppermute | solution.py:28
  30.0 3.2 %collective-permute-start.3 = (bf16[32,1024]{1,0:T(8,128)(2,1)S(1)}, bf16[32,1024]{1,0:T(8,128)(2,1)S(1)}, u32[]{:S(2)}, u32[]{:S(2)}) collective-permute-start(bf16[32,1024]{1,0:T(8,128)(2,1)S(1)} %add_convert_fusion.4), channel_id=1, source_target_pairs={{0,16},{8,24},{16,0},{24,8},{32,48},{40,56},{48,32},{56,40},{64,80... | collective-permute-start | bytes 196616 | tf_op jit(solution)/shard_map/ppermute | solution.py:28
  30.1 2.1 %copy-start = (f32[7680,128]{1,0:T(8,128)S(1)}, f32[7680,128]{1,0:T(8,128)}, u32[]{:S(2)}) copy-start(f32[7680,128]{1,0:T(8,128)} %convert_dynamic-update-slice_fusion) | copy-start | bytes 11796484
  32.2 2.1 %copy-start.1 = (f32[7680,128]{1,0:T(8,128)S(1)}, f32[7680,128]{1,0:T(8,128)}, u32[]{:S(2)}) copy-start(f32[7680,128]{1,0:T(8,128)} %convert_dynamic-update-slice_fusion) | copy-start | bytes 11796484
  33.2 5.6 %collective-permute-start.4 = (bf16[32,1024]{1,0:T(8,128)(2,1)S(1)}, bf16[32,1024]{1,0:T(8,128)(2,1)S(1)}, u32[]{:S(2)}, u32[]{:S(2)}) collective-permute-start(bf16[32,1024]{1,0:T(8,128)(2,1)S(1)} %add_convert_fusion.3), channel_id=1, source_target_pairs={{0,32},{8,40},{16,48},{24,56},{32,0},{40,8},{48,16},{56,24},{64,96... | collective-permute-start | bytes 196616 | tf_op jit(solution)/shard_map/ppermute | solution.py:28
  38.9 8.2 %collective-permute-start.5 = (bf16[32,1024]{1,0:T(8,128)(2,1)S(1)}, bf16[32,1024]{1,0:T(8,128)(2,1)S(1)}, u32[]{:S(2)}, u32[]{:S(2)}) collective-permute-start(bf16[32,1024]{1,0:T(8,128)(2,1)S(1)} %add_convert_fusion.2), channel_id=1, source_target_pairs={{0,64},{8,72},{16,80},{24,88},{32,96},{40,104},{48,112},{56,120},{... | collective-permute-start | bytes 196616 | tf_op jit(solution)/shard_map/ppermute | solution.py:28
  47.1 9.1 %copy-start.7 = (f32[2,64,512]{2,1,0:T(8,128)S(1)}, f32[2,64,512]{2,1,0:T(8,128)}, u32[]{:S(2)}) copy-start(f32[2,64,512]{2,1,0:T(8,128)} %param.15) | copy-start | bytes 786436
  47.1 9.1 %copy-start.8 = (f32[64,512]{1,0:T(8,128)S(1)}, f32[64,512]{1,0:T(8,128)}, u32[]{:S(2)}) copy-start(f32[64,512]{1,0:T(8,128)} %param.14) | copy-start | bytes 393220
  47.1 6.0 %collective-permute-start.6 = (bf16[32,1024]{1,0:T(8,128)(2,1)S(1)}, bf16[32,1024]{1,0:T(8,128)(2,1)S(1)}, u32[]{:S(2)}, u32[]{:S(2)}) collective-permute-start(bf16[32,1024]{1,0:T(8,128)(2,1)S(1)} %add_convert_fusion.1), channel_id=1, source_target_pairs={{0,128},{8,136},{16,144},{24,152},{32,160},{40,168},{48,176},{56,1... | collective-permute-start | bytes 196616 | tf_op jit(solution)/shard_map/ppermute | solution.py:28
  53.2 3.1 %collective-permute-start.7 = (f32[32,1024]{1,0:T(8,128)S(1)}, f32[32,1024]{1,0:T(8,128)S(1)}, u32[]{:S(2)}, u32[]{:S(2)}) collective-permute-start(f32[32,1024]{1,0:T(8,128)S(1)} %convert_add_fusion), channel_id=1, source_target_pairs={{0,8},{8,0},{16,24},{24,16},{32,40},{40,32},{48,56},{56,48},{64,72... | collective-permute-start | bytes 393224 | tf_op jit(solution)/shard_map/ppermute | solution.py:28
  63.1 22.1 %all-to-all-start = ((bf16[8,64,768]{2,1,0:T(8,128)(2,1)}), bf16[8,64,768]{2,1,0:T(8,128)(2,1)S(1)}, u32[]{:S(2)}, u32[]{:S(2)}) async-start(bf16[8,64,768]{2,1,0:T(8,128)(2,1)} %long_parts.1), calls=%async_computation | async-start | bytes 1572864 | tf_op jit(solution)/shard_map/all_to_all | solution.py:403
  69.5 2.1 %copy-start.2 = (f32[7680,128]{1,0:T(8,128)S(1)}, f32[7680,128]{1,0:T(8,128)}, u32[]{:S(2)}) copy-start(f32[7680,128]{1,0:T(8,128)} %convert_dynamic-update-slice_fusion) | copy-start | bytes 11796484
